TPU v7x, 32 devices: a whole 2x2x4 slice. The times are simulated.
32 devices in a mesh: rep: 8 (over y, x, core), shard: 4 (over z).
Axes of the slice: x: 2, y: 2, z: 4, core: 2. Of those that a mesh axis runs over, the one named last changes fastest.
Arguments:
- tokens: bfloat16 [4096, 1024], P(('rep', 'shard')), may hold values from -6 to 6
- cotangent: bfloat16 [4096, 1024], P(('rep', 'shard')), may hold values from -6 to 6
- lengths: int32 [8], replicated, may hold values from 385 to 512, as said below
- assign: int32 [8], P('rep'), may hold values from 0 to 7, each once
- first_gain: bfloat16 [1024], P('shard'), may hold values from 0.5 to 1.5
- first_shift: bfloat16 [1024], P('shard'), may hold values from -1.5 to 1.5
- qkv_weight: bfloat16 [1024, 3072], P('shard'), may hold values from -0.1875 to 0.1875
- qv_bias: bfloat16 [2048], P('shard'), may hold values from -2.5 to 2.5
- out_weight: bfloat16 [1024, 1024], P('shard'), may hold values from -0.5 to 0.5
- out_bias: bfloat16 [1024], P('shard'), may hold values from -1.5 to 1.5
- second_gain: bfloat16 [1024], P('shard'), may hold values from 0.5 to 1.5
- second_shift: bfloat16 [1024], P('shard'), may hold values from -1.5 to 1.5
- up_weight: bfloat16 [1024, 4096], P('shard'), may hold values from -0.1875 to 0.1875
- up_bias: bfloat16 [4096], P('shard'), may hold values from -2.5 to 2.5
- down_weight: bfloat16 [4096, 1024], P('shard'), may hold values from -0.09375 to 0.09375
- down_bias: bfloat16 [1024], P('shard'), may hold values from -1.5 to 1.5
Outputs:
- layer_out: float32 [4096, 1024], P(('rep', 'shard'))
- tokens_grad: float32 [4096, 1024], P(('rep', 'shard'))
- first_gain_grad: float32 [1024], P(('rep', 'shard'))
- first_shift_grad: float32 [1024], P(('rep', 'shard'))
- qkv_weight_grad: float32 [1024, 3072], P(('rep', 'shard'))
- qv_bias_grad: float32 [2048], P(('rep', 'shard'))
- out_weight_grad: float32 [1024, 1024], P(('rep', 'shard'))
- out_bias_grad: float32 [1024], P(('rep', 'shard'))
- second_gain_grad: float32 [1024], P(('rep', 'shard'))
- second_shift_grad: float32 [1024], P(('rep', 'shard'))
- up_weight_grad: float32 [1024, 4096], P(('rep', 'shard'))
- up_bias_grad: float32 [4096], P(('rep', 'shard'))
- down_weight_grad: float32 [4096, 1024], P(('rep', 'shard'))
- down_bias_grad: float32 [1024], P(('rep', 'shard'))
Inputs may be any that keep to these rules, and one draw needn't show every extreme that they name: lengths[i] is the length of sequence i; at least one sequence has 512 tokens. assign holds each sequence number once.
All inputs are finite; a program needn't handle non-finite values.
Results may differ from a plain program's by a relative error of at most 0.015.
Values may be sent and summed in bfloat16 or wider, within the bound.
No kernel may reach another device: no remote copies, remote signals or barrier semaphores. Data moves between devices by JAX's collectives and lax.ppermute only.
A program may use at most 256 MiB of HBM per device.

v0:
```python
import math

import jax
import jax.numpy as jnp
from jax import lax
from jax.sharding import PartitionSpec as P

HEADS = 16


def for_sending(value):
    return jax.tree.map(lambda a: a.astype(jnp.bfloat16) if a.dtype == jnp.float32 else a, value)


def cut_along(value, dim, devices):
    before, after = (value.shape[:dim], value.shape[dim + 1 :])
    return jnp.moveaxis(value.reshape(*before, devices, -1, *after), dim, 0)


def summed_on_arrival(value, axis, dim):
    blocks = cut_along(value, dim, lax.axis_size(axis))
    arrived = lax.all_to_all(blocks, axis, split_axis=0, concat_axis=0, tiled=True)
    return arrived.astype(jnp.float32).sum(axis=0)


def layer_norm(rows_in, norm_gain, norm_shift):
    row_mean = jnp.mean(rows_in, -1, keepdims=True)
    centered = rows_in - row_mean
    variance = jnp.mean(centered * centered, -1, keepdims=True)
    return centered * lax.rsqrt(variance + 1e-05) * norm_gain + norm_shift


def gelu_tanh(values_in):
    return jax.nn.gelu(values_in, approximate=True)


def owner_order(values):
    rep_count = lax.axis_size("rep")
    shard_count = lax.axis_size("shard")
    lead = values.shape[:-1]
    width = values.shape[-1]
    block = width // (rep_count * shard_count)
    arranged = values.reshape(lead + (rep_count, shard_count, block))
    return jnp.swapaxes(arranged, -3, -2).reshape(lead + (width,))


def settle(grads):
    group_summed = jax.tree.map(
        lambda part: part.astype(jnp.float32),
        lax.psum_scatter(for_sending(grads), "shard", scatter_dimension=0, tiled=True),
    )
    return jax.tree.map(lambda part: summed_on_arrival(part, "rep", 0), for_sending(group_summed))


def head_scores(query_heads, key_heads, query_pos, key_pos, seq_length):
    head_count = query_heads.shape[1]
    score_scale = 1.0 / math.sqrt(query_heads.shape[2])
    slopes = jnp.exp2(-8.0 * (jnp.arange(head_count).astype(jnp.float32) + 1.0) / head_count)
    raw_scores = (
        jnp.einsum("qhd,khd->hqk", query_heads, key_heads, preferred_element_type=jnp.float32)
        * score_scale
    )
    distance = (query_pos[:, None] - key_pos[None, :]).astype(jnp.float32)
    raw_scores = raw_scores - slopes[:, None, None] * distance[None]
    allowed = (key_pos[None, :] <= query_pos[:, None]) & (key_pos[None, :] < seq_length)
    return jnp.where(allowed[None], raw_scores, -1e30)


def body(
    tokens,
    cotangent,
    lengths,
    assign,
    first_gain,
    first_shift,
    qkv_weight,
    qv_bias,
    out_weight,
    out_bias,
    second_gain,
    second_shift,
    up_weight,
    up_bias,
    down_weight,
    down_bias,
):
    rows_in = tokens.astype(jnp.float32)
    row_count = rows_in.shape[0]
    feature_count = rows_in.shape[1]
    head_count = HEADS
    head_size = feature_count // head_count
    score_scale = 1.0 / math.sqrt(head_size)
    group_size = row_count * lax.axis_size("shard")
    seq_length = jnp.sum(jnp.where(jnp.arange(lengths.shape[0]) == assign[0], lengths, 0))
    query_pos = lax.axis_index("shard") * row_count + jnp.arange(row_count)
    key_pos = jnp.arange(group_size)
    row_valid = (query_pos < seq_length)[:, None]
    owned = (
        first_gain,
        first_shift,
        qkv_weight,
        qv_bias,
        out_weight,
        out_bias,
        second_gain,
        second_shift,
        up_weight,
        up_bias,
        down_weight,
        down_bias,
    )
    gathered = (
        lax.all_gather(owned[0], "shard", axis=0, tiled=True),
        lax.all_gather(owned[1], "shard", axis=0, tiled=True),
        lax.all_gather(owned[2], "shard", axis=0, tiled=True),
        lax.all_gather(owned[3], "shard", axis=0, tiled=True),
        lax.all_gather(owned[4], "shard", axis=0, tiled=True),
        lax.all_gather(owned[5], "shard", axis=0, tiled=True),
        lax.all_gather(owned[6], "shard", axis=0, tiled=True),
        lax.all_gather(owned[7], "shard", axis=0, tiled=True),
        lax.all_gather(owned[8], "shard", axis=0, tiled=True),
        lax.all_gather(owned[9], "shard", axis=0, tiled=True),
        lax.all_gather(owned[10], "shard", axis=0, tiled=True),
        lax.all_gather(owned[11], "shard", axis=0, tiled=True),
    )
    gain_first = gathered[0].astype(jnp.float32)
    shift_first = gathered[1].astype(jnp.float32)
    bias_qv = gathered[3].astype(jnp.float32)
    bias_out = gathered[5].astype(jnp.float32)
    gain_second = gathered[6].astype(jnp.float32)
    shift_second = gathered[7].astype(jnp.float32)
    bias_up = gathered[9].astype(jnp.float32)
    bias_down = gathered[11].astype(jnp.float32)
    normed = layer_norm(rows_in, gain_first, shift_first)
    normed_low = normed.astype(jnp.bfloat16)
    joint_out = jnp.dot(normed_low, gathered[2], preferred_element_type=jnp.float32)
    query_low = (joint_out[:, :feature_count] + bias_qv[:feature_count]).astype(jnp.bfloat16)
    key_low = joint_out[:, feature_count : 2 * feature_count].astype(jnp.bfloat16)
    value_low = (joint_out[:, 2 * feature_count :] + bias_qv[feature_count:]).astype(jnp.bfloat16)
    key_all, value_all = (
        lax.all_gather(key_low, "shard", axis=0, tiled=True),
        lax.all_gather(value_low, "shard", axis=0, tiled=True),
    )
    query_heads = query_low.reshape(row_count, head_count, head_size)
    scores = head_scores(
        query_heads,
        key_all.reshape(group_size, head_count, head_size),
        query_pos,
        key_pos,
        seq_length,
    )
    row_top = jnp.max(scores, -1, keepdims=True)
    exp_scores = jnp.exp(scores - row_top)
    row_total = jnp.sum(exp_scores, -1, keepdims=True)
    log_total = row_top + jnp.log(row_total)
    attn_probs = exp_scores / row_total
    mixed_low = (
        jnp.einsum(
            "hqk,khd->qhd",
            attn_probs.astype(jnp.bfloat16),
            value_all.reshape(group_size, head_count, head_size),
            preferred_element_type=jnp.float32,
        )
        .reshape(row_count, feature_count)
        .astype(jnp.bfloat16)
    )
    attended = jnp.dot(mixed_low, gathered[4], preferred_element_type=jnp.float32) + bias_out
    middle = rows_in + attended
    normed_two_low = layer_norm(middle, gain_second, shift_second).astype(jnp.bfloat16)
    hidden = jnp.dot(normed_two_low, gathered[8], preferred_element_type=jnp.float32) + bias_up
    active_low = gelu_tanh(hidden).astype(jnp.bfloat16)
    branch = jnp.dot(active_low, gathered[10], preferred_element_type=jnp.float32) + bias_down
    layer_out = middle + branch
    back_keys = (key_all, value_all)
    key_heads_back = back_keys[0].reshape(group_size, head_count, head_size)
    value_heads_back = back_keys[1].reshape(group_size, head_count, head_size)
    seed_grad = jnp.where(row_valid, cotangent.astype(jnp.float32), 0.0)
    branch_grad = seed_grad.astype(jnp.bfloat16)
    down_grad = jnp.dot(owner_order(active_low).T, branch_grad, preferred_element_type=jnp.float32)
    down_bias_grad = owner_order(jnp.sum(branch_grad.astype(jnp.float32), 0))
    active_grad = jnp.dot(branch_grad, gathered[10].T, preferred_element_type=jnp.float32)
    unused, gelu_pull = jax.vjp(gelu_tanh, hidden)
    hidden_grad = gelu_pull(active_grad)[0].astype(jnp.bfloat16)
    up_grad = jnp.dot(
        owner_order(normed_two_low).T, hidden_grad, preferred_element_type=jnp.float32
    )
    up_bias_grad = owner_order(jnp.sum(hidden_grad.astype(jnp.float32), 0))
    normed_two_grad = jnp.dot(hidden_grad, gathered[8].T, preferred_element_type=jnp.float32)
    unused_two, second_pull = jax.vjp(layer_norm, middle, gain_second, shift_second)
    middle_from_norm, gain_second_grad, shift_second_grad = second_pull(normed_two_grad)
    middle_grad = seed_grad + middle_from_norm
    down_sums = settle((down_grad, down_bias_grad, up_bias_grad))
    up_sums = settle((up_grad, owner_order(gain_second_grad), owner_order(shift_second_grad)))
    attended_grad = middle_grad.astype(jnp.bfloat16)
    out_grad = jnp.dot(owner_order(mixed_low).T, attended_grad, preferred_element_type=jnp.float32)
    out_bias_grad = owner_order(jnp.sum(attended_grad.astype(jnp.float32), 0))
    mixed_grad = (
        jnp.dot(attended_grad, gathered[4].T, preferred_element_type=jnp.float32)
        .astype(jnp.bfloat16)
        .reshape(row_count, head_count, head_size)
    )
    scores_back = head_scores(query_heads, key_heads_back, query_pos, key_pos, seq_length)
    probs_back = jnp.exp(scores_back - log_total)
    probs_grad = jnp.einsum(
        "qhd,khd->hqk", mixed_grad, value_heads_back, preferred_element_type=jnp.float32
    )
    value_part = jnp.einsum(
        "hqk,qhd->khd",
        probs_back.astype(jnp.bfloat16),
        mixed_grad,
        preferred_element_type=jnp.float32,
    ).reshape(group_size, feature_count)
    row_dot = jnp.sum(probs_back * probs_grad, -1, keepdims=True)
    score_grad = (probs_back * (probs_grad - row_dot)).astype(jnp.bfloat16)
    query_grad = (
        jnp.einsum("hqk,khd->qhd", score_grad, key_heads_back, preferred_element_type=jnp.float32)
        * score_scale
    )
    key_part = (
        jnp.einsum(
            "hqk,qhd->khd", score_grad, query_heads, preferred_element_type=jnp.float32
        ).reshape(group_size, feature_count)
        * score_scale
    )
    key_grad, value_grad = (
        lax.psum_scatter(
            key_part.astype(jnp.bfloat16), "shard", scatter_dimension=0, tiled=True
        ).astype(jnp.float32),
        lax.psum_scatter(
            value_part.astype(jnp.bfloat16), "shard", scatter_dimension=0, tiled=True
        ).astype(jnp.float32),
    )
    joint_grad = jnp.concatenate(
        [query_grad.reshape(row_count, feature_count), key_grad, value_grad], 1
    ).astype(jnp.bfloat16)
    qkv_grad = jnp.dot(owner_order(normed_low).T, joint_grad, preferred_element_type=jnp.float32)
    joint_sums = jnp.sum(joint_grad.astype(jnp.float32), 0)
    qv_bias_grad = owner_order(
        jnp.concatenate([joint_sums[:feature_count], joint_sums[2 * feature_count :]], 0)
    )
    normed_grad = jnp.dot(joint_grad, gathered[2].T, preferred_element_type=jnp.float32)
    unused_three, first_pull = jax.vjp(layer_norm, rows_in, gain_first, shift_first)
    rows_from_norm, gain_first_grad, shift_first_grad = first_pull(normed_grad)
    tokens_grad = middle_grad + rows_from_norm
    attn_sums = settle(
        (
            qkv_grad,
            qv_bias_grad,
            out_grad,
            out_bias_grad,
            owner_order(gain_first_grad),
            owner_order(shift_first_grad),
        )
    )
    return (
        layer_out,
        tokens_grad,
        attn_sums[4],
        attn_sums[5],
        attn_sums[0],
        attn_sums[1],
        attn_sums[2],
        attn_sums[3],
        up_sums[1],
        up_sums[2],
        up_sums[0],
        down_sums[2],
        down_sums[0],
        down_sums[1],
    )


def solution(mesh):
    return jax.shard_map(
        body,
        mesh=mesh,
        in_specs=(
            P(("rep", "shard"), None),
            P(("rep", "shard"), None),
            P(),
            P("rep"),
            P("shard"),
            P("shard"),
            P("shard", None),
            P("shard"),
            P("shard", None),
            P("shard"),
            P("shard"),
            P("shard"),
            P("shard", None),
            P("shard"),
            P("shard", None),
            P("shard"),
        ),
        out_specs=(
            P(("rep", "shard"), None),
            P(("rep", "shard"), None),
            P(("rep", "shard")),
            P(("rep", "shard")),
            P(("rep", "shard"), None),
            P(("rep", "shard")),
            P(("rep", "shard"), None),
            P(("rep", "shard")),
            P(("rep", "shard")),
            P(("rep", "shard")),
            P(("rep", "shard"), None),
            P(("rep", "shard")),
            P(("rep", "shard"), None),
            P(("rep", "shard")),
        ),
        check_vma=False,
    )
```

profile of v0, /device:TPU:0, one launch (start us, length us, event | category | flops | bytes accessed | tf_op | source)
XLA Modules:
  0.0 1101.0 jit_solution(16494315522253080866)
XLA Ops:
  10.0 12.6 %all-gather.1 = bf16[4,1,256]{2,1,0:T(2,128)(2,1)S(1)} all-gather(bf16[1,1,256]{2,1,0:T(2,128)(2,1)S(1)} %reshape.354), channel_id=1, replica_groups=mesh['rep'=8,'shard'=4] {'shard'}, dimensions={0}, use_global_device_ids=true | all-gather | bytes 2560 | tf_op jit(solution)/shard_map/all_gather | solution.py:114
  22.6 7.8 all-gather
  30.3 14.4 %all-gather.2 = bf16[4,1,512]{2,1,0:T(2,128)(2,1)S(1)} all-gather(bf16[1,1,512]{2,1,0:T(2,128)(2,1)S(1)} %reshape.356), channel_id=1, replica_groups=mesh['rep'=8,'shard'=4] {'shard'}, dimensions={0}, use_global_device_ids=true | all-gather | bytes 5120 | tf_op jit(solution)/shard_map/all_gather | solution.py:116
  47.2 80.6 %all-gather.14.cloned.1.call-done = bf16[1024,3072]{1,0:T(8,128)(2,1)} async-done(((bf16[256,3072]{1,0:T(8,128)(2,1)}), bf16[1024,3072]{1,0:T(8,128)(2,1)}) %all-gather.14.cloned.1.call-update) | async-done | bytes 6291472 | tf_op jit(solution)/shard_map/all_gather | solution.py:115
  135.8 8.0 all-gather.5
  143.9 9.2 all-gather.4
  153.1 8.0 all-gather.3
  161.1 12.0 %all_gather.53 = bf16[4096]{0:T(1024)(128)(2,1)S(1)} all-gather(bf16[1024]{0:T(1024)(128)(2,1)S(1)} %copy-done.26), channel_id=1, replica_groups=mesh['rep'=8,'shard'=4] {'shard'}, dimensions={0}, use_global_device_ids=true | all-gather | bytes 10240 | tf_op jit(solution)/shard_map/all_gather | solution.py:122
  177.1 11.5 %all-gather.18.cloned.1.call-done = bf16[512,1024]{1,0:T(8,128)(2,1)} async-done(((bf16[128,1024]{1,0:T(8,128)(2,1)}), bf16[512,1024]{1,0:T(8,128)(2,1)}) %all-gather.18.cloned.1.call-update) | async-done | bytes 1048592 | tf_op jit(solution)/shard_map/all_gather | solution.py:141
  194.9 40.6 %all-gather.20.cloned.1.call-done = bf16[1024,1024]{1,0:T(8,128)(2,1)} async-done(((bf16[256,1024]{1,0:T(8,128)(2,1)}), bf16[1024,1024]{1,0:T(8,128)(2,1)}) %all-gather.20.cloned.1.call-update) | async-done | bytes 2097168 | tf_op jit(solution)/shard_map/all_gather | solution.py:117
  238.0 147.2 %all-gather.22.cloned.1.call-done = bf16[1024,4096]{1,0:T(8,128)(2,1)} async-done(((bf16[256,4096]{1,0:T(8,128)(2,1)}), bf16[1024,4096]{1,0:T(8,128)(2,1)}) %all-gather.22.cloned.1.call-update) | async-done | bytes 8388624 | tf_op jit(solution)/shard_map/all_gather | solution.py:121
  385.3 6.9 multiply_convert_fusion.2
  392.2 142.4 %all-gather.24.cloned.1.call-done = bf16[4096,1024]{1,0:T(8,128)(2,1)} async-done(((bf16[1024,1024]{1,0:T(8,128)(2,1)}), bf16[4096,1024]{1,0:T(8,128)(2,1)}) %all-gather.24.cloned.1.call-update) | async-done | bytes 8388624 | tf_op jit(solution)/shard_map/all_gather | solution.py:123
  534.6 7.8 fusion.56
  580.1 27.1 %reduce-scatter.19.cloned.1.call-done = bf16[128,1024]{1,0:T(8,128)(2,1)} async-done(((bf16[512,1024]{1,0:T(8,128)(2,1)}), bf16[128,1024]{1,0:T(8,128)(2,1)}) %reduce-scatter.19.cloned.1.call-update) | async-done | bytes 262160
  639.4 17.5 %all-reduce.8 = (bf16[1024]{0:T(1024)(128)(2,1)S(1)}, bf16[1024]{0:T(1024)(128)(2,1)S(1)}, bf16[2048]{0:T(1024)(128)(2,1)S(1)}, bf16[1024]{0:T(1024)(128)(2,1)S(...) all-reduce(bf16[1024]{0:T(1024)(128)(2,1)S(1)} %convert_element_typ, ...), channel_id=4, replica_groups=mesh['rep'=8,'shard'=4] {'shard'}, use_global_device_ids=true, to_apply=%region_15.16.clone | all-reduce | flops 12288 | bytes 49152
  713.0 7.0 all_to_all.99
  720.0 13.9 %all_to_all.100 = bf16[8,32,1024]{2,1,0:T(8,128)(2,1)} all-to-all(bf16[8,32,1024]{2,1,0:T(8,128)(2,1)} %bitcast.119), channel_id=1, replica_groups=mesh['rep'=8,'shard'=4] {'rep'}, dimensions={0} | all-to-all | bytes 1048576 | tf_op jit(solution)/shard_map/all_to_all | solution.py:22
  733.8 31.4 %reduce-scatter.11.cloned.1.call-done = bf16[256,3072]{1,0:T(8,128)(2,1)} async-done(((bf16[1024,3072]{1,0:T(8,128)(2,1)}), bf16[256,3072]{1,0:T(8,128)(2,1)}) %reduce-scatter.11.cloned.1.call-update) | async-done | bytes 1572880 | tf_op jit(solution)/shard_map/reduce_scatter | solution.py:50
  765.2 25.3 %all_to_all.101 = bf16[8,32,3072]{2,1,0:T(8,128)(2,1)} all-to-all(bf16[8,32,3072]{2,1,0:T(8,128)(2,1)} %bitcast.110), channel_id=1, replica_groups=mesh['rep'=8,'shard'=4] {'rep'}, dimensions={0} | all-to-all | bytes 3145728 | tf_op jit(solution)/shard_map/all_to_all | solution.py:22
  790.5 122.2 %reduce-scatter.17.cloned.1.call-done = bf16[1024,1024]{1,0:T(8,128)(2,1)} async-done(((bf16[4096,1024]{1,0:T(8,128)(2,1)}), bf16[1024,1024]{1,0:T(8,128)(2,1)}) %reduce-scatter.17.cloned.1.call-update) | async-done | bytes 2097168 | tf_op jit(solution)/shard_map/reduce_scatter | solution.py:50
  916.5 10.7 all-gather.6
  933.0 127.3 %reduce-scatter.15.cloned.1.call-done = bf16[256,4096]{1,0:T(8,128)(2,1)} async-done(((bf16[1024,4096]{1,0:T(8,128)(2,1)}), bf16[256,4096]{1,0:T(8,128)(2,1)}) %reduce-scatter.15.cloned.1.call-update) | async-done | bytes 2097168 | tf_op jit(solution)/shard_map/reduce_scatter | solution.py:50
  1074.2 17.2 %all-to-all-done.8 = bf16[8,32,4096]{2,1,0:T(8,128)(2,1)} async-done(((bf16[8,32,4096]{2,1,0:T(8,128)(2,1)}), bf16[8,32,4096]{2,1,0:T(8,128)(2,1)}, u32[]{:S(2)}, u32[]{:S(2)}) %all-to-all-start.8) | async-done | bytes 2097184 | tf_op jit(solution)/shard_map/all_to_all | solution.py:22
  (240 shorter events, 175.1 us)
Async XLA Ops:
  7.2 120.6 %all-gather.14.cloned.1.call-start = ((), (), s32[]{:S(2)}) async-start(), calls=%async_computation.18 | async-start | bytes 7864320 | tf_op jit(solution)/shard_map/all_gather | solution.py:115
  7.9 167.5 %all-gather.16.cloned.1.call-start = ((), (), s32[]{:S(2)}) async-start(), calls=%async_computation.19 | async-start | bytes 1310720 | tf_op jit(solution)/shard_map/all_gather | solution.py:142
  132.5 56.1 %all-gather.18.cloned.1.call-start = ((), (), s32[]{:S(2)}) async-start(), calls=%async_computation.20 | async-start | bytes 1310720 | tf_op jit(solution)/shard_map/all_gather | solution.py:141
  133.3 102.2 %all-gather.20.cloned.1.call-start = ((), (), s32[]{:S(2)}) async-start(), calls=%async_computation.21 | async-start | bytes 2621440 | tf_op jit(solution)/shard_map/all_gather | solution.py:117
  133.9 251.4 %all-gather.22.cloned.1.call-start = ((), (), s32[]{:S(2)}) async-start(), calls=%async_computation.22 | async-start | bytes 10485760 | tf_op jit(solution)/shard_map/all_gather | solution.py:121
  134.5 400.1 %all-gather.24.cloned.1.call-start = ((), (), s32[]{:S(2)}) async-start(), calls=%async_computation.23 | async-start | bytes 10485760 | tf_op jit(solution)/shard_map/all_gather | solution.py:123
  135.1 443.9 %reduce-scatter.21.cloned.1.call-start = ((), (), s32[]{:S(2)}) async-start(), calls=%async_computation.29 | async-start | bytes 1310720
  238.0 154.2 %copy-start.21 = (bf16[128,1024]{1,0:T(8,128)(2,1)}, bf16[128,1024]{1,0:T(8,128)(2,1)S(1)}, u32[]{:S(2)}) copy-start(bf16[128,1024]{1,0:T(8,128)(2,1)S(1)} %add_convert_fusion) | copy-start | bytes 786436
  238.0 296.6 %copy-start.11 = (bf16[128,1024]{1,0:T(8,128)(2,1)S(1)}, bf16[128,1024]{1,0:T(8,128)(2,1)}, u32[]{:S(2)}) copy-start(bf16[128,1024]{1,0:T(8,128)(2,1)} %param.17) | copy-start | bytes 786436
  553.4 53.8 %reduce-scatter.19.cloned.1.call-start = ((), (), s32[]{:S(2)}) async-start(), calls=%async_computation.28 | async-start | bytes 1310720
  562.3 157.7 %reduce-scatter.13.cloned.1.call-start = ((), (), s32[]{:S(2)}) async-start(), calls=%async_computation.25 | async-start | bytes 2621440 | tf_op jit(solution)/shard_map/reduce_scatter | solution.py:50
  566.3 198.9 %reduce-scatter.11.cloned.1.call-start = ((), (), s32[]{:S(2)}) async-start(), calls=%async_computation.24 | async-start | bytes 7864320 | tf_op jit(solution)/shard_map/reduce_scatter | solution.py:50
  614.0 298.8 %reduce-scatter.17.cloned.1.call-start = ((), (), s32[]{:S(2)}) async-start(), calls=%async_computation.27 | async-start | bytes 10485760 | tf_op jit(solution)/shard_map/reduce_scatter | solution.py:50
  623.5 436.7 %reduce-scatter.15.cloned.1.call-start = ((), (), s32[]{:S(2)}) async-start(), calls=%async_computation.26 | async-start | bytes 10485760 | tf_op jit(solution)/shard_map/reduce_scatter | solution.py:50
  638.1 152.4 %copy-start.19 = (f32[128,1024]{1,0:T(8,128)}, f32[128,1024]{1,0:T(8,128)S(1)}, u32[]{:S(2)}) copy-start(f32[128,1024]{1,0:T(8,128)S(1)} %get-tuple-element.49) | copy-start | bytes 1572868
  657.7 8.3 all-to-all-start
  666.0 7.8 all-to-all-start.1
  673.8 7.8 all-to-all-start.5
  681.6 7.8 all-to-all-start.6
  689.5 7.8 all-to-all-start.7
  697.3 7.8 all-to-all-start.11
  705.1 7.8 all-to-all-start.3
  912.7 147.6 %all-to-all-start.10 = ((bf16[8,128,1024]{2,1,0:T(8,128)(2,1)}), bf16[8,128,1024]{2,1,0:T(8,128)(2,1)S(1)}, u32[]{:S(2)}, u32[]{:S(2)}) async-start(bf16[8,128,1024]{2,1,0:T(8,128)(2,1)} %bitcast.108), calls=%async_computation.14 | async-start | bytes 4194304 | tf_op jit(solution)/shard_map/all_to_all | solution.py:22
  1060.3 31.1 %all-to-all-start.8 = ((bf16[8,32,4096]{2,1,0:T(8,128)(2,1)}), bf16[8,32,4096]{2,1,0:T(8,128)(2,1)}, u32[]{:S(2)}, u32[]{:S(2)}) async-start(bf16[8,32,4096]{2,1,0:T(8,128)(2,1)} %bitcast.107), calls=%async_computation.11 | async-start | bytes 4194304 | tf_op jit(solution)/shard_map/all_to_all | solution.py:22
  (30 other events, 351.4 us)
Sparse Core Ops, SparseCore 0:
  9.6 118.1 all-gather.13
  132.6 26.3 all-gather.15
  161.1 27.4 all-gather.17
  190.0 45.4 all-gather.19
  236.9 148.3 all-gather.21
  386.7 147.8 all-gather.23
  553.5 25.3 reduce-scatter.20
  581.3 25.7 reduce-scatter.18
  609.4 43.0 reduce-scatter.12
  654.8 110.4 reduce-scatter.10
  767.7 144.9 reduce-scatter.16
  915.1 145.1 reduce-scatter.14
where the time goes:
time: 1100 us
  waiting for transfers between devices  782 us (71%)
  blocking collectives  146 us (13%)
  matrix products  70.3 us (6%)
  starting transfers between devices  32.6 us (3%)
  local copies, waits for them, and re-layouts  30.9 us (3%)
  other arithmetic  21.5 us (2%)
  between operations  17.5 us (2%)
    reduce_scatter x4, waiting for transfers between devices, settle(): lax.psum_scatter(for_sending(grads), 'shard', scatter_dimension=0, tiled=...  281 us
    all_gather x1, waiting for transfers between devices, body(): lax.all_gather(owned[8], 'shard', axis=0, tiled=True)  147 us
    all_gather x1, waiting for transfers between devices, body(): lax.all_gather(owned[10], 'shard', axis=0, tiled=True)  142 us
    all_gather x1, waiting for transfers between devices, body(): lax.all_gather(owned[2], 'shard', axis=0, tiled=True)  80.6 us
    all_to_all x3, blocking collectives, summed_on_arrival(): lax.all_to_all(blocks, axis, split_axis=0, concat_axis=0, tiled=True)  46.1 us
    all_to_all x9, waiting for transfers between devices, summed_on_arrival(): lax.all_to_all(blocks, axis, split_axis=0, concat_axis=0, tiled=True)  43 us
    all_gather x1, waiting for transfers between devices, body(): lax.all_gather(owned[4], 'shard', axis=0, tiled=True)  40.6 us
    unnamed x14, waiting for transfers between devices  35.8 us
  transfers between devices with their start and end apart: 21, of which 18 were waited for; matrix products, arithmetic and copies ran while one was open for 8% of the time, Pallas kernels for 0%

commit v1 on v0

--- a/solution.py
+++ b/solution.py
@@ -3,6 +3,8 @@
 import jax
 import jax.numpy as jnp
 from jax import lax
+from jax.experimental import pallas as pl
+from jax.experimental.pallas import tpu as pltpu
 from jax.sharding import PartitionSpec as P
 
 HEADS = 16
@@ -66,7 +68,7 @@
     return jnp.where(allowed[None], raw_scores, -1e30)
 
 
-def body(
+def body_generic(
     tokens,
     cotangent,
     lengths,
@@ -270,9 +272,379 @@
     )
 
 
+PLANE = 8
+DEPTH = 4
+QUARTERS = 4
+
+
+def is_planes(mesh):
+    return mesh.shape["rep"] == PLANE and mesh.shape["shard"] == DEPTH
+
+
+def over_rep(value, partner):
+    return lax.ppermute(value, "rep", [(i, partner(i)) for i in range(PLANE)])
+
+
+def over_z(value, step):
+    return lax.ppermute(value, "shard", [(i, (i + step) % DEPTH) for i in range(DEPTH)])
+
+
+def first_way(i):
+    return i ^ (4 if i & 1 else 2)
+
+
+def second_way(i):
+    return i ^ (2 if i & 1 else 4)
+
+
+def sibling(i):
+    return i ^ 1
+
+
+def home_of(index):
+    rep, z = index // DEPTH, index % DEPTH
+    return ((rep & 1) * 4 + z) * DEPTH + rep // 2
+
+
+def to_home(value):
+    pairs = [(i, home_of(i)) for i in range(PLANE * DEPTH)]
+    return lax.ppermute(value, ("rep", "shard"), pairs)
+
+
+def from_home(value):
+    pairs = [(home_of(i), i) for i in range(PLANE * DEPTH)]
+    return lax.ppermute(value, ("rep", "shard"), pairs)
+
+
+def spread(block):
+    arrived = jnp.concatenate([over_z(block, step) for step in (1, 2, 3)], 0)
+    beside = over_rep(arrived, first_way)
+    pair = jnp.concatenate([arrived, beside], 0)
+    mine = jnp.concatenate([pair, over_rep(pair, second_way)], 0)
+    return mine, over_rep(mine, sibling)
+
+
+def assemble_kernel(rows, own_ref, mine_ref, other_ref, out_ref, sems):
+    rep = lax.axis_index("rep")
+    z = lax.axis_index("shard")
+    copies = [
+        pltpu.make_async_copy(
+            own_ref, out_ref.at[pl.ds(z * (PLANE * rows), PLANE * rows)], sems.at[24]
+        )
+    ]
+    for side, held in enumerate((mine_ref, other_ref)):
+        base = rep ^ side
+        odd = base & 1
+        for slot in range(4):
+            if slot == 0:
+                source = base
+            elif slot == 1:
+                source = base ^ (2 + 2 * odd)
+            elif slot == 2:
+                source = base ^ (4 - 2 * odd)
+            else:
+                source = base ^ 6
+            for step in (1, 2, 3):
+                plane = lax.rem(z + (DEPTH - step), DEPTH)
+                place = plane * (PLANE * rows) + source * rows
+                index = slot * 3 + step - 1
+                copies.append(
+                    pltpu.make_async_copy(
+                        held.at[pl.ds(index * rows, rows)],
+                        out_ref.at[pl.ds(pl.multiple_of(place, rows), rows)],
+                        sems.at[side * 12 + index],
+                    )
+                )
+    for copy in copies:
+        copy.start()
+    for copy in copies:
+        copy.wait()
+
+
+def assemble(own, pieces):
+    rows = own.shape[0] // PLANE
+
+    def kernel(*refs):
+        assemble_kernel(rows, *refs)
+
+    whole = (own.shape[0] * DEPTH, own.shape[1])
+    return pl.pallas_call(
+        kernel,
+        out_shape=jax.ShapeDtypeStruct(whole, own.dtype),
+        in_specs=[pl.BlockSpec(memory_space=pl.ANY)] * 3,
+        out_specs=pl.BlockSpec(memory_space=pltpu.VMEM),
+        scratch_shapes=[pltpu.SemaphoreType.DMA((25,))],
+        compiler_params=pltpu.CompilerParams(vmem_limit_bytes=24 * 2**20),
+        cost_estimate=pl.CostEstimate(
+            flops=0, bytes_accessed=4 * whole[0] * whole[1], transcendentals=0
+        ),
+    )(own, *pieces)
+
+
+def block_at(blocks, index):
+    return lax.dynamic_index_in_dim(blocks, index, 0, keepdims=False)
+
+
+def summed_over_z(blocks):
+    z = lax.axis_index("shard")
+    low = blocks.astype(jnp.bfloat16)
+    total = block_at(blocks, z)
+    for step in (1, 2, 3):
+        sent = block_at(low, lax.rem(z + step, DEPTH))
+        total = total + over_z(sent, step).astype(jnp.float32)
+    return total
+
+
+def by_plane(value):
+    count, width = value.shape
+    blocks = jnp.swapaxes(value.reshape(count, PLANE, width // PLANE), 0, 1)
+    arrived = lax.all_to_all(blocks, "rep", 0, 0, tiled=True)
+    return arrived.reshape(PLANE * count, width // PLANE)
+
+
+def plane_rows(value):
+    return lax.all_gather(value, "rep", axis=0, tiled=True)
+
+
+def outer(left, right):
+    return lax.dot_general(
+        left, right, (((0,), (0,)), ((), ())), preferred_element_type=jnp.float32
+    )
+
+
+def column_parts_to_rows(grad):
+    rows, width = grad.shape
+    parts = grad.reshape(PLANE, DEPTH, rows // (PLANE * DEPTH), width)
+    summed = summed_over_z(jnp.swapaxes(parts, 0, 1)).astype(jnp.bfloat16)
+    arrived = lax.all_to_all(summed, "rep", 0, 0, tiled=True)
+    return jnp.swapaxes(arrived, 0, 1).reshape(-1, PLANE * width).astype(jnp.float32)
+
+
+def body_planes(
+    tokens,
+    cotangent,
+    lengths,
+    assign,
+    first_gain,
+    first_shift,
+    qkv_weight,
+    qv_bias,
+    out_weight,
+    out_bias,
+    second_gain,
+    second_shift,
+    up_weight,
+    up_bias,
+    down_weight,
+    down_bias,
+):
+    row_count, feature_count = tokens.shape
+    head_count = HEADS
+    head_size = feature_count // head_count
+    score_scale = 1.0 / math.sqrt(head_size)
+    group_size = row_count * QUARTERS
+    rep = lax.axis_index("rep")
+    z = lax.axis_index("shard")
+    quarter = rep & 3
+
+    own_length = jnp.sum(jnp.where(jnp.arange(lengths.shape[0]) == assign[0], lengths, 0))
+    seq_length = to_home(own_length.astype(jnp.float32).reshape(1, 1)).astype(jnp.int32)[0, 0]
+    tokens = to_home(tokens)
+    cotangent = to_home(cotangent)
+
+    small = (
+        first_gain,
+        first_shift,
+        qv_bias,
+        out_bias,
+        second_gain,
+        second_shift,
+        up_bias,
+        down_bias,
+    )
+    packed = jnp.concatenate(small, 0).reshape(1, -1)
+    around = [packed] + [over_z(packed, step) for step in (1, 2, 3)]
+    parts = []
+    for plane in range(DEPTH):
+        back = lax.rem(z + (DEPTH - plane), DEPTH)
+        parts.append(
+            sum(
+                jnp.where(back == step, around[step].astype(jnp.float32), 0.0)
+                for step in range(DEPTH)
+            )
+        )
+    stacked = jnp.concatenate(parts, 0)
+    whole_small = []
+    start = 0
+    for item in small:
+        size = item.shape[0]
+        whole_small.append(stacked[:, start : start + size].reshape(-1))
+        start += size
+    (
+        gain_first,
+        shift_first,
+        bias_qv,
+        bias_out,
+        gain_second,
+        shift_second,
+        bias_up,
+        bias_down,
+    ) = whole_small
+
+    weights = (qkv_weight, out_weight, up_weight, down_weight)
+    eighths = lax.optimization_barrier(
+        tuple(
+            lax.dynamic_slice_in_dim(w, rep * (w.shape[0] // PLANE), w.shape[0] // PLANE, 0)
+            for w in weights
+        )
+    )
+    qkv_all, out_all, up_all, down_all = [
+        assemble(w, spread(part)) for w, part in zip(weights, eighths)
+    ]
+
+    rows_in = tokens.astype(jnp.float32)
+    query_pos = quarter * row_count + jnp.arange(row_count)
+    order = jnp.array([0, 2, 1, 3])
+    key_pos = ((quarter ^ order)[:, None] * row_count + jnp.arange(row_count)[None]).reshape(-1)
+    row_valid = (query_pos < seq_length)[:, None]
+    seed_grad = jnp.where(row_valid, cotangent.astype(jnp.float32), 0.0)
+    branch_grad = seed_grad.astype(jnp.bfloat16)
+    branch_grad_plane = plane_rows(branch_grad)
+
+    normed_low = layer_norm(rows_in, gain_first, shift_first).astype(jnp.bfloat16)
+    normed_plane = plane_rows(normed_low)
+    joint_out = jnp.dot(normed_low, qkv_all, preferred_element_type=jnp.float32)
+    query_low = (joint_out[:, :feature_count] + bias_qv[:feature_count]).astype(jnp.bfloat16)
+    key_low = joint_out[:, feature_count : 2 * feature_count].astype(jnp.bfloat16)
+    value_low = (joint_out[:, 2 * feature_count :] + bias_qv[feature_count:]).astype(jnp.bfloat16)
+    own_pair = jnp.stack([key_low, value_low], 0)
+    near = jnp.concatenate([own_pair, over_rep(own_pair, lambda i: i ^ 2)], 1)
+    pair_all = jnp.concatenate([near, over_rep(near, sibling)], 1)
+    key_heads = pair_all[0].reshape(group_size, head_count, head_size)
+    value_heads = pair_all[1].reshape(group_size, head_count, head_size)
+    query_heads = query_low.reshape(row_count, head_count, head_size)
+    scores = head_scores(query_heads, key_heads, query_pos, key_pos, seq_length)
+    row_top = jnp.max(scores, -1, keepdims=True)
+    exp_scores = jnp.exp(scores - row_top)
+    row_total = jnp.sum(exp_scores, -1, keepdims=True)
+    attn_probs = exp_scores / row_total
+    probs_low = attn_probs.astype(jnp.bfloat16)
+    mixed_low = (
+        jnp.einsum("hqk,khd->qhd", probs_low, value_heads, preferred_element_type=jnp.float32)
+        .reshape(row_count, feature_count)
+        .astype(jnp.bfloat16)
+    )
+    middle = rows_in + jnp.dot(mixed_low, out_all, preferred_element_type=jnp.float32) + bias_out
+    normed_two_low = layer_norm(middle, gain_second, shift_second).astype(jnp.bfloat16)
+    normed_two_plane = plane_rows(normed_two_low)
+    hidden = jnp.dot(normed_two_low, up_all, preferred_element_type=jnp.float32) + bias_up
+    active_low = gelu_tanh(hidden).astype(jnp.bfloat16)
+    branch = jnp.dot(active_low, down_all, preferred_element_type=jnp.float32) + bias_down
+    layer_out = from_home((middle + branch).astype(jnp.bfloat16)).astype(jnp.float32)
+
+    active_plane = by_plane(active_low)
+    active_grad = jnp.dot(branch_grad, down_all.T, preferred_element_type=jnp.float32)
+    unused, gelu_pull = jax.vjp(gelu_tanh, hidden)
+    hidden_grad = gelu_pull(active_grad)[0].astype(jnp.bfloat16)
+    hidden_grad_plane = by_plane(hidden_grad)
+    normed_two_grad = jnp.dot(hidden_grad, up_all.T, preferred_element_type=jnp.float32)
+    unused_two, second_pull = jax.vjp(layer_norm, middle, gain_second, shift_second)
+    middle_from_norm, gain_second_grad, shift_second_grad = second_pull(normed_two_grad)
+    middle_grad = seed_grad + middle_from_norm
+
+    down_slice = outer(active_plane, branch_grad_plane)
+    down_grad = summed_over_z(down_slice.reshape(DEPTH, -1, feature_count))
+    up_grad = column_parts_to_rows(outer(normed_two_plane, hidden_grad_plane))
+
+    attended_grad = middle_grad.astype(jnp.bfloat16)
+    attended_grad_plane = plane_rows(attended_grad)
+    mixed_plane = by_plane(mixed_low)
+    out_slice = outer(mixed_plane, attended_grad_plane)
+    out_grad = summed_over_z(out_slice.reshape(DEPTH, -1, feature_count))
+
+    mixed_grad = (
+        jnp.dot(attended_grad, out_all.T, preferred_element_type=jnp.float32)
+        .astype(jnp.bfloat16)
+        .reshape(row_count, head_count, head_size)
+    )
+    probs_grad = jnp.einsum(
+        "qhd,khd->hqk", mixed_grad, value_heads, preferred_element_type=jnp.float32
+    )
+    value_part = jnp.einsum(
+        "hqk,qhd->khd", probs_low, mixed_grad, preferred_element_type=jnp.float32
+    ).reshape(group_size, feature_count)
+    row_dot = jnp.sum(attn_probs * probs_grad, -1, keepdims=True)
+    score_grad = (attn_probs * (probs_grad - row_dot)).astype(jnp.bfloat16)
+    query_grad = (
+        jnp.einsum("hqk,khd->qhd", score_grad, key_heads, preferred_element_type=jnp.float32)
+        * score_scale
+    )
+    key_part = (
+        jnp.einsum(
+            "hqk,qhd->khd", score_grad, query_heads, preferred_element_type=jnp.float32
+        ).reshape(group_size, feature_count)
+        * score_scale
+    )
+    back = jnp.stack([key_part, value_part], 0)
+    half = group_size // 2
+    given = over_rep(back[:, half:].astype(jnp.bfloat16), sibling)
+    back = back[:, :half] + given.astype(jnp.float32)
+    given = over_rep(back[:, row_count:].astype(jnp.bfloat16), lambda i: i ^ 2)
+    back = back[:, :row_count] + given.astype(jnp.float32)
+    joint_grad = jnp.concatenate(
+        [query_grad.reshape(row_count, feature_count), back[0], back[1]], 1
+    ).astype(jnp.bfloat16)
+    joint_grad_plane = by_plane(joint_grad)
+    qkv_grad = column_parts_to_rows(outer(normed_plane, joint_grad_plane))
+    normed_grad = jnp.dot(joint_grad, qkv_all.T, preferred_element_type=jnp.float32)
+    unused_three, first_pull = jax.vjp(layer_norm, rows_in, gain_first, shift_first)
+    rows_from_norm, gain_first_grad, shift_first_grad = first_pull(normed_grad)
+    tokens_grad = from_home((middle_grad + rows_from_norm).astype(jnp.bfloat16)).astype(jnp.float32)
+
+    joint_sums = jnp.sum(joint_grad.astype(jnp.float32), 0)
+    small_grads = (
+        gain_first_grad,
+        shift_first_grad,
+        jnp.concatenate([joint_sums[:feature_count], joint_sums[2 * feature_count :]], 0),
+        jnp.sum(attended_grad.astype(jnp.float32), 0),
+        gain_second_grad,
+        shift_second_grad,
+        jnp.sum(hidden_grad.astype(jnp.float32), 0),
+        jnp.sum(branch_grad.astype(jnp.float32), 0),
+    )
+    devices = PLANE * DEPTH
+    small_packed = jnp.concatenate(
+        [g.reshape(devices, g.shape[0] // devices) for g in small_grads], 1
+    ).astype(jnp.bfloat16)
+    small_arrived = lax.all_to_all(small_packed, ("rep", "shard"), 0, 0, tiled=True)
+    small_sums = jnp.sum(small_arrived.astype(jnp.float32), 0)
+    sums = []
+    start = 0
+    for g in small_grads:
+        size = g.shape[0] // devices
+        sums.append(small_sums[start : start + size])
+        start += size
+    return (
+        layer_out,
+        tokens_grad,
+        sums[0],
+        sums[1],
+        qkv_grad,
+        sums[2],
+        out_grad,
+        sums[3],
+        sums[4],
+        sums[5],
+        up_grad,
+        sums[6],
+        down_grad,
+        sums[7],
+    )
+
+
 def solution(mesh):
     return jax.shard_map(
-        body,
+        body_planes if is_planes(mesh) else body_generic,
         mesh=mesh,
         in_specs=(
             P(("rep", "shard"), None),

time: 1100 us -> 508 us (0.46)
  waiting for transfers between devices: 782 us -> 136 us
  blocking collectives: 146 us -> 0 us
  starting transfers between devices: 32.6 us -> 155 us
  local copies, waits for them, and re-layouts: 30.9 us -> 79.1 us
  Pallas kernels: 0 us -> 16.5 us
  other arithmetic: 21.5 us -> 32.6 us
    all_gather x6 -> x4, waiting for transfers between devices: 422 us -> 0.03 us  [plane_rows(): return lax.all_gather(value, 'rep', axis=0, tiled=True)]
    reduce_scatter x4 -> x0, waiting for transfers between devices: 281 us -> none  [settle(): lax.psum_scatter(for_sending(grads), 'shard', scatter_dimension=0, tiled=...]
    ppermute x0 -> x48, starting transfers between devices: none -> 124 us  [the longest x27 100 us: over_z(): lax.ppermute(value, 'shard', [(i, (i + step) % DEPTH) for i in range(DEPT...]
    ppermute x0 -> x48, waiting for transfers between devices: none -> 100 us  [the longest x16 73 us: over_rep(): return lax.ppermute(value, 'rep', [(i, partner(i)) for i in range(PLANE)])]
    all_gather x8 -> x0, blocking collectives: 82.6 us -> none  [the longest x1 14.4 us: body(): lax.all_gather(owned[3], 'shard', axis=0, tiled=True)]
    all_to_all x3 -> x0, blocking collectives: 46.1 us -> none  [summed_on_arrival(): lax.all_to_all(blocks, axis, split_axis=0, concat_axis=0, tiled=True)]
    unnamed x14 -> x4, waiting for transfers between devices: 35.8 us -> 0.07 us
    unnamed x85 -> x155, local copies, waits for them, and re-layouts: 13.6 us -> 35.6 us
  transfers between devices with their start and end apart: 21 -> 59, of which waited for: 18 -> 20; matrix products, arithmetic and copies ran while one was open for 8% -> 30% of each run, Pallas kernels for 0% -> 3%
where the time goes in v1:
time: 508 us; the launch traced here: 498 us
  starting transfers between devices  155 us (31%)
  waiting for transfers between devices  136 us (27%)
  local copies, waits for them, and re-layouts  79.1 us (16%)
  matrix products  61.1 us (12%)
  other arithmetic  32.6 us (6%)
  between operations  17.4 us (3%)
  Pallas kernels  16.5 us (3%)
    ppermute x27, starting transfers between devices, over_z(): lax.ppermute(value, 'shard', [(i, (i + step) % DEPTH) for i in range(DEPT...  100 us
    ppermute x16, waiting for transfers between devices, over_rep(): return lax.ppermute(value, 'rep', [(i, partner(i)) for i in range(PLANE)])  73 us
    unnamed x155, local copies, waits for them, and re-layouts  35.6 us
    ppermute x27, waiting for transfers between devices, over_z(): lax.ppermute(value, 'shard', [(i, (i + step) % DEPTH) for i in range(DEPT...  27.4 us
    all_to_all x4, waiting for transfers between devices, by_plane(): arrived = lax.all_to_all(blocks, 'rep', 0, 0, tiled=True)  20.2 us
    ppermute x16, starting transfers between devices, over_rep(): return lax.ppermute(value, 'rep', [(i, partner(i)) for i in range(PLANE)])  18.1 us
    all_to_all x4, starting transfers between devices, by_plane(): arrived = lax.all_to_all(blocks, 'rep', 0, 0, tiled=True)  17.4 us
    pallas_call x4, Pallas kernels, assemble(): pl.pallas_call(kernel, out_shape=jax.ShapeDtypeStruct(whole, own.dtype),...  16.5 us
  transfers between devices with their start and end apart: 59, of which 20 were waited for; matrix products, arithmetic and copies ran while one was open for 30% of the time, Pallas kernels for 3%

profile of v1, /device:TPU:0, one launch (start us, length us, event | category | flops | bytes accessed | tf_op | source)
XLA Modules:
  0.0 498.1 jit_solution(13887089759117748003)
XLA Ops:
  14.0 5.1 %collective-permute-start.3 = (bf16[1,3072]{1,0:T(2,128)(2,1)S(1)}, bf16[1,3072]{1,0:T(2,128)(2,1)S(1)}, u32[]{:S(2)}, u32[]{:S(2)}) collective-permute-start(bf16[1,3072]{1,0:T(2,128)(2,1)S(1)} %reshape.675), channel_id=1, source_target_pairs={{0,3},{1,0},{2,1},{3,2},{4,7},{5,4},{6,5},{7,6},{8,11},{9,8},{10,9... | collective-permute-start | bytes 18440 | tf_op jit(solution)/shard_map/ppermute | solution.py:289
  52.0 6.7 %collective-permute-start.25 = (bf16[128,1024]{1,0:T(8,128)(2,1)}, bf16[128,1024]{1,0:T(8,128)(2,1)S(1)}, u32[]{:S(2)}, u32[]{:S(2)}) collective-permute-start(bf16[128,1024]{1,0:T(8,128)(2,1)} %constant_dynamic-slice_fusion), channel_id=1, source_target_pairs={{0,1},{1,2},{2,3},{3,0},{4,5},{5,6},{6,7},{7,4},{8,9},{9,10},{10,1... | collective-permute-start | bytes 786440 | tf_op jit(solution)/shard_map/ppermute | solution.py:289
  60.6 32.0 %collective-permute-start.26 = (bf16[128,1024]{1,0:T(8,128)(2,1)S(1)}, bf16[128,1024]{1,0:T(8,128)(2,1)S(1)}, u32[]{:S(2)}, u32[]{:S(2)}) collective-permute-start(bf16[128,1024]{1,0:T(8,128)(2,1)S(1)} %copy-done.48), channel_id=1, source_target_pairs={{0,2},{1,3},{2,0},{3,1},{4,6},{5,7},{6,4},{7,5},{8,10},{9,11},{10,... | collective-permute-start | bytes 786440 | tf_op jit(solution)/shard_map/ppermute | solution.py:289
  94.0 7.8 %collective-permute-start.13 = (bf16[32,1024]{1,0:T(8,128)(2,1)}, bf16[32,1024]{1,0:T(8,128)(2,1)S(1)}, u32[]{:S(2)}, u32[]{:S(2)}) collective-permute-start(bf16[32,1024]{1,0:T(8,128)(2,1)} %constant_dynamic-slice_fusion.2), channel_id=1, source_target_pairs={{0,1},{1,2},{2,3},{3,0},{4,5},{5,6},{6,7},{7,4},{8,9},{9,10},{10,1... | collective-permute-start | bytes 196616 | tf_op jit(solution)/shard_map/ppermute | solution.py:289
  118.0 12.5 %collective-permute-done.22 = bf16[96,4096]{1,0:T(8,128)(2,1)S(1)} collective-permute-done((bf16[96,4096]{1,0:T(8,128)(2,1)}, bf16[96,4096]{1,0:T(8,128)(2,1)S(1)}, u32[]{:S(2)}, u32[]{:S(2)}) %collective-permute-start.22) | collective-permute-done | bytes 786464 | tf_op jit(solution)/shard_map/ppermute | solution.py:285
  131.9 17.3 %collective-permute-done.8 = bf16[192,3072]{1,0:T(8,128)(2,1)S(1)} collective-permute-done((bf16[192,3072]{1,0:T(8,128)(2,1)S(1)}, bf16[192,3072]{1,0:T(8,128)(2,1)S(1)}, u32[]{:S(2)}, u32[]{:S(2)}) %collective-permute-start.8) | collective-permute-done | bytes 1179680 | tf_op jit(solution)/shard_map/ppermute | solution.py:285
  160.3 5.8 %collective-permute-done.23 = bf16[192,4096]{1,0:T(8,128)(2,1)S(1)} collective-permute-done((bf16[192,4096]{1,0:T(8,128)(2,1)S(1)}, bf16[192,4096]{1,0:T(8,128)(2,1)S(1)}, u32[]{:S(2)}, u32[]{:S(2)}) %collective-permute-start.23) | collective-permute-done | bytes 1572896 | tf_op jit(solution)/shard_map/ppermute | solution.py:285
  169.4 13.5 %collective-permute-done.29 = bf16[768,1024]{1,0:T(8,128)(2,1)S(1)} collective-permute-done((bf16[768,1024]{1,0:T(8,128)(2,1)S(1)}, bf16[768,1024]{1,0:T(8,128)(2,1)S(1)}, u32[]{:S(2)}, u32[]{:S(2)}) %collective-permute-start.29) | collective-permute-done | bytes 1572896 | tf_op jit(solution)/shard_map/ppermute | solution.py:285
  198.8 7.1 %shard_map.272 = bf16[1024,3072]{1,0:T(8,128)(2,1)S(1)} custom-call(bf16[256,3072]{1,0:T(8,128)(2,1)S(1)} %copy-done.5, bf16[384,3072]{1,0:T(8,128)(2,1)S(1)} %constant_dynamic-update-slice_fusion.8.refs_1_, bf16[384,3072]{1,0:T(8,128)(2,1)S(1)} %collective-permute-done.9.refs_2_), custom_call_target="tpu_custom_call" | custom-call | bytes 12582912 | tf_op jit(solution)/shard_map/pallas_call | solution.py:371
  213.7 11.1 %collective-permute-done.10 = bf16[2,128,1024]{2,1,0:T(8,128)(2,1)S(1)} collective-permute-done((bf16[2,128,1024]{2,1,0:T(8,128)(2,1)S(1)}, bf16[2,128,1024]{2,1,0:T(8,128)(2,1)S(1)}, u32[]{:S(2)}, u32[]{:S(2)}) %collective-permute-start.10) | collective-permute-done | bytes 524320 | tf_op jit(solution)/shard_map/ppermute | solution.py:285
  258.4 5.0 %fusion.89 = (f32[16,128]{1,0:T(8,128)S(1)}, f32[16,128,512]{2,1,0:T(8,128)}) fusion(f32[128,512]{1,0:T(8,128)S(1)} %copy-done.49, f32[16]{0:T(128)S(1)} %copy-done.54, pred[128,512]{1,0:T(8,128)(4,1)S(1)} %copy-done.52, bf16[128,16,64]{0,2,1:T(8,128)(2,1)S(1)} %bitcast.224, bf16[512,16,64]{0,2,1:T(8,128)(2,1)} %bitcast.216), kind=kOutput, calls=%fused_computation.232 | convolution fusion | flops 140509696 | bytes 5840960 | tf_op jit(solution)/shard_map/sub | solution.py:528
  267.9 6.4 %multiply_convert_fusion.1 = (bf16[128,4096]{1,0:T(8,128)(2,1)}, f32[128,4096]{1,0:T(8,128)S(1)}) fusion(f32[4096]{0:T(1024)S(1)} %bitcast.250, bf16[128,1024]{1,0:T(8,128)(2,1)S(1)} %add_convert_fusion.1, bf16[1024,4096]{1,0:T(8,128)(2,1)} %copy-done.2), kind=kOutput, calls=%fused_computation.27 | convolution fusion | flops 1078984704 | bytes 11812864 | tf_op jit(solution)/shard_map/dot_general | solution.py:540
  274.3 7.2 %fusion.80 = (bf16[4096]{0:T(1024)(128)(2,1)S(1)}, bf16[128,4096]{1,0:T(8,128)(2,1)S(1)}) fusion(f32[128,4096]{1,0:T(8,128)S(1)} %get-tuple-element.79, bf16[128,1024]{1,0:T(8,128)(2,1)S(1)} %copy-done.44, bf16[4096,1024]{1,0:T(8,128)(2,1)} %copy-done.1), kind=kOutput, calls=%fused_computation.225 | convolution fusion | flops 1084747776 | bytes 11804672 | tf_op jit(solution)/shard_map/dot_general | solution.py:546
  317.0 5.8 %fusion.23 = bf16[128,1024]{1,0:T(8,128)(2,1)} fusion(f32[128,1024]{1,0:T(8,128)S(1)} %get-tuple-element.77, bf16[128,4096]{1,0:T(8,128)(2,1)} %get-tuple-element.78, bf16[4096,1024]{1,0:T(8,128)(2,1)} %copy-done.1, f32[1024]{0:T(1024)S(1)} %bitcast.249), kind=kOutput, calls=%fused_computation.43 | convolution fusion | flops 1074135040 | bytes 10227712 | tf_op jit(solution)/shard_map/dot_general | solution.py:542
  336.9 4.3 fusion.94
  351.7 4.9 all-to-all-start.1
  356.6 5.1 %fusion.77 = (bf16[1024]{0:T(1024)(128)(2,1)S(1)}, f32[128]{0:T(128)S(1)}, f32[128,1024]{1,0:T(8,128)S(1)}) fusion(f32[1024]{0:T(1024)S(1)} %bitcast.238, f32[128]{0:T(128)S(1)} %broadcast_multiply_fusion.1, bf16[128,1024]{1,0:T(8,128)(2,1)S(1)} %copy-done.12, bf16[128,3072]{0,1:T(8,128)(2,1)S(1)} %get-tuple-element.36, bf16[1024,3072]{1,0:T(8,128)(2,1)} %copy-done), kind=kOutput, calls=%fused_computation.223 | convolution fusion | flops 806091648 | bytes 7871488 | tf_op jit(solution)/shard_map/dot_general | solution.py:599
  361.7 7.6 %all-to-all-done.1 = bf16[8,128,384]{2,1,0:T(8,128)(2,1)} async-done(((bf16[8,128,384]{2,1,0:T(8,128)(2,1)}), bf16[8,128,384]{2,1,0:T(8,128)(2,1)}, u32[]{:S(2)}, u32[]{:S(2)}) %all-to-all-start.1) | async-done | bytes 786464 | tf_op jit(solution)/shard_map/all_to_all | solution.py:401
  383.2 13.6 %collective-permute-start.45 = (bf16[128,1024]{1,0:T(8,128)(2,1)S(1)}, bf16[128,1024]{1,0:T(8,128)(2,1)S(1)}, u32[]{:S(2)}, u32[]{:S(2)}) collective-permute-start(bf16[128,1024]{1,0:T(8,128)(2,1)S(1)} %get-tuple-element.43), channel_id=1, source_target_pairs={{0,1},{1,2},{2,3},{3,0},{4,5},{5,6},{6,7},{7,4},{8,9},{9,10},{10,1... | collective-permute-start | bytes 786440 | tf_op jit(solution)/shard_map/ppermute | solution.py:289
  403.4 5.4 %all-to-all-done = bf16[32,2,192]{2,1,0:T(2,128)(2,1)S(1)} async-done(((bf16[32,2,192]{2,1,0:T(2,128)(2,1)}), bf16[32,2,192]{2,1,0:T(2,128)(2,1)S(1)}, u32[]{:S(2)}, u32[]{:S(2)}) %all-to-all-start) | async-done | bytes 24608 | tf_op jit(solution)/shard_map/all_to_all | solution.py:619
  430.4 10.2 %all-to-all-done.4 = bf16[8,128,512]{2,1,0:T(8,128)(2,1)} async-done(((bf16[8,128,512]{2,1,0:T(8,128)(2,1)}), bf16[8,128,512]{2,1,0:T(8,128)(2,1)}, u32[]{:S(2)}, u32[]{:S(2)}) %all-to-all-start.4) | async-done | bytes 1048608 | tf_op jit(solution)/shard_map/all_to_all | solution.py:401
  456.6 17.5 %collective-permute-done.43 = bf16[8,32,512]{2,1,0:T(8,128)(2,1)S(1)} collective-permute-done((bf16[8,32,512]{2,1,0:T(8,128)(2,1)S(1)}, bf16[8,32,512]{2,1,0:T(8,128)(2,1)S(1)}, u32[]{:S(2)}, u32[]{:S(2)}) %collective-permute-start.43) | collective-permute-done | bytes 262176 | tf_op jit(solution)/shard_map/ppermute | solution.py:289
  475.9 7.3 %all-to-all-start.5 = ((bf16[8,32,512]{2,1,0:T(8,128)(2,1)}), bf16[8,32,512]{2,1,0:T(8,128)(2,1)S(1)}, u32[]{:S(2)}, u32[]{:S(2)}) async-start(bf16[8,32,512]{2,1,0:T(8,128)(2,1)} %fusion.46), calls=%async_computation.5 | async-start | bytes 524288 | tf_op jit(solution)/shard_map/all_to_all | solution.py:419
  484.0 6.2 %all-to-all-done.5 = bf16[8,32,512]{2,1,0:T(8,128)(2,1)S(1)} async-done(((bf16[8,32,512]{2,1,0:T(8,128)(2,1)}), bf16[8,32,512]{2,1,0:T(8,128)(2,1)S(1)}, u32[]{:S(2)}, u32[]{:S(2)}) %all-to-all-start.5) | async-done | bytes 262176 | tf_op jit(solution)/shard_map/all_to_all | solution.py:419
  (385 shorter events, 255.1 us)
Async XLA Ops:
  7.2 296.8 %all-gather.5.cloned.1.call-start = ((), (), s32[]{:S(2)}) async-start(), calls=%async_computation.7 | async-start | bytes 2359296 | tf_op jit(solution)/shard_map/all_gather | solution.py:406
  40.9 51.8 %collective-permute-start.19 = (bf16[32,4096]{1,0:T(8,128)(2,1)}, bf16[32,4096]{1,0:T(8,128)(2,1)S(1)}, u32[]{:S(2)}, u32[]{:S(2)}) collective-permute-start(bf16[32,4096]{1,0:T(8,128)(2,1)} %constant_dynamic-slice_fusion.1), channel_id=1, source_target_pairs={{0,1},{1,2},{2,3},{3,0},{4,5},{5,6},{6,7},{7,4},{8,9},{9,10},{10,1... | collective-permute-start | bytes 786440 | tf_op jit(solution)/shard_map/ppermute | solution.py:289
  41.5 51.3 %collective-permute-start.20 = (bf16[32,4096]{1,0:T(8,128)(2,1)}, bf16[32,4096]{1,0:T(8,128)(2,1)S(1)}, u32[]{:S(2)}, u32[]{:S(2)}) collective-permute-start(bf16[32,4096]{1,0:T(8,128)(2,1)} %constant_dynamic-slice_fusion.1), channel_id=1, source_target_pairs={{0,2},{1,3},{2,0},{3,1},{4,6},{5,7},{6,4},{7,5},{8,10},{9,11},{10,... | collective-permute-start | bytes 786440 | tf_op jit(solution)/shard_map/ppermute | solution.py:289
  43.7 50.3 %collective-permute-start.21 = (bf16[32,4096]{1,0:T(8,128)(2,1)}, bf16[32,4096]{1,0:T(8,128)(2,1)S(1)}, u32[]{:S(2)}, u32[]{:S(2)}) collective-permute-start(bf16[32,4096]{1,0:T(8,128)(2,1)} %constant_dynamic-slice_fusion.1), channel_id=1, source_target_pairs={{0,3},{1,0},{2,1},{3,2},{4,7},{5,4},{6,5},{7,6},{8,11},{9,8},{10,9... | collective-permute-start | bytes 786440 | tf_op jit(solution)/shard_map/ppermute | solution.py:289
  52.0 51.0 %collective-permute-start.25 = (bf16[128,1024]{1,0:T(8,128)(2,1)}, bf16[128,1024]{1,0:T(8,128)(2,1)S(1)}, u32[]{:S(2)}, u32[]{:S(2)}) collective-permute-start(bf16[128,1024]{1,0:T(8,128)(2,1)} %constant_dynamic-slice_fusion), channel_id=1, source_target_pairs={{0,1},{1,2},{2,3},{3,0},{4,5},{5,6},{6,7},{7,4},{8,9},{9,10},{10,1... | collective-permute-start | bytes 786440 | tf_op jit(solution)/shard_map/ppermute | solution.py:289
  60.6 42.7 %collective-permute-start.26 = (bf16[128,1024]{1,0:T(8,128)(2,1)S(1)}, bf16[128,1024]{1,0:T(8,128)(2,1)S(1)}, u32[]{:S(2)}, u32[]{:S(2)}) collective-permute-start(bf16[128,1024]{1,0:T(8,128)(2,1)S(1)} %copy-done.48), channel_id=1, source_target_pairs={{0,2},{1,3},{2,0},{3,1},{4,6},{5,7},{6,4},{7,5},{8,10},{9,11},{10,... | collective-permute-start | bytes 786440 | tf_op jit(solution)/shard_map/ppermute | solution.py:289
  92.8 93.6 %collective-permute-start.12 = (f32[1,1]{1,0:T(1,128)}, f32[1,1]{1,0:T(1,128)}, u32[]{:S(2)}, u32[]{:S(2)}) collective-permute-start(f32[1,1]{1,0:T(1,128)} %bitcast.5), channel_id=1, source_target_pairs={{0,0},{1,4},{2,8},{3,12},{4,16},{5,20},{6,24},{7,28},{8,1},{9,5},{... | collective-permute-start | bytes 20 | tf_op jit(solution)/shard_map/ppermute | solution.py:311
  94.0 95.5 %collective-permute-start.13 = (bf16[32,1024]{1,0:T(8,128)(2,1)}, bf16[32,1024]{1,0:T(8,128)(2,1)S(1)}, u32[]{:S(2)}, u32[]{:S(2)}) collective-permute-start(bf16[32,1024]{1,0:T(8,128)(2,1)} %constant_dynamic-slice_fusion.2), channel_id=1, source_target_pairs={{0,1},{1,2},{2,3},{3,0},{4,5},{5,6},{6,7},{7,4},{8,9},{9,10},{10,1... | collective-permute-start | bytes 196616 | tf_op jit(solution)/shard_map/ppermute | solution.py:289
  106.2 46.8 %collective-permute-start.28 = (bf16[384,1024]{1,0:T(8,128)(2,1)}, bf16[384,1024]{1,0:T(8,128)(2,1)}, u32[]{:S(2)}, u32[]{:S(2)}) collective-permute-start(bf16[384,1024]{1,0:T(8,128)(2,1)} %pad_maximum_fusion.7), channel_id=1, source_target_pairs={{0,8},{4,20},{8,0},{12,28},{16,24},{20,4},{24,16},{28,12},{1,9},{5... | collective-permute-start | bytes 2359304 | tf_op jit(solution)/shard_map/ppermute | solution.py:285
  107.3 229.6 %all-gather.11.cloned.1.call-start = ((), (), s32[]{:S(2)}) async-start(), calls=%async_computation.10 | async-start | bytes 2359296 | tf_op jit(solution)/shard_map/all_gather | solution.py:406
  114.6 34.6 %collective-permute-start.8 = (bf16[192,3072]{1,0:T(8,128)(2,1)S(1)}, bf16[192,3072]{1,0:T(8,128)(2,1)S(1)}, u32[]{:S(2)}, u32[]{:S(2)}) collective-permute-start(bf16[192,3072]{1,0:T(8,128)(2,1)S(1)} %pad_maximum_fusion.4), channel_id=1, source_target_pairs={{0,16},{4,12},{8,24},{12,4},{16,0},{20,28},{24,8},{28,20},{1,17},{... | collective-permute-start | bytes 3538952 | tf_op jit(solution)/shard_map/ppermute | solution.py:285
  130.6 35.5 %collective-permute-start.23 = (bf16[192,4096]{1,0:T(8,128)(2,1)S(1)}, bf16[192,4096]{1,0:T(8,128)(2,1)S(1)}, u32[]{:S(2)}, u32[]{:S(2)}) collective-permute-start(bf16[192,4096]{1,0:T(8,128)(2,1)S(1)} %pad_maximum_fusion.2), channel_id=1, source_target_pairs={{0,16},{4,12},{8,24},{12,4},{16,0},{20,28},{24,8},{28,20},{1,17},{... | collective-permute-start | bytes 4718600 | tf_op jit(solution)/shard_map/ppermute | solution.py:285
  149.3 49.4 %collective-permute-start.9 = (bf16[384,3072]{1,0:T(8,128)(2,1)S(1)}, bf16[384,3072]{1,0:T(8,128)(2,1)S(1)}, u32[]{:S(2)}, u32[]{:S(2)}) collective-permute-start(bf16[384,3072]{1,0:T(8,128)(2,1)S(1)} %constant_dynamic-update-slice_fusion.8.refs_1_), channel_id=1, source_target_pairs={{0,4},{4,0},{8,12},{12,8},{16,20},{20,16},{24,28},{28,24},{1,5},{5... | collective-permute-start | bytes 7077896 | tf_op jit(solution)/shard_map/ppermute | solution.py:285
  154.3 28.6 %collective-permute-start.29 = (bf16[768,1024]{1,0:T(8,128)(2,1)S(1)}, bf16[768,1024]{1,0:T(8,128)(2,1)S(1)}, u32[]{:S(2)}, u32[]{:S(2)}) collective-permute-start(bf16[768,1024]{1,0:T(8,128)(2,1)S(1)} %pad_maximum_fusion.3), channel_id=1, source_target_pairs={{0,16},{4,12},{8,24},{12,4},{16,0},{20,28},{24,8},{28,20},{1,17},{... | collective-permute-start | bytes 4718600 | tf_op jit(solution)/shard_map/ppermute | solution.py:285
  167.4 68.0 %collective-permute-start.24 = (bf16[384,4096]{1,0:T(8,128)(2,1)}, bf16[384,4096]{1,0:T(8,128)(2,1)}, u32[]{:S(2)}, u32[]{:S(2)}) collective-permute-start(bf16[384,4096]{1,0:T(8,128)(2,1)} %constant_dynamic-update-slice_fusion.18.refs_1_), channel_id=1, source_target_pairs={{0,4},{4,0},{8,12},{12,8},{16,20},{20,16},{24,28},{28,24},{1,5},{5... | collective-permute-start | bytes 9437192 | tf_op jit(solution)/shard_map/ppermute | solution.py:285
  184.2 59.5 %collective-permute-start.30 = (bf16[1536,1024]{1,0:T(8,128)(2,1)}, bf16[1536,1024]{1,0:T(8,128)(2,1)}, u32[]{:S(2)}, u32[]{:S(2)}) collective-permute-start(bf16[1536,1024]{1,0:T(8,128)(2,1)} %constant_dynamic-update-slice_fusion.23.refs_1_), channel_id=1, source_target_pairs={{0,4},{4,0},{8,12},{12,8},{16,20},{20,16},{24,28},{28,24},{1,5},{5... | collective-permute-start | bytes 9437192 | tf_op jit(solution)/shard_map/ppermute | solution.py:285
  192.5 35.5 %collective-permute-start.32 = (bf16[128,1024]{1,0:T(8,128)(2,1)S(1)}, bf16[128,1024]{1,0:T(8,128)(2,1)S(1)}, u32[]{:S(2)}, u32[]{:S(2)}) collective-permute-start(bf16[128,1024]{1,0:T(8,128)(2,1)S(1)} %copy-done.53), channel_id=1, source_target_pairs={{0,0},{1,4},{2,8},{3,12},{4,16},{5,20},{6,24},{7,28},{8,1},{9,5},{... | collective-permute-start | bytes 786440 | tf_op jit(solution)/shard_map/ppermute | solution.py:311
  228.9 198.6 %all-gather.9.cloned.1.call-start = ((), (), s32[]{:S(2)}) async-start(), calls=%async_computation.9 | async-start | bytes 2359296 | tf_op jit(solution)/shard_map/all_gather | solution.py:406
  316.9 133.7 %all-gather.7.cloned.1.call-start = ((), (), s32[]{:S(2)}) async-start(), calls=%async_computation.8 | async-start | bytes 2359296 | tf_op jit(solution)/shard_map/all_gather | solution.py:406
  342.0 70.2 %collective-permute-start.47 = (bf16[128,1024]{1,0:T(8,128)(2,1)}, bf16[128,1024]{1,0:T(8,128)(2,1)}, u32[]{:S(2)}, u32[]{:S(2)}) collective-permute-start(bf16[128,1024]{1,0:T(8,128)(2,1)} %get-tuple-element.44), channel_id=1, source_target_pairs={{0,3},{1,0},{2,1},{3,2},{4,7},{5,4},{6,5},{7,6},{8,11},{9,8},{10,9... | collective-permute-start | bytes 786440 | tf_op jit(solution)/shard_map/ppermute | solution.py:289
  346.2 66.0 %collective-permute-start.46 = (bf16[128,1024]{1,0:T(8,128)(2,1)S(1)}, bf16[128,1024]{1,0:T(8,128)(2,1)}, u32[]{:S(2)}, u32[]{:S(2)}) collective-permute-start(bf16[128,1024]{1,0:T(8,128)(2,1)S(1)} %get-tuple-element.45), channel_id=1, source_target_pairs={{0,2},{1,3},{2,0},{3,1},{4,6},{5,7},{6,4},{7,5},{8,10},{9,11},{10,... | collective-permute-start | bytes 786440 | tf_op jit(solution)/shard_map/ppermute | solution.py:289
  383.2 29.0 %collective-permute-start.45 = (bf16[128,1024]{1,0:T(8,128)(2,1)S(1)}, bf16[128,1024]{1,0:T(8,128)(2,1)S(1)}, u32[]{:S(2)}, u32[]{:S(2)}) collective-permute-start(bf16[128,1024]{1,0:T(8,128)(2,1)S(1)} %get-tuple-element.43), channel_id=1, source_target_pairs={{0,1},{1,2},{2,3},{3,0},{4,5},{5,6},{6,7},{7,4},{8,9},{9,10},{10,1... | collective-permute-start | bytes 786440 | tf_op jit(solution)/shard_map/ppermute | solution.py:289
  452.7 30.6 %collective-permute-start.41 = (bf16[32,1024]{1,0:T(8,128)(2,1)S(1)}, bf16[32,1024]{1,0:T(8,128)(2,1)S(1)}, u32[]{:S(2)}, u32[]{:S(2)}) collective-permute-start(bf16[32,1024]{1,0:T(8,128)(2,1)S(1)} %get-tuple-element.55), channel_id=1, source_target_pairs={{0,3},{1,0},{2,1},{3,2},{4,7},{5,4},{6,5},{7,6},{8,11},{9,8},{10,9... | collective-permute-start | bytes 196616 | tf_op jit(solution)/shard_map/ppermute | solution.py:289
  454.6 28.6 %collective-permute-start.40 = (bf16[32,1024]{1,0:T(8,128)(2,1)S(1)}, bf16[32,1024]{1,0:T(8,128)(2,1)S(1)}, u32[]{:S(2)}, u32[]{:S(2)}) collective-permute-start(bf16[32,1024]{1,0:T(8,128)(2,1)S(1)} %get-tuple-element.56), channel_id=1, source_target_pairs={{0,2},{1,3},{2,0},{3,1},{4,6},{5,7},{6,4},{7,5},{8,10},{9,11},{10,... | collective-permute-start | bytes 196616 | tf_op jit(solution)/shard_map/ppermute | solution.py:289
  (92 other events, 1209.1 us)
Sparse Core Ops, SparseCore 0:
  107.4 36.9 all-gather.4
  229.0 25.9 all-gather.10
  289.5 28.0 all-gather.8
  331.2 30.1 all-gather.6

commit v2 on v0

--- a/solution.py
+++ b/solution.py
@@ -3,6 +3,8 @@
 import jax
 import jax.numpy as jnp
 from jax import lax
+from jax.experimental import pallas as pl
+from jax.experimental.pallas import tpu as pltpu
 from jax.sharding import PartitionSpec as P
 
 HEADS = 16
@@ -66,7 +68,7 @@
     return jnp.where(allowed[None], raw_scores, -1e30)
 
 
-def body(
+def body_generic(
     tokens,
     cotangent,
     lengths,
@@ -270,9 +272,560 @@
     )
 
 
+PLANE = 8
+DEPTH = 4
+QUARTERS = 4
+VMEM_BYTES = 48 * 2**20
+
+
+def is_planes(mesh):
+    return mesh.shape["rep"] == PLANE and mesh.shape["shard"] == DEPTH
+
+
+def over_rep(value, flip):
+    return lax.ppermute(value, "rep", [(i, i ^ flip) for i in range(PLANE)])
+
+
+def over_z(value, step):
+    return lax.ppermute(value, "shard", [(i, (i + step) % DEPTH) for i in range(DEPTH)])
+
+
+def over_all(value, place):
+    pairs = [(i, place(i)) for i in range(PLANE * DEPTH) if place(i) is not None]
+    return lax.ppermute(value, ("rep", "shard"), pairs)
+
+
+def home_of(index):
+    rep, z = index // DEPTH, index % DEPTH
+    return ((rep & 1) * 4 + z) * DEPTH + rep // 2
+
+
+HOME = [home_of(i) for i in range(PLANE * DEPTH)]
+
+
+def to_home(value):
+    return over_all(value, lambda i: HOME[i])
+
+
+def from_home(value):
+    return over_all(value, HOME.index)
+
+
+def after(value, *earlier):
+    return lax.optimization_barrier((value, *earlier))[0]
+
+
+def gather_plane(rows):
+    beside = [over_rep(rows, flip) for flip in (2, 4, 6)]
+    quad = jnp.stack([rows, *beside], 0).reshape(2, 1, 2, *rows.shape)
+    return jnp.concatenate([quad, over_rep(quad, 1)], 1).reshape(-1, rows.shape[1])
+
+
+def scatter_plane(keep, give):
+    both = keep.astype(jnp.float32) + over_rep(give, 1).astype(jnp.float32)
+    total = both[0, 0]
+    for flip, part in ((2, both[0, 1]), (4, both[1, 0]), (6, both[1, 1])):
+        total = total + over_rep(part.astype(jnp.bfloat16), flip).astype(jnp.float32)
+    return total
+
+
+def block_at(blocks, index):
+    return lax.dynamic_index_in_dim(blocks, index, 0, keepdims=False)
+
+
+def summed_over_z(blocks):
+    z = lax.axis_index("shard")
+    low = blocks.astype(jnp.bfloat16)
+    total = block_at(blocks, z)
+    for step in (1, 2, 3):
+        sent = block_at(low, lax.rem(z + step, DEPTH))
+        total = total + over_z(sent, step).astype(jnp.float32)
+    return total
+
+
+def outer(left, right):
+    return lax.dot_general(
+        left, right, (((0,), (0,)), ((), ())), preferred_element_type=jnp.float32
+    )
+
+
+def column_parts_to_rows(grad):
+    rows, width = grad.shape
+    parts = grad.reshape(PLANE, DEPTH, rows // (PLANE * DEPTH), width)
+    summed = summed_over_z(jnp.swapaxes(parts, 0, 1)).astype(jnp.bfloat16)
+    arrived = lax.all_to_all(summed, "rep", 0, 0, tiled=True)
+    block = rows // (PLANE * DEPTH)
+    spread = arrived.reshape(PLANE, block, -1, 128)
+    return jnp.transpose(spread, (1, 2, 0, 3)).reshape(block, -1).astype(jnp.float32)
+
+
+def dot_nn(left, right):
+    return jnp.dot(left, right, preferred_element_type=jnp.float32)
+
+
+def dot_nt(left, right):
+    return lax.dot_general(
+        left, right, (((1,), (1,)), ((), ())), preferred_element_type=jnp.float32
+    )
+
+
+def place_pieces(pieces, whole, sems):
+    z = lax.axis_index("shard")
+    rows = pieces[0].shape[0]
+    copies = []
+    for step, piece in enumerate(pieces):
+        plane = lax.rem(z + (DEPTH - step), DEPTH)
+        at = pl.ds(pl.multiple_of(plane * rows, rows), rows)
+        copies.append(pltpu.make_async_copy(piece, whole.at[at], sems.at[step]))
+    for copy in copies:
+        copy.start()
+    return copies
+
+
+def wait_all(copies):
+    for copy in copies:
+        copy.wait()
+
+
+def row_positions(shape, axis, rep, first):
+    index = lax.broadcasted_iota(jnp.int32, shape, axis) + first
+    block = index >> 7
+    x = (block & 1) ^ ((rep >> 1) & 1)
+    core = (block >> 1) ^ (rep & 1)
+    return ((x * 2 + core) << 7) + (index & 127)
+
+
+def scores_of(query, keys, slope, distance, allowed, scale):
+    raw = dot_nt(query, keys) * scale - slope * distance
+    return jnp.where(allowed, raw, -1e30)
+
+
+ANYWHERE = pl.BlockSpec(memory_space=pl.ANY)
+LOCAL = pl.BlockSpec(memory_space=pltpu.VMEM)
+SCALARS = pl.BlockSpec(memory_space=pltpu.SMEM)
+
+
+def sds(shape, dtype):
+    return jax.ShapeDtypeStruct(shape, dtype)
+
+
+def kernel_call(kernel, ins, outs, scratch, flops, operands):
+    return pl.pallas_call(
+        kernel,
+        out_shape=outs,
+        in_specs=ins,
+        out_specs=[LOCAL] * len(outs),
+        scratch_shapes=scratch,
+        compiler_params=pltpu.CompilerParams(vmem_limit_bytes=VMEM_BYTES),
+        cost_estimate=pl.CostEstimate(flops=flops, bytes_accessed=2**23, transcendentals=2**20),
+    )(*operands)
+
+
+def attention_forward(lens, slopes, normed, weights, out_part, bias_q, bias_v):
+    rows, features = normed.shape
+    span = rows // 2
+    width = weights[0].shape[1]
+    own = width // 3
+    head_size = own // 2
+    scale = 1.0 / math.sqrt(head_size)
+    step_rows = span // QUARTERS
+
+    def kernel(
+        lens_ref, slopes_ref, normed_ref, w0, w1, w2, w3, out_ref, bq_ref, bv_ref,
+        joint_ref, mixed_ref, keep_ref, give_ref, weight_ref, sems,
+    ):
+        rep = lax.axis_index("rep")
+        wait_all(place_pieces((w0, w1, w2, w3), weight_ref, sems))
+        for s in range(2):
+            for c in range(2):
+                at = pl.ds((2 * s + c) * (span // 2), span // 2)
+                joint = dot_nn(normed_ref[at, :], weight_ref[...])
+                joint_ref[at, :own] = (joint[:, :own] + bq_ref[...]).astype(jnp.bfloat16)
+                joint_ref[at, own : 2 * own] = joint[:, own : 2 * own].astype(jnp.bfloat16)
+                joint_ref[at, 2 * own :] = (joint[:, 2 * own :] + bv_ref[...]).astype(jnp.bfloat16)
+        lane = lax.broadcasted_iota(jnp.int32, (step_rows, own), 1)
+        key_pos = row_positions((1, span), 1, rep, 0)
+        for s in range(2):
+            keys = joint_ref[pl.ds(s * span, span), own : 2 * own]
+            values = joint_ref[pl.ds(s * span, span), 2 * own :]
+
+            @pl.loop(0, QUARTERS)
+            def _(i):
+                first = pl.multiple_of(i * step_rows, step_rows)
+                at = pl.ds(s * span + first, step_rows)
+                query_pos = row_positions((step_rows, 1), 0, rep, first)
+                allowed = (key_pos <= query_pos) & (key_pos < lens_ref[s])
+                distance = (query_pos - key_pos).astype(jnp.float32)
+                query = joint_ref[at, :own]
+                mixed = jnp.zeros((step_rows, own), jnp.float32)
+                for j in range(2):
+                    mine = (lane >= j * head_size) & (lane < (j + 1) * head_size)
+                    masked = jnp.where(mine, query, jnp.zeros_like(query))
+                    scores = scores_of(masked, keys, slopes_ref[j], distance, allowed, scale)
+                    top = jnp.max(scores, 1, keepdims=True)
+                    exps = jnp.exp(scores - top)
+                    probs = exps / jnp.sum(exps, 1, keepdims=True)
+                    mixed = jnp.where(mine, dot_nn(probs.astype(jnp.bfloat16), values), mixed)
+                mixed_ref[at, :] = mixed.astype(jnp.bfloat16)
+
+            for c, part_ref in enumerate((keep_ref, give_ref)):
+                at = pl.ds((2 * s + c) * (span // 2), span // 2)
+                part = dot_nn(mixed_ref[at, :], out_ref[...]).astype(jnp.bfloat16)
+                part_ref[s] = part.reshape(2, span // 4, features)
+
+    half = sds((2, 2, span // 4, features), jnp.bfloat16)
+    return kernel_call(
+        kernel,
+        [SCALARS, SCALARS, LOCAL] + [ANYWHERE] * 4 + [LOCAL] * 3,
+        [sds((rows, width), jnp.bfloat16), sds((rows, own), jnp.bfloat16), half, half],
+        [pltpu.VMEM((features, width), jnp.bfloat16), pltpu.SemaphoreType.DMA((DEPTH,))],
+        2 * rows * features * (width + own) + 8 * rows * span * own,
+        (lens, slopes, normed, *weights, out_part, bias_q, bias_v),
+    )
+
+
+def attention_backward(lens, slopes, grad, joint, weights, out_part):
+    rows, features = grad.shape
+    span = rows // 2
+    width = weights[0].shape[1]
+    own = width // 3
+    head_size = own // 2
+    scale = 1.0 / math.sqrt(head_size)
+    step_rows = span // QUARTERS
+
+    def kernel(
+        lens_ref, slopes_ref, grad_ref, joint_ref, w0, w1, w2, w3, out_ref,
+        joint_grad_ref, sums_ref, keep_ref, give_ref,
+        weight_ref, mixed_grad_ref, key_acc, value_acc, sems,
+    ):
+        rep = lax.axis_index("rep")
+        copies = place_pieces((w0, w1, w2, w3), weight_ref, sems)
+        for s in range(2):
+            for c in range(2):
+                at = pl.ds((2 * s + c) * (span // 2), span // 2)
+                mixed_grad_ref[at, :] = dot_nt(grad_ref[at, :], out_ref[...]).astype(jnp.bfloat16)
+        lane = lax.broadcasted_iota(jnp.int32, (step_rows, own), 1)
+        lane_all = lax.broadcasted_iota(jnp.int32, (span, own), 1)
+        key_pos = row_positions((1, span), 1, rep, 0)
+        for s in range(2):
+            keys = joint_ref[pl.ds(s * span, span), own : 2 * own]
+            values = joint_ref[pl.ds(s * span, span), 2 * own :]
+            key_acc[...] = jnp.zeros_like(key_acc)
+            value_acc[...] = jnp.zeros_like(value_acc)
+
+            @pl.loop(0, QUARTERS)
+            def _(i):
+                first = pl.multiple_of(i * step_rows, step_rows)
+                at = pl.ds(s * span + first, step_rows)
+                query_pos = row_positions((step_rows, 1), 0, rep, first)
+                allowed = (key_pos <= query_pos) & (key_pos < lens_ref[s])
+                distance = (query_pos - key_pos).astype(jnp.float32)
+                query = joint_ref[at, :own]
+                mixed_grad = mixed_grad_ref[at, :]
+                query_grad = jnp.zeros((step_rows, own), jnp.float32)
+                for j in range(2):
+                    mine = (lane >= j * head_size) & (lane < (j + 1) * head_size)
+                    masked = jnp.where(mine, query, jnp.zeros_like(query))
+                    masked_grad = jnp.where(mine, mixed_grad, jnp.zeros_like(mixed_grad))
+                    scores = scores_of(masked, keys, slopes_ref[j], distance, allowed, scale)
+                    top = jnp.max(scores, 1, keepdims=True)
+                    exps = jnp.exp(scores - top)
+                    probs = exps / jnp.sum(exps, 1, keepdims=True)
+                    probs_grad = dot_nt(masked_grad, values)
+                    row_dot = jnp.sum(probs * probs_grad, 1, keepdims=True)
+                    score_grad = (probs * (probs_grad - row_dot)).astype(jnp.bfloat16)
+                    query_grad = jnp.where(mine, dot_nn(score_grad, keys), query_grad)
+                    key_acc[...] += outer(score_grad, masked)
+                    value_acc[...] += outer(probs.astype(jnp.bfloat16), masked_grad)
+                joint_grad_ref[at, :own] = (query_grad * scale).astype(jnp.bfloat16)
+
+            at = pl.ds(s * span, span)
+            joint_grad_ref[at, own : 2 * own] = (key_acc[...] * scale).astype(jnp.bfloat16)
+            joint_grad_ref[at, 2 * own :] = value_acc[...].astype(jnp.bfloat16)
+        wait_all(copies)
+        total = jnp.zeros((1, width), jnp.float32)
+        for s in range(2):
+            for c, part_ref in enumerate((keep_ref, give_ref)):
+                at = pl.ds((2 * s + c) * (span // 2), span // 2)
+                joint_grad = joint_grad_ref[at, :]
+                total = total + jnp.sum(joint_grad.astype(jnp.float32), 0, keepdims=True)
+                part = dot_nt(joint_grad, weight_ref[...]).astype(jnp.bfloat16)
+                part_ref[s] = part.reshape(2, span // 4, features)
+        sums_ref[...] = total
+
+    half = sds((2, 2, span // 4, features), jnp.bfloat16)
+    return kernel_call(
+        kernel,
+        [SCALARS, SCALARS, LOCAL, LOCAL] + [ANYWHERE] * 4 + [LOCAL],
+        [sds((rows, width), jnp.bfloat16), sds((1, width), jnp.float32), half, half],
+        [
+            pltpu.VMEM((features, width), jnp.bfloat16),
+            pltpu.VMEM((rows, own), jnp.bfloat16),
+            pltpu.VMEM((span, own), jnp.float32),
+            pltpu.VMEM((span, own), jnp.float32),
+            pltpu.SemaphoreType.DMA((DEPTH,)),
+        ],
+        2 * rows * features * (width + own) + 20 * rows * span * own,
+        (lens, slopes, grad, joint, *weights, out_part),
+    )
+
+
+def feed_forward(normed, grad, ups, downs, bias_up):
+    rows, features = normed.shape
+    units = ups[0].shape[1]
+    tile = rows // 4
+    root = math.sqrt(2.0 / math.pi)
+    bend = 0.044715
+
+    def kernel(
+        normed_ref, grad_ref, u0, u1, u2, u3, d0, d1, d2, d3, bias_ref,
+        active_ref, hidden_grad_ref, sums_ref, keep_ref, give_ref, back_keep_ref, back_give_ref,
+        up_ref, down_ref, sems,
+    ):
+        up_copies = place_pieces((u0, u1, u2, u3), up_ref, sems.at[0])
+        down_copies = place_pieces((d0, d1, d2, d3), down_ref, sems.at[1])
+        wait_all(up_copies)
+        wait_all(down_copies)
+        sums_ref[...] = jnp.zeros_like(sums_ref)
+
+        @pl.loop(0, 2)
+        def _(s):
+            for c in range(2):
+                at = pl.ds(pl.multiple_of((2 * s + c) * tile, tile), tile)
+                v = dot_nn(normed_ref[at, :], up_ref[...]) + bias_ref[...]
+                square = v * v
+                t = jnp.tanh(root * v * (1.0 + bend * square))
+                half = 0.5 * (1.0 + t)
+                active = (v * half).astype(jnp.bfloat16)
+                slope = half + (0.5 * root) * v * (1.0 - t * t) * (1.0 + 3.0 * bend * square)
+                active_ref[at, :] = active
+                hidden_grad = (dot_nt(grad_ref[at, :], down_ref[...]) * slope).astype(jnp.bfloat16)
+                hidden_grad_ref[at, :] = hidden_grad
+                sums_ref[...] += jnp.sum(hidden_grad.astype(jnp.float32), 0, keepdims=True)
+                part = dot_nn(active, down_ref[...]).astype(jnp.bfloat16)
+                (keep_ref, give_ref)[c][s] = part.reshape(2, tile // 2, features)
+                back = dot_nt(hidden_grad, up_ref[...]).astype(jnp.bfloat16)
+                (back_keep_ref, back_give_ref)[c][s] = back.reshape(2, tile // 2, features)
+
+    half = sds((2, 2, rows // 8, features), jnp.bfloat16)
+    wide = sds((rows, units), jnp.bfloat16)
+    return kernel_call(
+        kernel,
+        [LOCAL, LOCAL] + [ANYWHERE] * 8 + [LOCAL],
+        [wide, wide, sds((1, units), jnp.float32), half, half, half, half],
+        [
+            pltpu.VMEM((features, units), jnp.bfloat16),
+            pltpu.VMEM((units, features), jnp.bfloat16),
+            pltpu.SemaphoreType.DMA((2, DEPTH)),
+        ],
+        8 * rows * features * units,
+        (normed, grad, *ups, *downs, bias_up),
+    )
+
+
+def body_planes(
+    tokens,
+    cotangent,
+    lengths,
+    assign,
+    first_gain,
+    first_shift,
+    qkv_weight,
+    qv_bias,
+    out_weight,
+    out_bias,
+    second_gain,
+    second_shift,
+    up_weight,
+    up_bias,
+    down_weight,
+    down_bias,
+):
+    row_count, feature_count = tokens.shape
+    rep = lax.axis_index("rep")
+    z = lax.axis_index("shard")
+    quarter = rep & 3
+    own = feature_count // PLANE
+
+    own_length = jnp.sum(jnp.where(jnp.arange(lengths.shape[0]) == assign[0], lengths, 0))
+    ones = jnp.ones((16, feature_count), jnp.float32)
+    length_rows = jnp.where(
+        jnp.arange(16)[:, None] == 0, ones * (own_length // 16), ones * (own_length % 16)
+    )
+    moved = to_home(jnp.concatenate([tokens, cotangent, length_rows.astype(jnp.bfloat16)], 0))
+    tokens, cotangent = moved[:row_count], moved[row_count : 2 * row_count]
+    length_parts = moved[2 * row_count : 2 * row_count + 2, 0].astype(jnp.int32)
+    seq_length = 16 * length_parts[0] + length_parts[1]
+    other_length = over_rep(seq_length.astype(jnp.float32).reshape(1, 1), 4)
+    lens = jnp.stack([seq_length, other_length.astype(jnp.int32)[0, 0]])
+    heads = (2 * rep + jnp.arange(2)).astype(jnp.float32)
+    slopes = jnp.exp2(-8.0 * (heads + 1.0) / HEADS)
+
+    small = (
+        first_gain,
+        first_shift,
+        qv_bias,
+        out_bias,
+        second_gain,
+        second_shift,
+        up_bias,
+        down_bias,
+    )
+    packed = jnp.concatenate([item.reshape(-1, 256) for item in small], 0)
+    around = [packed] + [over_z(packed, step) for step in (1, 2, 3)]
+    parts = []
+    for plane in range(DEPTH):
+        back = lax.rem(z + (DEPTH - plane), DEPTH)
+        parts.append(
+            sum(
+                jnp.where(back == step, around[step].astype(jnp.float32), 0.0)
+                for step in range(DEPTH)
+            )
+        )
+    stacked = jnp.stack(parts, 0)
+    whole_small = []
+    start = 0
+    for item in small:
+        size = item.shape[0] // 256
+        whole_small.append(stacked[:, start : start + size].reshape(-1))
+        start += size
+    (
+        gain_first,
+        shift_first,
+        bias_qv,
+        bias_out,
+        gain_second,
+        shift_second,
+        bias_up,
+        bias_down,
+    ) = whole_small
+
+    def columns(weight):
+        blocks = weight.reshape(weight.shape[0], -1, PLANE, 128)
+        return lax.dynamic_index_in_dim(blocks, rep, 2, keepdims=False).reshape(weight.shape[0], -1)
+
+    def rows_of(weight, index, count):
+        return lax.dynamic_slice_in_dim(weight, index * count, count, 0)
+
+    qkv_own = columns(qkv_weight)
+    up_own = columns(up_weight)
+    down_own = rows_of(down_weight, rep, down_weight.shape[0] // PLANE)
+    out_own = rows_of(out_weight, rep & 1, own)
+    qkv_own, up_own, down_own, out_own = lax.optimization_barrier(
+        (qkv_own, up_own, down_own, out_own)
+    )
+
+    def to_planes(block):
+        return [block] + [over_z(block, step) for step in (1, 2, 3)]
+
+    qkv_parts = to_planes(qkv_own)
+    out_part = jnp.where(z == rep >> 1, out_own, jnp.zeros_like(out_own))
+    for step in (1, 2, 3):
+        out_part = out_part + over_all(
+            out_own,
+            lambda i, step=step: (
+                i - i % DEPTH + (i % DEPTH + step) % DEPTH if i % DEPTH == i // 8 else None
+            ),
+        )
+    up_parts = to_planes(up_own)
+    down_parts = to_planes(down_own)
+
+    rows_in = tokens.astype(jnp.float32)
+    row_valid = (quarter * row_count + jnp.arange(row_count) < seq_length)[:, None]
+    seed_grad = jnp.where(row_valid, cotangent.astype(jnp.float32), 0.0)
+    branch_grad = seed_grad.astype(jnp.bfloat16)
+
+    normed_low = layer_norm(rows_in, gain_first, shift_first).astype(jnp.bfloat16)
+    normed_plane = gather_plane(normed_low)
+    bias_blocks = bias_qv.reshape(2, PLANE, own)
+    bias_own = lax.dynamic_index_in_dim(bias_blocks, rep, 1, keepdims=False)
+    joint, mixed_plane, keep, give = attention_forward(
+        lens, slopes, normed_plane, qkv_parts, out_part, bias_own[:1], bias_own[1:]
+    )
+    branch_grad_plane = gather_plane(branch_grad)
+    middle = rows_in + scatter_plane(keep, give) + bias_out
+    normed_two_low = layer_norm(middle, gain_second, shift_second).astype(jnp.bfloat16)
+    normed_two_plane = gather_plane(normed_two_low)
+    bias_up_own = lax.dynamic_index_in_dim(bias_up.reshape(-1, PLANE, 128), rep, 1, keepdims=False)
+    active, hidden_grad, hidden_sums, keep, give, back_keep, back_give = feed_forward(
+        normed_two_plane, branch_grad_plane, up_parts, down_parts, bias_up_own.reshape(1, -1)
+    )
+    normed_two_grad = scatter_plane(back_keep, back_give)
+    unused_two, second_pull = jax.vjp(layer_norm, middle, gain_second, shift_second)
+    middle_from_norm, gain_second_grad, shift_second_grad = second_pull(normed_two_grad)
+    middle_grad = seed_grad + middle_from_norm
+    attended_grad = middle_grad.astype(jnp.bfloat16)
+    attended_grad_plane = gather_plane(attended_grad)
+    joint_grad, joint_sums, back_keep, back_give = attention_backward(
+        lens, slopes, attended_grad_plane, joint, qkv_parts, out_part
+    )
+    normed_grad = scatter_plane(back_keep, back_give)
+    qkv_grad = column_parts_to_rows(outer(normed_plane, joint_grad))
+
+    branch = scatter_plane(keep, give) + bias_down
+    layer_out = from_home((middle + branch).astype(jnp.bfloat16)).astype(jnp.float32)
+    down_slice = outer(active, branch_grad_plane).reshape(DEPTH, -1, feature_count)
+    down_summed = summed_over_z(down_slice).astype(jnp.bfloat16)
+    down_grad = over_all(
+        down_summed, lambda i: (2 * (i % DEPTH) + i // 16) * DEPTH + (i // DEPTH) % DEPTH
+    ).astype(jnp.float32)
+    up_grad = column_parts_to_rows(outer(normed_two_plane, hidden_grad))
+    out_slice = outer(mixed_plane, attended_grad_plane)
+    out_grad = summed_over_z(out_slice.reshape(DEPTH, -1, feature_count))
+
+    unused_three, first_pull = jax.vjp(layer_norm, rows_in, gain_first, shift_first)
+    rows_from_norm, gain_first_grad, shift_first_grad = first_pull(normed_grad)
+    tokens_grad = from_home((middle_grad + rows_from_norm).astype(jnp.bfloat16)).astype(jnp.float32)
+
+    at_rep = (jnp.arange(PLANE) == rep)[None, :, None]
+
+    def placed(sums):
+        return jnp.where(at_rep, sums.reshape(-1, 1, 128), 0.0).reshape(-1)
+
+    joint_parts = joint_sums.reshape(3, own)
+    small_grads = (
+        gain_first_grad,
+        shift_first_grad,
+        placed(jnp.concatenate([joint_parts[:1], joint_parts[2:]], 0)),
+        jnp.sum(attended_grad.astype(jnp.float32), 0),
+        gain_second_grad,
+        shift_second_grad,
+        placed(hidden_sums),
+        jnp.sum(branch_grad.astype(jnp.float32), 0),
+    )
+    devices = PLANE * DEPTH
+    small_packed = jnp.concatenate(
+        [g.reshape(devices, g.shape[0] // devices) for g in small_grads], 1
+    ).astype(jnp.bfloat16)
+    small_arrived = lax.all_to_all(small_packed, ("rep", "shard"), 0, 0, tiled=True)
+    small_sums = jnp.sum(small_arrived.astype(jnp.float32), 0)
+    sums = []
+    start = 0
+    for g in small_grads:
+        size = g.shape[0] // devices
+        sums.append(small_sums[start : start + size])
+        start += size
+    return (
+        layer_out,
+        tokens_grad,
+        sums[0],
+        sums[1],
+        qkv_grad,
+        sums[2],
+        out_grad,
+        sums[3],
+        sums[4],
+        sums[5],
+        up_grad,
+        sums[6],
+        down_grad,
+        sums[7],
+    )
+
+
 def solution(mesh):
     return jax.shard_map(
-        body,
+        body_planes if is_planes(mesh) else body_generic,
         mesh=mesh,
         in_specs=(
             P(("rep", "shard"), None),

time: 1100 us -> 434 us (0.39)
  the two profiles are of different devices: /device:TPU:0 before, /device:TPU:4 now
where the time goes in v2:
time: 434 us; the launch traced here: 433 us
  starting transfers between devices  186 us (43%)
  waiting for transfers between devices  100 us (23%)
  other arithmetic  46.4 us (11%)
  local copies, waits for them, and re-layouts  45.7 us (11%)
  Pallas kernels  36.9 us (9%)
  matrix products  10.5 us (2%)
  between operations  7.01 us (2%)
    ppermute x24, starting transfers between devices, over_z(): lax.ppermute(value, 'shard', [(i, (i + step) % DEPTH) for i in range(DEPT...  82.7 us
    ppermute x33, starting transfers between devices, over_rep(): return lax.ppermute(value, 'rep', [(i, i ^ flip) for i in range(PLANE)])  74.9 us
    ppermute x33, waiting for transfers between devices, over_rep(): return lax.ppermute(value, 'rep', [(i, i ^ flip) for i in range(PLANE)])  46.3 us
    pallas_call x3, Pallas kernels, kernel_call(): pl.pallas_call(kernel, out_shape=outs, in_specs=ins, out_specs=[LOCAL] *...  36.9 us
    ppermute x24, waiting for transfers between devices, over_z(): lax.ppermute(value, 'shard', [(i, (i + step) % DEPTH) for i in range(DEPT...  27.1 us
    ppermute x7, waiting for transfers between devices, over_all(): return lax.ppermute(value, ('rep', 'shard'), pairs)  19.7 us
    unnamed x149, local copies, waits for them, and re-layouts  13.7 us
    ppermute x7, starting transfers between devices, over_all(): return lax.ppermute(value, ('rep', 'shard'), pairs)  11.5 us
  transfers between devices with their start and end apart: 67, of which 26 were waited for; matrix products, arithmetic and copies ran while one was open for 18% of the time, Pallas kernels for 0%

profile of v2, /device:TPU:4, one launch (start us, length us, event | category | flops | bytes accessed | tf_op | source)
XLA Modules:
  0.0 432.7 jit_solution(17219006691439839362)
XLA Ops:
  23.4 8.8 %collective-permute-done = bf16[272,1024]{1,0:T(8,128)(2,1)S(1)} collective-permute-done((bf16[272,1024]{1,0:T(8,128)(2,1)S(1)}, bf16[272,1024]{1,0:T(8,128)(2,1)S(1)}, u32[]{:S(2)}, u32[]{:S(2)}) %collective-permute-start) | collective-permute-done | bytes 557088 | tf_op jit(solution)/shard_map/ppermute | solution.py:295
  32.8 17.5 %collective-permute-start.5 = (bf16[128,1024]{1,0:T(8,128)(2,1)S(1)}, bf16[128,1024]{1,0:T(8,128)(2,1)S(1)}, u32[]{:S(2)}, u32[]{:S(2)}) collective-permute-start(bf16[128,1024]{1,0:T(8,128)(2,1)S(1)} %fusion.11), channel_id=1, source_target_pairs={{0,8},{4,12},{8,0},{12,4},{16,24},{20,28},{24,16},{28,20},{1,9},{5... | collective-permute-start | bytes 786440 | tf_op jit(solution)/shard_map/ppermute | solution.py:286
  55.2 6.2 %collective-permute-done.6 = bf16[128,1024]{1,0:T(8,128)(2,1)S(1)} collective-permute-done((bf16[128,1024]{1,0:T(8,128)(2,1)S(1)}, bf16[128,1024]{1,0:T(8,128)(2,1)S(1)}, u32[]{:S(2)}, u32[]{:S(2)}) %collective-permute-start.6) | collective-permute-done | bytes 262176 | tf_op jit(solution)/shard_map/ppermute | solution.py:286
  61.5 5.5 %collective-permute-start.8 = (bf16[2,1,2,128,1024]{4,3,2,0,1:T(8,128)(2,1)S(1)}, bf16[2,1,2,128,1024]{4,3,2,0,1:T(8,128)(2,1)}, u32[]{:S(2)}, u32[]{:S(2)}) collective-permute-start(bf16[2,1,2,128,1024]{4,3,2,0,1:T(8,128)(2,1)S(1)} %bitcast.253), channel_id=1, source_target_pairs={{0,4},{4,0},{8,12},{12,8},{16,20},{20,16},{24,28},{28,24},{1,5},{5... | collective-permute-start | bytes 3145736 | tf_op jit(solution)/shard_map/ppermute | solution.py:286
  72.3 7.5 %collective-permute-start.10 = (bf16[256,384]{1,0:T(8,128)(2,1)S(1)}, bf16[256,384]{1,0:T(8,128)(2,1)S(1)}, u32[]{:S(2)}, u32[]{:S(2)}) collective-permute-start(bf16[256,384]{1,0:T(8,128)(2,1)S(1)} %copy.108.w0), channel_id=1, source_target_pairs={{0,2},{1,3},{2,0},{3,1},{4,6},{5,7},{6,4},{7,5},{8,10},{9,11},{10,... | collective-permute-start | bytes 589832 | tf_op jit(solution)/shard_map/ppermute | solution.py:290
  80.0 7.4 %collective-permute-start.11 = (bf16[256,384]{1,0:T(8,128)(2,1)S(1)}, bf16[256,384]{1,0:T(8,128)(2,1)S(1)}, u32[]{:S(2)}, u32[]{:S(2)}) collective-permute-start(bf16[256,384]{1,0:T(8,128)(2,1)S(1)} %copy.108.w0), channel_id=1, source_target_pairs={{0,3},{1,0},{2,1},{3,2},{4,7},{5,4},{6,5},{7,6},{8,11},{9,8},{10,9... | collective-permute-start | bytes 589832 | tf_op jit(solution)/shard_map/ppermute | solution.py:290
  91.1 7.2 %collective-permute-start.1 = (f32[1,1]{1,0:T(1,128)}, f32[1,1]{1,0:T(1,128)}, u32[]{:S(2)}, u32[]{:S(2)}) collective-permute-start(f32[1,1]{1,0:T(1,128)} %bitcast.3), channel_id=1, source_target_pairs={{0,16},{4,20},{8,24},{12,28},{16,0},{20,4},{24,8},{28,12},{1,17},{... | collective-permute-start | bytes 20 | tf_op jit(solution)/shard_map/ppermute | solution.py:286
  102.2 12.8 %shard_map.263 = (bf16[1024,384]{1,0:T(8,128)(2,1)S(1)}, bf16[1024,128]{1,0:T(8,128)(2,1)S(1)}, bf16[2,2,128,1024]{3,2,1,0:T(8,128)(2,1)S(1)}, bf16[2,2,128,1024]{3,2,1,0:T(8,128)(2,1)}) custom-call(s32[2]{0:T(128)S(1)} %pad_add_fusion.lens_ref, f32[2]{0:T(128)S(1)} %multiply_exponential_fusion.slopes_ref, bf16[1024,1024]{1,0:T(8,128)(2,1)} %bitcast.247, ...), custom_call_target="tpu_custom_call" | custom-call | flops 1610612736 | bytes 8388608 | tf_op jit(solution)/shard_map/pallas_call | solution.py:413
  120.7 4.9 %collective-permute-start.16 = (bf16[128,1024]{1,0:T(8,128)(2,1)S(1)}, bf16[128,1024]{1,0:T(8,128)(2,1)S(1)}, u32[]{:S(2)}, u32[]{:S(2)}) collective-permute-start(bf16[128,1024]{1,0:T(8,128)(2,1)S(1)} %get-tuple-element.92), channel_id=1, source_target_pairs={{0,8},{4,12},{8,0},{12,4},{16,24},{20,28},{24,16},{28,20},{1,9},{5... | collective-permute-start | bytes 786440 | tf_op jit(solution)/shard_map/ppermute | solution.py:286
  155.3 6.8 %collective-permute-done.20 = bf16[128,1024]{1,0:T(8,128)(2,1)S(1)} collective-permute-done((bf16[128,1024]{1,0:T(8,128)(2,1)S(1)}, bf16[128,1024]{1,0:T(8,128)(2,1)S(1)}, u32[]{:S(2)}, u32[]{:S(2)}) %collective-permute-start.20) | collective-permute-done | bytes 262176 | tf_op jit(solution)/shard_map/ppermute | solution.py:286
  169.7 4.6 %collective-permute-done.27.u1 = bf16[256,512]{1,0:T(8,128)(2,1)S(1)} collective-permute-done((bf16[256,512]{1,0:T(8,128)(2,1)S(1)}, bf16[256,512]{1,0:T(8,128)(2,1)S(1)}, u32[]{:S(2)}, u32[]{:S(2)}) %collective-permute-start.27) | collective-permute-done | bytes 262176 | tf_op jit(solution)/shard_map/ppermute | solution.py:290
  174.3 10.9 %collective-permute-start.30 = (bf16[128,1024]{1,0:T(8,128)(2,1)S(1)}, bf16[128,1024]{1,0:T(8,128)(2,1)S(1)}, u32[]{:S(2)}, u32[]{:S(2)}) collective-permute-start(bf16[128,1024]{1,0:T(8,128)(2,1)S(1)} %get-tuple-element.38.d0), channel_id=1, source_target_pairs={{0,1},{1,2},{2,3},{3,0},{4,5},{5,6},{6,7},{7,4},{8,9},{9,10},{10,1... | collective-permute-start | bytes 786440 | tf_op jit(solution)/shard_map/ppermute | solution.py:290
  197.6 10.0 %collective-permute-done.31.d2 = bf16[128,1024]{1,0:T(8,128)(2,1)S(1)} collective-permute-done((bf16[128,1024]{1,0:T(8,128)(2,1)S(1)}, bf16[128,1024]{1,0:T(8,128)(2,1)S(1)}, u32[]{:S(2)}, u32[]{:S(2)}) %collective-permute-start.31) | collective-permute-done | bytes 262176 | tf_op jit(solution)/shard_map/ppermute | solution.py:290
  209.5 9.0 %shard_map.264 = (bf16[1024,512]{1,0:T(8,128)(2,1)S(1)}, bf16[1024,512]{1,0:T(8,128)(2,1)S(1)}, f32[1,512]{1,0:T(1,128)S(1)}, bf16[2,2,128,1024]{3,2,1,0:T(8,128...) custom-call(bf16[1024,1024]{1,0:T(8,128)(2,1)} %bitcast.249, ...), custom_call_target="tpu_custom_call" | custom-call | flops 4294967296 | bytes 8388608 | tf_op jit(solution)/shard_map/pallas_call | solution.py:413
  235.4 5.5 %collective-permute-done.40 = bf16[128,1024]{1,0:T(8,128)(2,1)S(1)} collective-permute-done((bf16[128,1024]{1,0:T(8,128)(2,1)S(1)}, bf16[128,1024]{1,0:T(8,128)(2,1)S(1)}, u32[]{:S(2)}, u32[]{:S(2)}) %collective-permute-start.40) | collective-permute-done | bytes 262176 | tf_op jit(solution)/shard_map/ppermute | solution.py:286
  261.1 6.1 %collective-permute-start.60 = (bf16[128,1024]{1,0:T(8,128)(2,1)}, bf16[128,1024]{1,0:T(8,128)(2,1)}, u32[]{:S(2)}, u32[]{:S(2)}) collective-permute-start(bf16[128,1024]{1,0:T(8,128)(2,1)} %get-tuple-element.77), channel_id=1, source_target_pairs={{0,1},{1,2},{2,3},{3,0},{4,5},{5,6},{6,7},{7,4},{8,9},{9,10},{10,1... | collective-permute-start | bytes 786440 | tf_op jit(solution)/shard_map/ppermute | solution.py:290
  281.7 5.7 %collective-permute-start.58 = (bf16[8,32,512]{2,1,0:T(8,128)(2,1)}, bf16[8,32,512]{2,1,0:T(8,128)(2,1)}, u32[]{:S(2)}, u32[]{:S(2)}) collective-permute-start(bf16[8,32,512]{2,1,0:T(8,128)(2,1)} %get-tuple-element.82), channel_id=1, source_target_pairs={{0,2},{1,3},{2,0},{3,1},{4,6},{5,7},{6,4},{7,5},{8,10},{9,11},{10,... | collective-permute-start | bytes 786440 | tf_op jit(solution)/shard_map/ppermute | solution.py:290
  287.4 14.9 %collective-permute-start.59 = (bf16[8,32,512]{2,1,0:T(8,128)(2,1)S(1)}, bf16[8,32,512]{2,1,0:T(8,128)(2,1)}, u32[]{:S(2)}, u32[]{:S(2)}) collective-permute-start(bf16[8,32,512]{2,1,0:T(8,128)(2,1)S(1)} %get-tuple-element.81), channel_id=1, source_target_pairs={{0,3},{1,0},{2,1},{3,2},{4,7},{5,4},{6,5},{7,6},{8,11},{9,8},{10,9... | collective-permute-start | bytes 786440 | tf_op jit(solution)/shard_map/ppermute | solution.py:290
  335.6 15.1 %shard_map.265 = (bf16[1024,384]{1,0:T(8,128)(2,1)S(1)}, f32[1,384]{1,0:T(1,128)S(1)}, bf16[2,2,128,1024]{3,2,1,0:T(8,128)(2,1)S(1)}, bf16[2,2,128,1024]{3,2,1,0:T(8,128)(2,1)S(1)}) custom-call(s32[2]{0:T(128)S(1)} %pad_add_fusion.lens_ref, f32[2]{0:T(128)S(1)} %multiply_exponential_fusion.slopes_ref, bf16[1024,1024]{1,0:T(8,128)(2,1)} %bitcast.251, ...), custom_call_target="tpu_custom_call" | custom-call | flops 2415919104 | bytes 8388608 | tf_op jit(solution)/shard_map/pallas_call | solution.py:413
  350.7 7.8 %collective-permute-start.46 = (bf16[2,2,128,1024]{3,2,1,0:T(8,128)(2,1)S(1)}, bf16[2,2,128,1024]{3,2,1,0:T(8,128)(2,1)}, u32[]{:S(2)}, u32[]{:S(2)}) collective-permute-start(bf16[2,2,128,1024]{3,2,1,0:T(8,128)(2,1)S(1)} %get-tuple-element.45), channel_id=1, source_target_pairs={{0,4},{4,0},{8,12},{12,8},{16,20},{20,16},{24,28},{28,24},{1,5},{5... | collective-permute-start | bytes 3145736 | tf_op jit(solution)/shard_map/ppermute | solution.py:286
  379.5 5.7 %collective-permute-done.52 = bf16[8,32,384]{2,1,0:T(8,128)(2,1)} collective-permute-done((bf16[8,32,384]{2,1,0:T(8,128)(2,1)S(1)}, bf16[8,32,384]{2,1,0:T(8,128)(2,1)}, u32[]{:S(2)}, u32[]{:S(2)}) %collective-permute-start.52) | collective-permute-done | bytes 196640 | tf_op jit(solution)/shard_map/ppermute | solution.py:290
  389.9 5.3 %all-to-all-start.1 = ((bf16[8,32,384]{2,1,0:T(8,128)(2,1)}), bf16[8,32,384]{2,1,0:T(8,128)(2,1)S(1)}, u32[]{:S(2)}, u32[]{:S(2)}) async-start(bf16[8,32,384]{2,1,0:T(8,128)(2,1)} %fusion.40), calls=%async_computation.1 | async-start | bytes 393216 | tf_op jit(solution)/shard_map/all_to_all | solution.py:356
  405.2 8.4 %all-to-all-start = ((bf16[32,2,192]{2,1,0:T(2,128)(2,1)}), bf16[32,2,192]{2,1,0:T(2,128)(2,1)S(1)}, u32[]{:S(2)}, u32[]{:S(2)}) async-start(bf16[32,2,192]{2,1,0:T(2,128)(2,1)} %reshape.443), calls=%async_computation | async-start | bytes 65536 | tf_op jit(solution)/shard_map/all_to_all | solution.py:800
  421.7 10.2 %collective-permute-done.50 = bf16[128,1024]{1,0:T(8,128)(2,1)S(1)} collective-permute-done((bf16[128,1024]{1,0:T(8,128)(2,1)S(1)}, bf16[128,1024]{1,0:T(8,128)(2,1)S(1)}, u32[]{:S(2)}, u32[]{:S(2)}) %collective-permute-start.50) | collective-permute-done | bytes 262176 | tf_op jit(solution)/shard_map/ppermute | solution.py:295
  (381 shorter events, 221.7 us)
Async XLA Ops:
  32.8 22.4 %collective-permute-start.5 = (bf16[128,1024]{1,0:T(8,128)(2,1)S(1)}, bf16[128,1024]{1,0:T(8,128)(2,1)S(1)}, u32[]{:S(2)}, u32[]{:S(2)}) collective-permute-start(bf16[128,1024]{1,0:T(8,128)(2,1)S(1)} %fusion.11), channel_id=1, source_target_pairs={{0,8},{4,12},{8,0},{12,4},{16,24},{20,28},{24,16},{28,20},{1,9},{5... | collective-permute-start | bytes 786440 | tf_op jit(solution)/shard_map/ppermute | solution.py:286
  61.5 37.7 %collective-permute-start.8 = (bf16[2,1,2,128,1024]{4,3,2,0,1:T(8,128)(2,1)S(1)}, bf16[2,1,2,128,1024]{4,3,2,0,1:T(8,128)(2,1)}, u32[]{:S(2)}, u32[]{:S(2)}) collective-permute-start(bf16[2,1,2,128,1024]{4,3,2,0,1:T(8,128)(2,1)S(1)} %bitcast.253), channel_id=1, source_target_pairs={{0,4},{4,0},{8,12},{12,8},{16,20},{20,16},{24,28},{28,24},{1,5},{5... | collective-permute-start | bytes 3145736 | tf_op jit(solution)/shard_map/ppermute | solution.py:286
  72.3 29.8 %collective-permute-start.10 = (bf16[256,384]{1,0:T(8,128)(2,1)S(1)}, bf16[256,384]{1,0:T(8,128)(2,1)S(1)}, u32[]{:S(2)}, u32[]{:S(2)}) collective-permute-start(bf16[256,384]{1,0:T(8,128)(2,1)S(1)} %copy.108.w0), channel_id=1, source_target_pairs={{0,2},{1,3},{2,0},{3,1},{4,6},{5,7},{6,4},{7,5},{8,10},{9,11},{10,... | collective-permute-start | bytes 589832 | tf_op jit(solution)/shard_map/ppermute | solution.py:290
  80.0 22.2 %collective-permute-start.11 = (bf16[256,384]{1,0:T(8,128)(2,1)S(1)}, bf16[256,384]{1,0:T(8,128)(2,1)S(1)}, u32[]{:S(2)}, u32[]{:S(2)}) collective-permute-start(bf16[256,384]{1,0:T(8,128)(2,1)S(1)} %copy.108.w0), channel_id=1, source_target_pairs={{0,3},{1,0},{2,1},{3,2},{4,7},{5,4},{6,5},{7,6},{8,11},{9,8},{10,9... | collective-permute-start | bytes 589832 | tf_op jit(solution)/shard_map/ppermute | solution.py:290
  129.9 21.8 %collective-permute-start.24 = (bf16[128,1024]{1,0:T(8,128)(2,1)S(1)}, bf16[128,1024]{1,0:T(8,128)(2,1)S(1)}, u32[]{:S(2)}, u32[]{:S(2)}) collective-permute-start(bf16[128,1024]{1,0:T(8,128)(2,1)S(1)} %get-tuple-element.60), channel_id=1, source_target_pairs={{0,16},{4,20},{8,24},{12,28},{16,0},{20,4},{24,8},{28,12},{1,17},{... | collective-permute-start | bytes 786440 | tf_op jit(solution)/shard_map/ppermute | solution.py:286
  142.8 19.4 %collective-permute-start.20 = (bf16[128,1024]{1,0:T(8,128)(2,1)S(1)}, bf16[128,1024]{1,0:T(8,128)(2,1)S(1)}, u32[]{:S(2)}, u32[]{:S(2)}) collective-permute-start(bf16[128,1024]{1,0:T(8,128)(2,1)S(1)} %add_convert_fusion.1), channel_id=1, source_target_pairs={{0,16},{4,20},{8,24},{12,28},{16,0},{20,4},{24,8},{28,12},{1,17},{... | collective-permute-start | bytes 786440 | tf_op jit(solution)/shard_map/ppermute | solution.py:286
  151.9 33.2 %collective-permute-start.26 = (bf16[2,1,2,128,1024]{4,3,2,0,1:T(8,128)(2,1)S(1)}, bf16[2,1,2,128,1024]{4,3,2,0,1:T(8,128)(2,1)}, u32[]{:S(2)}, u32[]{:S(2)}) collective-permute-start(bf16[2,1,2,128,1024]{4,3,2,0,1:T(8,128)(2,1)S(1)} %bitcast.255), channel_id=1, source_target_pairs={{0,4},{4,0},{8,12},{12,8},{16,20},{20,16},{24,28},{28,24},{1,5},{5... | collective-permute-start | bytes 3145736 | tf_op jit(solution)/shard_map/ppermute | solution.py:286
  163.2 23.9 %collective-permute-start.22 = (bf16[2,1,2,128,1024]{4,3,2,0,1:T(8,128)(2,1)}, bf16[2,1,2,128,1024]{4,3,2,0,1:T(8,128)(2,1)}, u32[]{:S(2)}, u32[]{:S(2)}) collective-permute-start(bf16[2,1,2,128,1024]{4,3,2,0,1:T(8,128)(2,1)} %bitcast.32), channel_id=1, source_target_pairs={{0,4},{4,0},{8,12},{12,8},{16,20},{20,16},{24,28},{28,24},{1,5},{5... | collective-permute-start | bytes 3145736 | tf_op jit(solution)/shard_map/ppermute | solution.py:286
  165.0 31.2 %collective-permute-start.28 = (bf16[256,512]{1,0:T(8,128)(2,1)S(1)}, bf16[256,512]{1,0:T(8,128)(2,1)S(1)}, u32[]{:S(2)}, u32[]{:S(2)}) collective-permute-start(bf16[256,512]{1,0:T(8,128)(2,1)S(1)} %bitcast.243), channel_id=1, source_target_pairs={{0,2},{1,3},{2,0},{3,1},{4,6},{5,7},{6,4},{7,5},{8,10},{9,11},{10,... | collective-permute-start | bytes 786440 | tf_op jit(solution)/shard_map/ppermute | solution.py:290
  166.8 30.1 %collective-permute-start.29 = (bf16[256,512]{1,0:T(8,128)(2,1)S(1)}, bf16[256,512]{1,0:T(8,128)(2,1)S(1)}, u32[]{:S(2)}, u32[]{:S(2)}) collective-permute-start(bf16[256,512]{1,0:T(8,128)(2,1)S(1)} %bitcast.244), channel_id=1, source_target_pairs={{0,3},{1,0},{2,1},{3,2},{4,7},{5,4},{6,5},{7,6},{8,11},{9,8},{10,9... | collective-permute-start | bytes 786440 | tf_op jit(solution)/shard_map/ppermute | solution.py:290
  174.3 23.3 %collective-permute-start.30 = (bf16[128,1024]{1,0:T(8,128)(2,1)S(1)}, bf16[128,1024]{1,0:T(8,128)(2,1)S(1)}, u32[]{:S(2)}, u32[]{:S(2)}) collective-permute-start(bf16[128,1024]{1,0:T(8,128)(2,1)S(1)} %get-tuple-element.38.d0), channel_id=1, source_target_pairs={{0,1},{1,2},{2,3},{3,0},{4,5},{5,6},{6,7},{7,4},{8,9},{9,10},{10,1... | collective-permute-start | bytes 786440 | tf_op jit(solution)/shard_map/ppermute | solution.py:290
  185.1 22.4 %collective-permute-start.31 = (bf16[128,1024]{1,0:T(8,128)(2,1)S(1)}, bf16[128,1024]{1,0:T(8,128)(2,1)S(1)}, u32[]{:S(2)}, u32[]{:S(2)}) collective-permute-start(bf16[128,1024]{1,0:T(8,128)(2,1)S(1)} %get-tuple-element.38.d0), channel_id=1, source_target_pairs={{0,2},{1,3},{2,0},{3,1},{4,6},{5,7},{6,4},{7,5},{8,10},{9,11},{10,... | collective-permute-start | bytes 786440 | tf_op jit(solution)/shard_map/ppermute | solution.py:290
  187.1 20.4 %collective-permute-start.32 = (bf16[128,1024]{1,0:T(8,128)(2,1)S(1)}, bf16[128,1024]{1,0:T(8,128)(2,1)S(1)}, u32[]{:S(2)}, u32[]{:S(2)}) collective-permute-start(bf16[128,1024]{1,0:T(8,128)(2,1)S(1)} %get-tuple-element.38.d0), channel_id=1, source_target_pairs={{0,3},{1,0},{2,1},{3,2},{4,7},{5,4},{6,5},{7,6},{8,11},{9,8},{10,9... | collective-permute-start | bytes 786440 | tf_op jit(solution)/shard_map/ppermute | solution.py:290
  261.1 20.6 %collective-permute-start.60 = (bf16[128,1024]{1,0:T(8,128)(2,1)}, bf16[128,1024]{1,0:T(8,128)(2,1)}, u32[]{:S(2)}, u32[]{:S(2)}) collective-permute-start(bf16[128,1024]{1,0:T(8,128)(2,1)} %get-tuple-element.77), channel_id=1, source_target_pairs={{0,1},{1,2},{2,3},{3,0},{4,5},{5,6},{6,7},{7,4},{8,9},{9,10},{10,1... | collective-permute-start | bytes 786440 | tf_op jit(solution)/shard_map/ppermute | solution.py:290
  267.2 20.2 %collective-permute-start.61 = (bf16[128,1024]{1,0:T(8,128)(2,1)}, bf16[128,1024]{1,0:T(8,128)(2,1)}, u32[]{:S(2)}, u32[]{:S(2)}) collective-permute-start(bf16[128,1024]{1,0:T(8,128)(2,1)} %get-tuple-element.79), channel_id=1, source_target_pairs={{0,2},{1,3},{2,0},{3,1},{4,6},{5,7},{6,4},{7,5},{8,10},{9,11},{10,... | collective-permute-start | bytes 786440 | tf_op jit(solution)/shard_map/ppermute | solution.py:290
  272.4 30.0 %collective-permute-start.62 = (bf16[128,1024]{1,0:T(8,128)(2,1)S(1)}, bf16[128,1024]{1,0:T(8,128)(2,1)S(1)}, u32[]{:S(2)}, u32[]{:S(2)}) collective-permute-start(bf16[128,1024]{1,0:T(8,128)(2,1)S(1)} %get-tuple-element.78), channel_id=1, source_target_pairs={{0,3},{1,0},{2,1},{3,2},{4,7},{5,4},{6,5},{7,6},{8,11},{9,8},{10,9... | collective-permute-start | bytes 786440 | tf_op jit(solution)/shard_map/ppermute | solution.py:290
  274.7 57.7 %collective-permute-start.45 = (bf16[2,1,2,128,1024]{4,3,2,1,0:T(8,128)(2,1)}, bf16[2,1,2,128,1024]{4,3,2,1,0:T(8,128)(2,1)}, u32[]{:S(2)}, u32[]{:S(2)}) collective-permute-start(bf16[2,1,2,128,1024]{4,3,2,1,0:T(8,128)(2,1)} %bitcast.55), channel_id=1, source_target_pairs={{0,4},{4,0},{8,12},{12,8},{16,20},{20,16},{24,28},{28,24},{1,5},{5... | collective-permute-start | bytes 3145736 | tf_op jit(solution)/shard_map/ppermute | solution.py:286
  279.8 27.5 %collective-permute-start.57 = (bf16[8,32,512]{2,1,0:T(8,128)(2,1)}, bf16[8,32,512]{2,1,0:T(8,128)(2,1)}, u32[]{:S(2)}, u32[]{:S(2)}) collective-permute-start(bf16[8,32,512]{2,1,0:T(8,128)(2,1)} %get-tuple-element.80), channel_id=1, source_target_pairs={{0,1},{1,2},{2,3},{3,0},{4,5},{5,6},{6,7},{7,4},{8,9},{9,10},{10,1... | collective-permute-start | bytes 786440 | tf_op jit(solution)/shard_map/ppermute | solution.py:290
  281.7 26.6 %collective-permute-start.58 = (bf16[8,32,512]{2,1,0:T(8,128)(2,1)}, bf16[8,32,512]{2,1,0:T(8,128)(2,1)}, u32[]{:S(2)}, u32[]{:S(2)}) collective-permute-start(bf16[8,32,512]{2,1,0:T(8,128)(2,1)} %get-tuple-element.82), channel_id=1, source_target_pairs={{0,2},{1,3},{2,0},{3,1},{4,6},{5,7},{6,4},{7,5},{8,10},{9,11},{10,... | collective-permute-start | bytes 786440 | tf_op jit(solution)/shard_map/ppermute | solution.py:290
  287.4 24.5 %collective-permute-start.59 = (bf16[8,32,512]{2,1,0:T(8,128)(2,1)S(1)}, bf16[8,32,512]{2,1,0:T(8,128)(2,1)}, u32[]{:S(2)}, u32[]{:S(2)}) collective-permute-start(bf16[8,32,512]{2,1,0:T(8,128)(2,1)S(1)} %get-tuple-element.81), channel_id=1, source_target_pairs={{0,3},{1,0},{2,1},{3,2},{4,7},{5,4},{6,5},{7,6},{8,11},{9,8},{10,9... | collective-permute-start | bytes 786440 | tf_op jit(solution)/shard_map/ppermute | solution.py:290
  305.4 21.4 %collective-permute-start.63 = (bf16[128,1024]{1,0:T(8,128)(2,1)}, bf16[128,1024]{1,0:T(8,128)(2,1)}, u32[]{:S(2)}, u32[]{:S(2)}) collective-permute-start(bf16[128,1024]{1,0:T(8,128)(2,1)} %fusion.33), channel_id=1, source_target_pairs={{0,0},{1,8},{2,16},{3,24},{4,1},{5,9},{6,17},{7,25},{8,2},{9,10},{... | collective-permute-start | bytes 786440 | tf_op jit(solution)/shard_map/ppermute | solution.py:295
  362.1 33.1 %collective-permute-start.55 = (bf16[32,1024]{1,0:T(8,128)(2,1)}, bf16[32,1024]{1,0:T(8,128)(2,1)}, u32[]{:S(2)}, u32[]{:S(2)}) collective-permute-start(bf16[32,1024]{1,0:T(8,128)(2,1)} %get-tuple-element.101), channel_id=1, source_target_pairs={{0,2},{1,3},{2,0},{3,1},{4,6},{5,7},{6,4},{7,5},{8,10},{9,11},{10,... | collective-permute-start | bytes 196616 | tf_op jit(solution)/shard_map/ppermute | solution.py:290
  374.9 20.3 %collective-permute-start.56 = (bf16[32,1024]{1,0:T(8,128)(2,1)S(1)}, bf16[32,1024]{1,0:T(8,128)(2,1)S(1)}, u32[]{:S(2)}, u32[]{:S(2)}) collective-permute-start(bf16[32,1024]{1,0:T(8,128)(2,1)S(1)} %get-tuple-element.100), channel_id=1, source_target_pairs={{0,3},{1,0},{2,1},{3,2},{4,7},{5,4},{6,5},{7,6},{8,11},{9,8},{10,9... | collective-permute-start | bytes 196616 | tf_op jit(solution)/shard_map/ppermute | solution.py:290
  377.8 23.5 %collective-permute-start.47 = (bf16[128,1024]{1,0:T(8,128)(2,1)S(1)}, bf16[128,1024]{1,0:T(8,128)(2,1)S(1)}, u32[]{:S(2)}, u32[]{:S(2)}) collective-permute-start(bf16[128,1024]{1,0:T(8,128)(2,1)S(1)} %get-tuple-element.83), channel_id=1, source_target_pairs={{0,8},{4,12},{8,0},{12,4},{16,24},{20,28},{24,16},{28,20},{1,9},{5... | collective-permute-start | bytes 786440 | tf_op jit(solution)/shard_map/ppermute | solution.py:286
  (114 other events, 1651.6 us)

commit v3 on v2

--- a/solution.py
+++ b/solution.py
@@ -275,7 +275,8 @@
 PLANE = 8
 DEPTH = 4
 QUARTERS = 4
-VMEM_BYTES = 48 * 2**20
+VMEM_BYTES = 60 * 2**20
+ORDER = (0, 2, 1, 3, 4, 6, 5, 7)
 
 
 def is_planes(mesh):
@@ -297,7 +298,8 @@
 
 def home_of(index):
     rep, z = index // DEPTH, index % DEPTH
-    return ((rep & 1) * 4 + z) * DEPTH + rep // 2
+    y, x, core = rep >> 2, (rep >> 1) & 1, rep & 1
+    return (4 * x + 2 * (z & 1) + (z >> 1)) * DEPTH + 2 * core + y
 
 
 HOME = [home_of(i) for i in range(PLANE * DEPTH)]
@@ -316,31 +318,53 @@
 
 
 def gather_plane(rows):
-    beside = [over_rep(rows, flip) for flip in (2, 4, 6)]
-    quad = jnp.stack([rows, *beside], 0).reshape(2, 1, 2, *rows.shape)
-    return jnp.concatenate([quad, over_rep(quad, 1)], 1).reshape(-1, rows.shape[1])
-
-
-def scatter_plane(keep, give):
-    both = keep.astype(jnp.float32) + over_rep(give, 1).astype(jnp.float32)
-    total = both[0, 0]
-    for flip, part in ((2, both[0, 1]), (4, both[1, 0]), (6, both[1, 1])):
-        total = total + over_rep(part.astype(jnp.bfloat16), flip).astype(jnp.float32)
-    return total
-
-
-def block_at(blocks, index):
-    return lax.dynamic_index_in_dim(blocks, index, 0, keepdims=False)
-
-
-def summed_over_z(blocks):
-    z = lax.axis_index("shard")
-    low = blocks.astype(jnp.bfloat16)
-    total = block_at(blocks, z)
-    for step in (1, 2, 3):
-        sent = block_at(low, lax.rem(z + step, DEPTH))
-        total = total + over_z(sent, step).astype(jnp.float32)
-    return total
+    near = over_rep(rows, 1)
+    two, four, six = (over_rep(rows, flip) for flip in (2, 4, 6))
+    return [rows, near, two, over_rep(two, 1), four, over_rep(four, 1), six, over_rep(six, 1)]
+
+
+def add_halves(keep, received):
+    count, features = keep.shape[2:]
+
+    def kernel(keep_ref, received_ref, own_ref, two_ref, four_ref, six_ref, left, right, sems):
+        outs = {0: own_ref, 2: two_ref, 4: four_ref, 6: six_ref}
+        copies = {}
+        for flip in (6, 2, 4, 0):
+            y, x = flip >> 2, (flip >> 1) & 1
+            copies[flip] = [
+                pltpu.make_async_copy(ref.at[y, x], to.at[y, x], sems.at[i, flip // 2])
+                for i, (ref, to) in enumerate(((keep_ref, left), (received_ref, right)))
+            ]
+            for copy in copies[flip]:
+                copy.start()
+        for flip in (6, 2, 4, 0):
+            y, x = flip >> 2, (flip >> 1) & 1
+            wait_all(copies[flip])
+            total = left[y, x].astype(jnp.float32) + right[y, x].astype(jnp.float32)
+            outs[flip][...] = total.astype(outs[flip].dtype)
+
+    low = sds((count, features), jnp.bfloat16)
+    return kernel_call(
+        kernel,
+        [ANYWHERE] * 2,
+        [sds((count, features), jnp.float32), low, low, low],
+        [
+            pltpu.VMEM(keep.shape, keep.dtype),
+            pltpu.VMEM(keep.shape, keep.dtype),
+            pltpu.SemaphoreType.DMA((2, 4)),
+        ],
+        0,
+        (keep, received),
+    )
+
+
+def send_parts(parts):
+    own, *others = parts
+    return [own] + [over_rep(part, flip) for part, flip in zip(others, (2, 4, 6))]
+
+
+def scattered_over_z(blocks):
+    return lax.psum_scatter(blocks, "shard", scatter_dimension=0, tiled=False)
 
 
 def outer(left, right):
@@ -349,14 +373,10 @@
     )
 
 
-def column_parts_to_rows(grad):
-    rows, width = grad.shape
-    parts = grad.reshape(PLANE, DEPTH, rows // (PLANE * DEPTH), width)
-    summed = summed_over_z(jnp.swapaxes(parts, 0, 1)).astype(jnp.bfloat16)
-    arrived = lax.all_to_all(summed, "rep", 0, 0, tiled=True)
-    block = rows // (PLANE * DEPTH)
-    spread = arrived.reshape(PLANE, block, -1, 128)
-    return jnp.transpose(spread, (1, 2, 0, 3)).reshape(block, -1).astype(jnp.float32)
+def columns_to_rows(parts):
+    arrived = lax.all_to_all(parts, "rep", 0, 0, tiled=True)
+    spread = arrived.reshape(PLANE, parts.shape[1], -1, 128)
+    return jnp.transpose(spread, (1, 2, 0, 3)).reshape(parts.shape[1], -1).astype(jnp.float32)
 
 
 def dot_nn(left, right):
@@ -387,12 +407,49 @@
         copy.wait()
 
 
+def quarter_of(rep):
+    return 2 * (rep & 1) + ((rep >> 1) & 1)
+
+
 def row_positions(shape, axis, rep, first):
     index = lax.broadcasted_iota(jnp.int32, shape, axis) + first
-    block = index >> 7
-    x = (block & 1) ^ ((rep >> 1) & 1)
-    core = (block >> 1) ^ (rep & 1)
-    return ((x * 2 + core) << 7) + (index & 127)
+    return (((index >> 7) ^ quarter_of(rep)) << 7) + (index & 127)
+
+
+def load_blocks(blocks, whole, sems):
+    count = blocks[0].shape[0]
+    copies = []
+    for place, k in enumerate(ORDER):
+        at = pl.ds(place * count, count)
+        copies.append(pltpu.make_async_copy(blocks[k], whole.at[at], sems.at[place]))
+        copies[-1].start()
+    return copies
+
+
+def load(ref, to, sem):
+    copy = pltpu.make_async_copy(ref, to, sem)
+    copy.start()
+    return copy
+
+
+def total_of(parts):
+    own, two, four, six = parts
+    return (own[...] + two[...].astype(jnp.float32)) + (
+        four[...].astype(jnp.float32) + six[...].astype(jnp.float32)
+    )
+
+
+def unit_rows(v):
+    centered = v - jnp.mean(v, 1, keepdims=True)
+    rstd = lax.rsqrt(jnp.mean(centered * centered, 1, keepdims=True) + 1e-05)
+    return centered * rstd, rstd
+
+
+def norm_back(grad, xhat, rstd, gain):
+    gx = grad * gain
+    return rstd * (
+        gx - jnp.mean(gx, 1, keepdims=True) - xhat * jnp.mean(gx * xhat, 1, keepdims=True)
+    )
 
 
 def scores_of(query, keys, slope, distance, allowed, scale):
@@ -400,6 +457,7 @@
     return jnp.where(allowed, raw, -1e30)
 
 
+VECTORS = ((0, 256), (1, 256), (6, 512), (2, 256), (3, 256), (4, 256), (8, 1024), (5, 256))
 ANYWHERE = pl.BlockSpec(memory_space=pl.ANY)
 LOCAL = pl.BlockSpec(memory_space=pltpu.VMEM)
 SCALARS = pl.BlockSpec(memory_space=pltpu.SMEM)
@@ -421,8 +479,153 @@
     )(*operands)
 
 
-def attention_forward(lens, slopes, normed, weights, out_part, bias_q, bias_v):
-    rows, features = normed.shape
+def own_eighths(qkv_weight, out_weight, up_weight, down_weight):
+    def kernel(qkv_ref, out_ref, up_ref, down_ref, qkv_own, out_own, up_own, down_own, sems):
+        rep = lax.axis_index("rep")
+        moves = []
+        for ref, own_ref in ((qkv_ref, qkv_own), (up_ref, up_own)):
+            for j in range(own_ref.shape[1] // 128):
+                at = pl.ds(pl.multiple_of(1024 * j + 128 * rep, 128), 128)
+                moves.append((ref.at[:, at], own_ref.at[:, pl.ds(128 * j, 128)]))
+        for ref, own_ref, index in ((out_ref, out_own, rep & 1), (down_ref, down_own, rep)):
+            count = own_ref.shape[0]
+            at = pl.ds(pl.multiple_of(index * count, count), count)
+            moves.append((ref.at[at, :], own_ref))
+        copies = [
+            pltpu.make_async_copy(src, dst, sems.at[i]) for i, (src, dst) in enumerate(moves)
+        ]
+        for copy in copies:
+            copy.start()
+        wait_all(copies)
+
+    height, features = qkv_weight.shape[0], out_weight.shape[1]
+    low = jnp.bfloat16
+    return kernel_call(
+        kernel,
+        [ANYWHERE] * 4,
+        [
+            sds((height, qkv_weight.shape[1] // PLANE), low),
+            sds((features // PLANE, features), low),
+            sds((height, up_weight.shape[1] // PLANE), low),
+            sds((down_weight.shape[0] // PLANE, features), low),
+        ],
+        [pltpu.SemaphoreType.DMA((9,))],
+        0,
+        (qkv_weight, out_weight, up_weight, down_weight),
+    )
+
+
+def first_norm(tokens, packs):
+    def kernel(tokens_ref, p0, p1, p2, p3, vectors_ref, normed_ref):
+        z = lax.axis_index("shard")
+        packs = [ref[...].astype(jnp.float32) for ref in (p0, p1, p2, p3)]
+        vectors_ref[...] = jnp.zeros_like(vectors_ref)
+        for plane in range(DEPTH):
+            back = lax.rem(z + (DEPTH - plane), DEPTH)
+            pack = packs[3]
+            for step in range(3):
+                pack = jnp.where(back == step, packs[step], pack)
+            start = 0
+            for row, size in VECTORS:
+                for i in range(size // 128):
+                    at = plane * size + i * 128
+                    lanes = pl.ds(at % 1024, 128)
+                    vectors_ref[row + at // 1024 : row + at // 1024 + 1, lanes] = pack[
+                        start + i : start + i + 1
+                    ]
+                start += size // 128
+        xhat, unused = unit_rows(tokens_ref[...].astype(jnp.float32))
+        normed = xhat * vectors_ref[0:1, :] + vectors_ref[1:2, :]
+        normed_ref[...] = normed.astype(jnp.bfloat16)
+
+    return kernel_call(
+        kernel,
+        [LOCAL] * 5,
+        [sds((16, tokens.shape[1]), jnp.float32), sds(tokens.shape, jnp.bfloat16)],
+        [],
+        0,
+        (tokens, *packs),
+    )
+
+
+def second_norm(tokens, vectors, parts):
+    def kernel(tokens_ref, vectors_ref, own, two, four, six, middle_ref, normed_ref):
+        attended = total_of((own, two, four, six)) + vectors_ref[2:3, :]
+        middle = tokens_ref[...].astype(jnp.float32) + attended
+        middle_ref[...] = middle
+        xhat, unused = unit_rows(middle)
+        normed = xhat * vectors_ref[3:4, :] + vectors_ref[4:5, :]
+        normed_ref[...] = normed.astype(jnp.bfloat16)
+
+    return kernel_call(
+        kernel,
+        [LOCAL] * 6,
+        [sds(tokens.shape, jnp.float32), sds(tokens.shape, jnp.bfloat16)],
+        [],
+        0,
+        (tokens, vectors, *parts),
+    )
+
+
+def second_norm_back(lens, vectors, middle, cotangent, parts):
+    rows, features = middle.shape
+
+    def kernel(
+        lens_ref, vectors_ref, middle_ref, cotangent_ref, own, two, four, six,
+        grad_ref, low_ref, sums_ref,
+    ):
+        first = quarter_of(lax.axis_index("rep")) * rows
+        position = lax.broadcasted_iota(jnp.int32, (rows, 1), 0) + first
+        seed = cotangent_ref[...].astype(jnp.float32)
+        seed = jnp.where(position < lens_ref[0], seed, 0.0)
+        grad = total_of((own, two, four, six))
+        xhat, rstd = unit_rows(middle_ref[...])
+        total = seed + norm_back(grad, xhat, rstd, vectors_ref[3:4, :])
+        grad_ref[...] = total
+        low = total.astype(jnp.bfloat16)
+        low_ref[...] = low
+        sums_ref[0:1, :] = jnp.sum(grad * xhat, 0, keepdims=True)
+        sums_ref[1:2, :] = jnp.sum(grad, 0, keepdims=True)
+        sums_ref[2:3, :] = jnp.sum(low.astype(jnp.float32), 0, keepdims=True)
+        sums_ref[3:4, :] = jnp.sum(seed, 0, keepdims=True)
+
+    return kernel_call(
+        kernel,
+        [SCALARS] + [LOCAL] * 7,
+        [
+            sds((rows, features), jnp.float32),
+            sds((rows, features), jnp.bfloat16),
+            sds((4, features), jnp.float32),
+        ],
+        [],
+        0,
+        (lens, vectors, middle, cotangent, *parts),
+    )
+
+
+def first_norm_back(tokens, vectors, middle_grad, parts):
+    rows, features = tokens.shape
+
+    def kernel(tokens_ref, vectors_ref, base_ref, own, two, four, six, grad_ref, sums_ref):
+        grad = total_of((own, two, four, six))
+        xhat, rstd = unit_rows(tokens_ref[...].astype(jnp.float32))
+        total = base_ref[...] + norm_back(grad, xhat, rstd, vectors_ref[0:1, :])
+        grad_ref[...] = total.astype(jnp.bfloat16)
+        sums_ref[0:1, :] = jnp.sum(grad * xhat, 0, keepdims=True)
+        sums_ref[1:2, :] = jnp.sum(grad, 0, keepdims=True)
+
+    return kernel_call(
+        kernel,
+        [LOCAL] * 7,
+        [sds((rows, features), jnp.bfloat16), sds((2, features), jnp.float32)],
+        [],
+        0,
+        (tokens, vectors, middle_grad, *parts),
+    )
+
+
+def attention_forward(lens, slopes, blocks, weights, out_part, vectors):
+    rows, features = PLANE * blocks[0].shape[0], blocks[0].shape[1]
     span = rows // 2
     width = weights[0].shape[1]
     own = width // 3
@@ -431,18 +634,24 @@
     step_rows = span // QUARTERS
 
     def kernel(
-        lens_ref, slopes_ref, normed_ref, w0, w1, w2, w3, out_ref, bq_ref, bv_ref,
-        joint_ref, mixed_ref, keep_ref, give_ref, weight_ref, sems,
+        lens_ref, slopes_ref, n0, n1, n2, n3, n4, n5, n6, n7, w0, w1, w2, w3, out_ref, vectors_ref,
+        joint_ref, mixed_ref, keep_ref, give_ref, weight_ref, normed_ref, out_all, sems, more_sems,
     ):
         rep = lax.axis_index("rep")
-        wait_all(place_pieces((w0, w1, w2, w3), weight_ref, sems))
+        weight_copies = place_pieces((w0, w1, w2, w3), weight_ref, sems)
+        copies = load_blocks((n0, n1, n2, n3, n4, n5, n6, n7), normed_ref, more_sems)
+        out_copy = load(out_ref, out_all, sems.at[DEPTH])
+        mine = pl.ds(pl.multiple_of(rep * own, own), own)
+        bias_q, bias_v = vectors_ref[6:7, mine], vectors_ref[7:8, mine]
+        wait_all(weight_copies)
         for s in range(2):
             for c in range(2):
                 at = pl.ds((2 * s + c) * (span // 2), span // 2)
+                wait_all(copies[4 * s + 2 * c : 4 * s + 2 * c + 2])
                 joint = dot_nn(normed_ref[at, :], weight_ref[...])
-                joint_ref[at, :own] = (joint[:, :own] + bq_ref[...]).astype(jnp.bfloat16)
+                joint_ref[at, :own] = (joint[:, :own] + bias_q).astype(jnp.bfloat16)
                 joint_ref[at, own : 2 * own] = joint[:, own : 2 * own].astype(jnp.bfloat16)
-                joint_ref[at, 2 * own :] = (joint[:, 2 * own :] + bv_ref[...]).astype(jnp.bfloat16)
+                joint_ref[at, 2 * own :] = (joint[:, 2 * own :] + bias_v).astype(jnp.bfloat16)
         lane = lax.broadcasted_iota(jnp.int32, (step_rows, own), 1)
         key_pos = row_positions((1, span), 1, rep, 0)
         for s in range(2):
@@ -468,24 +677,32 @@
                     mixed = jnp.where(mine, dot_nn(probs.astype(jnp.bfloat16), values), mixed)
                 mixed_ref[at, :] = mixed.astype(jnp.bfloat16)
 
+            if s == 0:
+                out_copy.wait()
             for c, part_ref in enumerate((keep_ref, give_ref)):
                 at = pl.ds((2 * s + c) * (span // 2), span // 2)
-                part = dot_nn(mixed_ref[at, :], out_ref[...]).astype(jnp.bfloat16)
+                part = dot_nn(mixed_ref[at, :], out_all[...]).astype(jnp.bfloat16)
                 part_ref[s] = part.reshape(2, span // 4, features)
 
     half = sds((2, 2, span // 4, features), jnp.bfloat16)
     return kernel_call(
         kernel,
-        [SCALARS, SCALARS, LOCAL] + [ANYWHERE] * 4 + [LOCAL] * 3,
+        [SCALARS] * 2 + [ANYWHERE] * 13 + [LOCAL],
         [sds((rows, width), jnp.bfloat16), sds((rows, own), jnp.bfloat16), half, half],
-        [pltpu.VMEM((features, width), jnp.bfloat16), pltpu.SemaphoreType.DMA((DEPTH,))],
+        [
+            pltpu.VMEM((features, width), jnp.bfloat16),
+            pltpu.VMEM((rows, features), jnp.bfloat16),
+            pltpu.VMEM((own, features), jnp.bfloat16),
+            pltpu.SemaphoreType.DMA((DEPTH + 1,)),
+            pltpu.SemaphoreType.DMA((PLANE,)),
+        ],
         2 * rows * features * (width + own) + 8 * rows * span * own,
-        (lens, slopes, normed, *weights, out_part, bias_q, bias_v),
-    )
-
-
-def attention_backward(lens, slopes, grad, joint, weights, out_part):
-    rows, features = grad.shape
+        (lens, slopes, *blocks, *weights, out_part, vectors),
+    )
+
+
+def attention_backward(lens, slopes, blocks, joint, weights, out_part):
+    rows, features = PLANE * blocks[0].shape[0], blocks[0].shape[1]
     span = rows // 2
     width = weights[0].shape[1]
     own = width // 3
@@ -494,16 +711,23 @@
     step_rows = span // QUARTERS
 
     def kernel(
-        lens_ref, slopes_ref, grad_ref, joint_ref, w0, w1, w2, w3, out_ref,
+        lens_ref, slopes_ref, g0, g1, g2, g3, g4, g5, g6, g7, joint_hbm, w0, w1, w2, w3, out_ref,
         joint_grad_ref, sums_ref, keep_ref, give_ref,
-        weight_ref, mixed_grad_ref, key_acc, value_acc, sems,
+        weight_ref, mixed_grad_ref, key_acc, value_acc, joint_ref, grad_ref, out_all, sems, more_sems,
     ):
         rep = lax.axis_index("rep")
+        out_copy = load(out_ref, out_all, sems.at[DEPTH])
+        grad_copies = load_blocks((g0, g1, g2, g3, g4, g5, g6, g7), grad_ref, more_sems)
+        joint_copy = load(joint_hbm, joint_ref, sems.at[DEPTH + 1])
         copies = place_pieces((w0, w1, w2, w3), weight_ref, sems)
+        out_copy.wait()
         for s in range(2):
             for c in range(2):
                 at = pl.ds((2 * s + c) * (span // 2), span // 2)
-                mixed_grad_ref[at, :] = dot_nt(grad_ref[at, :], out_ref[...]).astype(jnp.bfloat16)
+                wait_all(grad_copies[4 * s + 2 * c : 4 * s + 2 * c + 2])
+                mixed_grad = dot_nt(grad_ref[at, :], out_all[...])
+                mixed_grad_ref[at, :] = mixed_grad.astype(jnp.bfloat16)
+        joint_copy.wait()
         lane = lax.broadcasted_iota(jnp.int32, (step_rows, own), 1)
         lane_all = lax.broadcasted_iota(jnp.int32, (span, own), 1)
         key_pos = row_positions((1, span), 1, rep, 0)
@@ -556,70 +780,185 @@
     half = sds((2, 2, span // 4, features), jnp.bfloat16)
     return kernel_call(
         kernel,
-        [SCALARS, SCALARS, LOCAL, LOCAL] + [ANYWHERE] * 4 + [LOCAL],
+        [SCALARS] * 2 + [ANYWHERE] * 14,
         [sds((rows, width), jnp.bfloat16), sds((1, width), jnp.float32), half, half],
         [
             pltpu.VMEM((features, width), jnp.bfloat16),
             pltpu.VMEM((rows, own), jnp.bfloat16),
             pltpu.VMEM((span, own), jnp.float32),
             pltpu.VMEM((span, own), jnp.float32),
-            pltpu.SemaphoreType.DMA((DEPTH,)),
+            pltpu.VMEM((rows, width), jnp.bfloat16),
+            pltpu.VMEM((rows, features), jnp.bfloat16),
+            pltpu.VMEM((own, features), jnp.bfloat16),
+            pltpu.SemaphoreType.DMA((DEPTH + 2,)),
+            pltpu.SemaphoreType.DMA((PLANE,)),
         ],
         2 * rows * features * (width + own) + 20 * rows * span * own,
-        (lens, slopes, grad, joint, *weights, out_part),
-    )
-
-
-def feed_forward(normed, grad, ups, downs, bias_up):
-    rows, features = normed.shape
+        (lens, slopes, *blocks, joint, *weights, out_part),
+    )
+
+
+def feed_forward(blocks, grad, ups, down, vectors):
+    count, features = blocks[0].shape
+    rows = PLANE * count
     units = ups[0].shape[1]
-    tile = rows // 4
+    tile = 2 * count
     root = math.sqrt(2.0 / math.pi)
     bend = 0.044715
 
     def kernel(
-        normed_ref, grad_ref, u0, u1, u2, u3, d0, d1, d2, d3, bias_ref,
-        active_ref, hidden_grad_ref, sums_ref, keep_ref, give_ref, back_keep_ref, back_give_ref,
-        up_ref, down_ref, sems,
+        n0, n1, n2, n3, n4, n5, n6, n7, grad_hbm, u0, u1, u2, u3, down_hbm, vectors_ref,
+        active_ref, hidden_grad_ref, sums_ref, branch_keep_ref, branch_give_ref, keep_ref, give_ref,
+        up_ref, down_ref, normed_ref, grad_ref, sems, more_sems,
     ):
-        up_copies = place_pieces((u0, u1, u2, u3), up_ref, sems.at[0])
-        down_copies = place_pieces((d0, d1, d2, d3), down_ref, sems.at[1])
-        wait_all(up_copies)
-        wait_all(down_copies)
-        sums_ref[...] = jnp.zeros_like(sums_ref)
-
-        @pl.loop(0, 2)
-        def _(s):
+        rep = lax.axis_index("rep")
+        up_copies = place_pieces((u0, u1, u2, u3), up_ref, more_sems)
+        copies = load_blocks((n0, n1, n2, n3, n4, n5, n6, n7), normed_ref, sems)
+        down_copy = load(down_hbm, down_ref, more_sems.at[DEPTH])
+        grad_copy = load(grad_hbm, grad_ref, more_sems.at[DEPTH + 1])
+        mine = pl.ds(pl.multiple_of(rep * 128, 128), 128)
+        bias = jnp.concatenate([vectors_ref[8 + p : 9 + p, mine] for p in range(DEPTH)], 1)
+        total = jnp.zeros((1, units), jnp.float32)
+        for s in range(2):
             for c in range(2):
-                at = pl.ds(pl.multiple_of((2 * s + c) * tile, tile), tile)
-                v = dot_nn(normed_ref[at, :], up_ref[...]) + bias_ref[...]
+                sources = [rep ^ (4 * s + 2 * x + c) for x in range(2)]
+                at = pl.ds((2 * s + c) * tile, tile)
+                if (s, c) == (0, 0):
+                    wait_all(up_copies)
+                wait_all(copies[4 * s + 2 * c : 4 * s + 2 * c + 2])
+                v = dot_nn(normed_ref[at, :], up_ref[...]) + bias
                 square = v * v
                 t = jnp.tanh(root * v * (1.0 + bend * square))
                 half = 0.5 * (1.0 + t)
                 active = (v * half).astype(jnp.bfloat16)
                 slope = half + (0.5 * root) * v * (1.0 - t * t) * (1.0 + 3.0 * bend * square)
-                active_ref[at, :] = active
-                hidden_grad = (dot_nt(grad_ref[at, :], down_ref[...]) * slope).astype(jnp.bfloat16)
+                if (s, c) == (0, 0):
+                    grad_copy.wait()
+                    down_copy.wait()
+                grad = jnp.concatenate([grad_ref[source] for source in sources], 0)
+                hidden_grad = (dot_nt(grad, down_ref[...]) * slope).astype(jnp.bfloat16)
                 hidden_grad_ref[at, :] = hidden_grad
-                sums_ref[...] += jnp.sum(hidden_grad.astype(jnp.float32), 0, keepdims=True)
-                part = dot_nn(active, down_ref[...]).astype(jnp.bfloat16)
-                (keep_ref, give_ref)[c][s] = part.reshape(2, tile // 2, features)
+                total = total + jnp.sum(hidden_grad.astype(jnp.float32), 0, keepdims=True)
                 back = dot_nt(hidden_grad, up_ref[...]).astype(jnp.bfloat16)
-                (back_keep_ref, back_give_ref)[c][s] = back.reshape(2, tile // 2, features)
-
-    half = sds((2, 2, rows // 8, features), jnp.bfloat16)
-    wide = sds((rows, units), jnp.bfloat16)
+                (keep_ref, give_ref)[c][s] = back.reshape(2, count, features)
+                branch = dot_nn(active, down_ref[...]).astype(jnp.bfloat16)
+                (branch_keep_ref, branch_give_ref)[c][s] = branch.reshape(2, count, features)
+                for x, source in enumerate(sources):
+                    active_ref[source] = active[x * count : (x + 1) * count]
+        sums_ref[...] = total
+
+    half = sds((2, 2, count, features), jnp.bfloat16)
     return kernel_call(
         kernel,
-        [LOCAL, LOCAL] + [ANYWHERE] * 8 + [LOCAL],
-        [wide, wide, sds((1, units), jnp.float32), half, half, half, half],
+        [ANYWHERE] * 14 + [LOCAL],
+        [
+            sds((PLANE, count, units), jnp.bfloat16),
+            sds((rows, units), jnp.bfloat16),
+            sds((1, units), jnp.float32),
+            half,
+            half,
+            half,
+            half,
+        ],
         [
             pltpu.VMEM((features, units), jnp.bfloat16),
-            pltpu.VMEM((units, features), jnp.bfloat16),
-            pltpu.SemaphoreType.DMA((2, DEPTH)),
+            pltpu.VMEM(down.shape, jnp.bfloat16),
+            pltpu.VMEM((rows, features), jnp.bfloat16),
+            pltpu.VMEM(grad.shape, jnp.bfloat16),
+            pltpu.SemaphoreType.DMA((PLANE,)),
+            pltpu.SemaphoreType.DMA((DEPTH + 2,)),
         ],
         8 * rows * features * units,
-        (normed, grad, *ups, *downs, bias_up),
+        (*blocks, grad, *ups, down, vectors),
+    )
+
+
+def feed_forward_weights(blocks, hidden_grad, active, grad):
+    count, features = blocks[0].shape
+    rows, units = hidden_grad.shape
+
+    def kernel(
+        n0, n1, n2, n3, n4, n5, n6, n7, hidden_grad_hbm, active_hbm, grad_hbm, up_ref, down_ref,
+        normed_ref, hidden_grad_ref, active_ref, grad_ref, sems, more_sems,
+    ):
+        active_copies = [
+            load(active_hbm, active_ref, more_sems.at[0]),
+            load(grad_hbm, grad_ref, more_sems.at[1]),
+        ]
+        copies = [load(hidden_grad_hbm, hidden_grad_ref, more_sems.at[2])]
+        copies += load_blocks((n0, n1, n2, n3, n4, n5, n6, n7), normed_ref, sems)
+        wait_all(active_copies)
+        grad = grad_ref[...].reshape(rows, features)
+        for p in range(DEPTH):
+            part = active_ref[:, :, p * 128 : (p + 1) * 128].reshape(rows, 128)
+            down_ref[p] = outer(part, grad).astype(jnp.bfloat16)
+        wait_all(copies)
+        for r in range(PLANE):
+            part = outer(normed_ref[:, r * 128 : (r + 1) * 128], hidden_grad_ref[...])
+            up_ref[:, r] = part.astype(jnp.bfloat16).reshape(DEPTH, 32, units)
+
+    low = jnp.bfloat16
+    return kernel_call(
+        kernel,
+        [ANYWHERE] * 11,
+        [sds((DEPTH, PLANE, 32, units), low), sds((DEPTH, units // DEPTH, features), low)],
+        [
+            pltpu.VMEM((rows, features), low),
+            pltpu.VMEM((rows, units), low),
+            pltpu.VMEM(active.shape, low),
+            pltpu.VMEM(grad.shape, low),
+            pltpu.SemaphoreType.DMA((PLANE,)),
+            pltpu.SemaphoreType.DMA((3,)),
+        ],
+        4 * rows * features * units,
+        (*blocks, hidden_grad, active, grad),
+    )
+
+
+def attention_weights(blocks, joint_grad, mixed, grads):
+    count, features = blocks[0].shape
+    rows, width = joint_grad.shape
+    own = mixed.shape[1]
+
+    def kernel(
+        n0, n1, n2, n3, n4, n5, n6, n7, joint_grad_hbm, mixed_hbm, g0, g1, g2, g3, g4, g5, g6, g7,
+        q0, q1, q2, q3, out_ref, normed_ref, joint_grad_ref, mixed_ref, grad_ref, sems, more_sems,
+    ):
+        z = lax.axis_index("shard")
+        copies = [load(joint_grad_hbm, joint_grad_ref, more_sems.at[0])]
+        copies += load_blocks((n0, n1, n2, n3, n4, n5, n6, n7), normed_ref, sems.at[0])
+        out_copies = [load(mixed_hbm, mixed_ref, more_sems.at[1])]
+        out_copies += load_blocks((g0, g1, g2, g3, g4, g5, g6, g7), grad_ref, sems.at[1])
+        wait_all(copies)
+        for r in range(PLANE):
+            part = outer(normed_ref[:, r * 128 : (r + 1) * 128], joint_grad_ref[...])
+            part = part.astype(jnp.bfloat16).reshape(DEPTH, 32, width)
+            for step, ref in enumerate((q0, q1, q2, q3)):
+                for p in range(DEPTH):
+
+                    @pl.when(lax.rem(z + step, DEPTH) == p)
+                    def _():
+                        ref[r] = part[p]
+
+        wait_all(out_copies)
+        part = outer(mixed_ref[...], grad_ref[...])
+        out_ref[...] = part.astype(jnp.bfloat16).reshape(DEPTH, own // DEPTH, features)
+
+    low = jnp.bfloat16
+    return kernel_call(
+        kernel,
+        [ANYWHERE] * 18,
+        [sds((PLANE, 32, width), low)] * 4 + [sds((DEPTH, own // DEPTH, features), low)],
+        [
+            pltpu.VMEM((rows, features), low),
+            pltpu.VMEM((rows, width), low),
+            pltpu.VMEM((rows, own), low),
+            pltpu.VMEM((rows, features), low),
+            pltpu.SemaphoreType.DMA((2, PLANE)),
+            pltpu.SemaphoreType.DMA((2,)),
+        ],
+        2 * rows * features * (width + own),
+        (*blocks, joint_grad, mixed, *grads),
     )
 
 
@@ -644,22 +983,8 @@
     row_count, feature_count = tokens.shape
     rep = lax.axis_index("rep")
     z = lax.axis_index("shard")
-    quarter = rep & 3
     own = feature_count // PLANE
-
-    own_length = jnp.sum(jnp.where(jnp.arange(lengths.shape[0]) == assign[0], lengths, 0))
-    ones = jnp.ones((16, feature_count), jnp.float32)
-    length_rows = jnp.where(
-        jnp.arange(16)[:, None] == 0, ones * (own_length // 16), ones * (own_length % 16)
-    )
-    moved = to_home(jnp.concatenate([tokens, cotangent, length_rows.astype(jnp.bfloat16)], 0))
-    tokens, cotangent = moved[:row_count], moved[row_count : 2 * row_count]
-    length_parts = moved[2 * row_count : 2 * row_count + 2, 0].astype(jnp.int32)
-    seq_length = 16 * length_parts[0] + length_parts[1]
-    other_length = over_rep(seq_length.astype(jnp.float32).reshape(1, 1), 4)
-    lens = jnp.stack([seq_length, other_length.astype(jnp.int32)[0, 0]])
-    heads = (2 * rep + jnp.arange(2)).astype(jnp.float32)
-    slopes = jnp.exp2(-8.0 * (heads + 1.0) / HEADS)
+    devices = PLANE * DEPTH
 
     small = (
         first_gain,
@@ -671,54 +996,23 @@
         up_bias,
         down_bias,
     )
-    packed = jnp.concatenate([item.reshape(-1, 256) for item in small], 0)
-    around = [packed] + [over_z(packed, step) for step in (1, 2, 3)]
-    parts = []
-    for plane in range(DEPTH):
-        back = lax.rem(z + (DEPTH - plane), DEPTH)
-        parts.append(
-            sum(
-                jnp.where(back == step, around[step].astype(jnp.float32), 0.0)
-                for step in range(DEPTH)
-            )
-        )
-    stacked = jnp.stack(parts, 0)
-    whole_small = []
+    whole = sum(item.shape[0] for item in small)
     start = 0
+    packed = jnp.zeros((whole,), jnp.bfloat16)
     for item in small:
-        size = item.shape[0] // 256
-        whole_small.append(stacked[:, start : start + size].reshape(-1))
-        start += size
-    (
-        gain_first,
-        shift_first,
-        bias_qv,
-        bias_out,
-        gain_second,
-        shift_second,
-        bias_up,
-        bias_down,
-    ) = whole_small
-
-    def columns(weight):
-        blocks = weight.reshape(weight.shape[0], -1, PLANE, 128)
-        return lax.dynamic_index_in_dim(blocks, rep, 2, keepdims=False).reshape(weight.shape[0], -1)
-
-    def rows_of(weight, index, count):
-        return lax.dynamic_slice_in_dim(weight, index * count, count, 0)
-
-    qkv_own = columns(qkv_weight)
-    up_own = columns(up_weight)
-    down_own = rows_of(down_weight, rep, down_weight.shape[0] // PLANE)
-    out_own = rows_of(out_weight, rep & 1, own)
-    qkv_own, up_own, down_own, out_own = lax.optimization_barrier(
-        (qkv_own, up_own, down_own, out_own)
-    )
-
-    def to_planes(block):
-        return [block] + [over_z(block, step) for step in (1, 2, 3)]
-
-    qkv_parts = to_planes(qkv_own)
+        packed = packed + jnp.pad(item, (start, whole - start - item.shape[0]))
+        start += item.shape[0]
+    packed = packed.reshape(-1, 128)
+    packs = [packed] + [over_z(packed, step) for step in (1, 2, 3)]
+    tokens = to_home(tokens)
+
+    weights = after((qkv_weight, out_weight, up_weight, down_weight), tokens, packs)
+    qkv_own, out_own, up_own, down_own = own_eighths(*weights)
+    vectors, normed = first_norm(tokens, packs)
+    normed_blocks = gather_plane(normed)
+    qkv_own = after(qkv_own, normed)
+    qkv_parts = [qkv_own] + [over_z(qkv_own, step) for step in (1, 2, 3)]
+    out_own = after(out_own, qkv_parts)
     out_part = jnp.where(z == rep >> 1, out_own, jnp.zeros_like(out_own))
     for step in (1, 2, 3):
         out_part = out_part + over_all(
@@ -727,55 +1021,78 @@
                 i - i % DEPTH + (i % DEPTH + step) % DEPTH if i % DEPTH == i // 8 else None
             ),
         )
-    up_parts = to_planes(up_own)
-    down_parts = to_planes(down_own)
-
-    rows_in = tokens.astype(jnp.float32)
-    row_valid = (quarter * row_count + jnp.arange(row_count) < seq_length)[:, None]
-    seed_grad = jnp.where(row_valid, cotangent.astype(jnp.float32), 0.0)
-    branch_grad = seed_grad.astype(jnp.bfloat16)
-
-    normed_low = layer_norm(rows_in, gain_first, shift_first).astype(jnp.bfloat16)
-    normed_plane = gather_plane(normed_low)
-    bias_blocks = bias_qv.reshape(2, PLANE, own)
-    bias_own = lax.dynamic_index_in_dim(bias_blocks, rep, 1, keepdims=False)
-    joint, mixed_plane, keep, give = attention_forward(
-        lens, slopes, normed_plane, qkv_parts, out_part, bias_own[:1], bias_own[1:]
-    )
-    branch_grad_plane = gather_plane(branch_grad)
-    middle = rows_in + scatter_plane(keep, give) + bias_out
-    normed_two_low = layer_norm(middle, gain_second, shift_second).astype(jnp.bfloat16)
-    normed_two_plane = gather_plane(normed_two_low)
-    bias_up_own = lax.dynamic_index_in_dim(bias_up.reshape(-1, PLANE, 128), rep, 1, keepdims=False)
-    active, hidden_grad, hidden_sums, keep, give, back_keep, back_give = feed_forward(
-        normed_two_plane, branch_grad_plane, up_parts, down_parts, bias_up_own.reshape(1, -1)
-    )
-    normed_two_grad = scatter_plane(back_keep, back_give)
-    unused_two, second_pull = jax.vjp(layer_norm, middle, gain_second, shift_second)
-    middle_from_norm, gain_second_grad, shift_second_grad = second_pull(normed_two_grad)
-    middle_grad = seed_grad + middle_from_norm
-    attended_grad = middle_grad.astype(jnp.bfloat16)
-    attended_grad_plane = gather_plane(attended_grad)
-    joint_grad, joint_sums, back_keep, back_give = attention_backward(
-        lens, slopes, attended_grad_plane, joint, qkv_parts, out_part
-    )
-    normed_grad = scatter_plane(back_keep, back_give)
-    qkv_grad = column_parts_to_rows(outer(normed_plane, joint_grad))
-
-    branch = scatter_plane(keep, give) + bias_down
-    layer_out = from_home((middle + branch).astype(jnp.bfloat16)).astype(jnp.float32)
-    down_slice = outer(active, branch_grad_plane).reshape(DEPTH, -1, feature_count)
-    down_summed = summed_over_z(down_slice).astype(jnp.bfloat16)
+    up_own = after(up_own, out_part)
+    up_parts = [up_own] + [over_z(up_own, step) for step in (1, 2, 3)]
+
+    own_length = jnp.sum(jnp.where(jnp.arange(lengths.shape[0]) == assign[0], lengths, 0))
+    ones = jnp.ones((16, feature_count), jnp.float32)
+    length_rows = jnp.where(
+        jnp.arange(16)[:, None] == 0, ones * (own_length // 16), ones * (own_length % 16)
+    )
+    moved = to_home(
+        after(jnp.concatenate([cotangent, length_rows.astype(jnp.bfloat16)], 0), normed)
+    )
+    cotangent = moved[:row_count]
+    length_parts = moved[row_count : row_count + 2, 0].astype(jnp.int32)
+    seq_length = 16 * length_parts[0] + length_parts[1]
+    other_length = over_rep(seq_length.astype(jnp.float32).reshape(1, 1), 4)
+    lens = jnp.stack([seq_length, other_length.astype(jnp.int32)[0, 0]])
+    heads = (2 * rep + jnp.arange(2)).astype(jnp.float32)
+    slopes = jnp.exp2(-8.0 * (heads + 1.0) / HEADS)
+    position = quarter_of(rep) * row_count + jnp.arange(row_count)
+    branch_grad = jnp.where((position < seq_length)[:, None], cotangent, jnp.zeros_like(cotangent))
+
+    branch_grad_plane = lax.all_gather(branch_grad, "rep", axis=0, tiled=False)
+    down_all = lax.all_gather(after(down_own, branch_grad), "shard", axis=0, tiled=True)
+    joint, mixed, keep, give = attention_forward(
+        lens, slopes, normed_blocks, qkv_parts, out_part, vectors
+    )
+    parts = send_parts(add_halves(keep, over_rep(give, 1)))
+    middle, normed_two = second_norm(tokens, vectors, after(parts, up_parts))
+    normed_two_blocks = gather_plane(normed_two)
+    active, hidden_grad, hidden_sums, branch_keep, branch_give, keep, give = feed_forward(
+        normed_two_blocks, branch_grad_plane, up_parts, down_all, vectors
+    )
+    received = over_rep(give, 1)
+    branch_received = over_rep(after(branch_give, received), 1)
+    halves = add_halves(keep, received)
+    up_slice, down_slice = feed_forward_weights(
+        normed_two_blocks, after(hidden_grad, halves), active, branch_grad_plane
+    )
+    up_summed = scattered_over_z(up_slice)
+    down_summed = scattered_over_z(down_slice)
+    parts = after(send_parts(halves), up_slice, branch_received)
+    middle_grad, attended_grad, second_sums = second_norm_back(
+        lens, vectors, middle, cotangent, parts
+    )
+    attended_blocks = gather_plane(attended_grad)
+    branch_halves = add_halves(branch_keep, after(branch_received, attended_grad))
+    joint_grad, joint_sums, keep, give = attention_backward(
+        after(lens, branch_halves), slopes, attended_blocks, joint, qkv_parts, out_part
+    )
+    branch_own, *branch_rest = send_parts(branch_halves)
+    received = after(over_rep(give, 1), branch_rest)
+    halves = add_halves(keep, received)
+    *qkv_slices, out_slice = attention_weights(
+        normed_blocks, after(joint_grad, halves), mixed, attended_blocks
+    )
+    parts = after(send_parts(halves), qkv_slices)
+    tokens_grad, first_sums = first_norm_back(tokens, vectors, middle_grad, parts)
+    tokens_grad = from_home(tokens_grad).astype(jnp.float32)
+    qkv_summed = qkv_slices[0].astype(jnp.float32)
+    for step in (1, 2, 3):
+        qkv_summed = qkv_summed + over_z(qkv_slices[step], step).astype(jnp.float32)
+    qkv_grad = columns_to_rows(qkv_summed.astype(jnp.bfloat16))
+    out_grad = scattered_over_z(out_slice).astype(jnp.float32)
+
+    branch = branch_own + sum(part.astype(jnp.float32) for part in branch_rest)
+    layer_low = (middle + branch + vectors[5:6]).astype(jnp.bfloat16)
+    layer_out = from_home(after(layer_low, halves)).astype(jnp.float32)
     down_grad = over_all(
-        down_summed, lambda i: (2 * (i % DEPTH) + i // 16) * DEPTH + (i // DEPTH) % DEPTH
+        after(down_summed, halves),
+        lambda i: (2 * (i % DEPTH) + i // 16) * DEPTH + (i // DEPTH) % DEPTH,
     ).astype(jnp.float32)
-    up_grad = column_parts_to_rows(outer(normed_two_plane, hidden_grad))
-    out_slice = outer(mixed_plane, attended_grad_plane)
-    out_grad = summed_over_z(out_slice.reshape(DEPTH, -1, feature_count))
-
-    unused_three, first_pull = jax.vjp(layer_norm, rows_in, gain_first, shift_first)
-    rows_from_norm, gain_first_grad, shift_first_grad = first_pull(normed_grad)
-    tokens_grad = from_home((middle_grad + rows_from_norm).astype(jnp.bfloat16)).astype(jnp.float32)
+    up_grad = columns_to_rows(after(up_summed, halves))
 
     at_rep = (jnp.arange(PLANE) == rep)[None, :, None]
 
@@ -784,16 +1101,15 @@
 
     joint_parts = joint_sums.reshape(3, own)
     small_grads = (
-        gain_first_grad,
-        shift_first_grad,
+        first_sums[0],
+        first_sums[1],
         placed(jnp.concatenate([joint_parts[:1], joint_parts[2:]], 0)),
-        jnp.sum(attended_grad.astype(jnp.float32), 0),
-        gain_second_grad,
-        shift_second_grad,
+        second_sums[2],
+        second_sums[0],
+        second_sums[1],
         placed(hidden_sums),
-        jnp.sum(branch_grad.astype(jnp.float32), 0),
-    )
-    devices = PLANE * DEPTH
+        second_sums[3],
+    )
     small_packed = jnp.concatenate(
         [g.reshape(devices, g.shape[0] // devices) for g in small_grads], 1
     ).astype(jnp.bfloat16)

time: 434 us -> 335 us (0.77)
  the two profiles are of different devices: /device:TPU:4 before, /device:TPU:0 now
where the time goes in v3:
time: 335 us; the launch traced here: 334 us
  starting transfers between devices  117 us (35%)
  waiting for transfers between devices  90.8 us (27%)
  Pallas kernels  76.7 us (23%)
  between operations  20 us (6%)
  local copies, waits for them, and re-layouts  16.5 us (5%)
  other arithmetic  13.4 us (4%)
    pallas_call x14, Pallas kernels, kernel_call(): pl.pallas_call(kernel, out_shape=outs, in_specs=ins, out_specs=[LOCAL] *...  76.7 us
    ppermute x38, waiting for transfers between devices, over_rep(): return lax.ppermute(value, 'rep', [(i, i ^ flip) for i in range(PLANE)])  54.9 us
    ppermute x38, starting transfers between devices, over_rep(): return lax.ppermute(value, 'rep', [(i, i ^ flip) for i in range(PLANE)])  40 us
    ppermute x12, starting transfers between devices, over_z(): lax.ppermute(value, 'shard', [(i, (i + step) % DEPTH) for i in range(DEPT...  35.5 us
    ppermute x8, starting transfers between devices, over_all(): return lax.ppermute(value, ('rep', 'shard'), pairs)  22.6 us
    ppermute x12, waiting for transfers between devices, over_z(): lax.ppermute(value, 'shard', [(i, (i + step) % DEPTH) for i in range(DEPT...  21.4 us
    all_to_all x1, starting transfers between devices, body_planes(): lax.all_to_all(small_packed, ('rep', 'shard'), 0, 0, tiled=True)  11.2 us
    unnamed x120, local copies, waits for them, and re-layouts  11.2 us
  transfers between devices with their start and end apart: 66, of which 20 were waited for; matrix products, arithmetic and copies ran while one was open for 5% of the time, Pallas kernels for 17%

profile of v3, /device:TPU:0, one launch (start us, length us, event | category | flops | bytes accessed | tf_op | source)
XLA Modules:
  0.0 334.0 jit_solution(4268049476173109869)
XLA Ops:
  32.2 15.4 %collective-permute-start.13 = (bf16[256,384]{1,0:T(8,128)(2,1)}, bf16[256,384]{1,0:T(8,128)(2,1)S(1)}, u32[]{:S(2)}, u32[]{:S(2)}) collective-permute-start(bf16[256,384]{1,0:T(8,128)(2,1)} %get-tuple-element.103.w0), channel_id=1, source_target_pairs={{0,1},{1,2},{2,3},{3,0},{4,5},{5,6},{6,7},{7,4},{8,9},{9,10},{10,1... | collective-permute-start | bytes 589832 | tf_op jit(solution)/shard_map/ppermute | solution.py:291
  59.8 8.5 %collective-permute-done.14.w2 = bf16[256,384]{1,0:T(8,128)(2,1)S(1)} collective-permute-done((bf16[256,384]{1,0:T(8,128)(2,1)}, bf16[256,384]{1,0:T(8,128)(2,1)S(1)}, u32[]{:S(2)}, u32[]{:S(2)}) %collective-permute-start.14) | collective-permute-done | bytes 196640 | tf_op jit(solution)/shard_map/ppermute | solution.py:291
  68.3 12.2 %collective-permute-start.18 = (bf16[128,1024]{1,0:T(8,128)(2,1)}, bf16[128,1024]{1,0:T(8,128)(2,1)S(1)}, u32[]{:S(2)}, u32[]{:S(2)}) collective-permute-start(bf16[128,1024]{1,0:T(8,128)(2,1)} %get-tuple-element.105), channel_id=1, source_target_pairs={{0,3},{4,7},{9,8},{13,12},{18,17},{22,21},{27,26},{31,30}} | collective-permute-start | bytes 786440 | tf_op jit(solution)/shard_map/ppermute | solution.py:296
  85.4 3.9 %collective-permute-start.16 = (bf16[128,1024]{1,0:T(8,128)(2,1)}, bf16[128,1024]{1,0:T(8,128)(2,1)S(1)}, u32[]{:S(2)}, u32[]{:S(2)}) collective-permute-start(bf16[128,1024]{1,0:T(8,128)(2,1)} %get-tuple-element.105), channel_id=1, source_target_pairs={{0,1},{4,5},{9,10},{13,14},{18,19},{22,23},{27,24},{31,28}} | collective-permute-start | bytes 786440 | tf_op jit(solution)/shard_map/ppermute | solution.py:296
  98.2 13.6 %shard_map.265 = (bf16[1024,384]{1,0:T(8,128)(2,1)}, bf16[1024,128]{1,0:T(8,128)(2,1)}, bf16[2,2,128,1024]{3,2,1,0:T(8,128)(2,1)}, bf16[2,2,128,1024]{3,2,1,0:T(8,128)(2,1)}) custom-call(s32[2]{0:T(128)} %pad_add_fusion.lens_ref, f32[2]{0:T(128)} %multiply_exponential_fusion.slopes_ref, bf16[128,1024]{1,0:T(8,128)(2,1)} %get-tuple-element.96.n0, ...), custom_call_target="tpu_custom_call" | custom-call | flops 1610612736 | bytes 8388608 | tf_op jit(solution)/shard_map/pallas_call | solution.py:471
  119.5 6.4 %collective-permute-start.21 = (bf16[128,1024]{1,0:T(8,128)(2,1)}, bf16[128,1024]{1,0:T(8,128)(2,1)S(1)}, u32[]{:S(2)}, u32[]{:S(2)}) collective-permute-start(bf16[128,1024]{1,0:T(8,128)(2,1)} %get-tuple-element.110), channel_id=1, source_target_pairs={{0,16},{4,20},{8,24},{12,28},{16,0},{20,4},{24,8},{28,12},{1,17},{... | collective-permute-start | bytes 786440 | tf_op jit(solution)/shard_map/ppermute | solution.py:287
  128.9 4.8 %collective-permute-done.24.u2 = bf16[256,512]{1,0:T(8,128)(2,1)S(1)} collective-permute-done((bf16[256,512]{1,0:T(8,128)(2,1)S(1)}, bf16[256,512]{1,0:T(8,128)(2,1)S(1)}, u32[]{:S(2)}, u32[]{:S(2)}) %collective-permute-start.24) | collective-permute-done | bytes 262176 | tf_op jit(solution)/shard_map/ppermute | solution.py:291
  133.7 4.1 %collective-permute-done.21.four = bf16[128,1024]{1,0:T(8,128)(2,1)S(1)} collective-permute-done((bf16[128,1024]{1,0:T(8,128)(2,1)}, bf16[128,1024]{1,0:T(8,128)(2,1)S(1)}, u32[]{:S(2)}, u32[]{:S(2)}) %collective-permute-start.21) | collective-permute-done | bytes 262176 | tf_op jit(solution)/shard_map/ppermute | solution.py:287
  144.6 6.0 %collective-permute-done.27.n2 = bf16[128,1024]{1,0:T(8,128)(2,1)S(1)} collective-permute-done((bf16[128,1024]{1,0:T(8,128)(2,1)}, bf16[128,1024]{1,0:T(8,128)(2,1)S(1)}, u32[]{:S(2)}, u32[]{:S(2)}) %collective-permute-start.27) | collective-permute-done | bytes 262176 | tf_op jit(solution)/shard_map/ppermute | solution.py:287
  157.5 10.8 %shard_map.268 = (bf16[8,128,512]{2,1,0:T(8,128)(2,1)}, bf16[1024,512]{1,0:T(8,128)(2,1)}, f32[1,512]{1,0:T(1,128)}, bf16[2,2,128,1024]{3,2,1,0:T(8,128)(2,1)}, ...) custom-call(bf16[128,1024]{1,0:T(8,128)(2,1)} %get-tuple-element.119.n0, ...), custom_call_target="tpu_custom_call" | custom-call | flops 4294967296 | bytes 8388608 | tf_op jit(solution)/shard_map/pallas_call | solution.py:471
  174.9 6.2 %shard_map.270 = (bf16[4,8,32,512]{3,2,1,0:T(8,128)(2,1)}, bf16[4,128,1024]{2,1,0:T(8,128)(2,1)}) custom-call(bf16[128,1024]{1,0:T(8,128)(2,1)} %get-tuple-element.119.n0, bf16[128,1024]{1,0:T(8,128)(2,1)} %copy-done.42, bf16[128,1024]{1,0:T(8,128)(2,1)} %copy-done.39, bf16[128,1024]{1,0:T(8,128)(2,1)} %copy-done.43, bf16[128,1024]{1,0:T(8,128)(2,1)} %copy-done.40, ...), custom_call_target="tpu_custom_call" | custom-call | flops 2147483648 | bytes 8388608 | tf_op jit(solution)/shard_map/pallas_call | solution.py:471
  185.1 5.6 %collective-permute-done.35.two = bf16[128,1024]{1,0:T(8,128)(2,1)S(1)} collective-permute-done((bf16[128,1024]{1,0:T(8,128)(2,1)S(1)}, bf16[128,1024]{1,0:T(8,128)(2,1)S(1)}, u32[]{:S(2)}, u32[]{:S(2)}) %collective-permute-start.35) | collective-permute-done | bytes 262176 | tf_op jit(solution)/shard_map/ppermute | solution.py:287
  190.7 5.8 %collective-permute-done.36.four = bf16[128,1024]{1,0:T(8,128)(2,1)S(1)} collective-permute-done((bf16[128,1024]{1,0:T(8,128)(2,1)S(1)}, bf16[128,1024]{1,0:T(8,128)(2,1)S(1)}, u32[]{:S(2)}, u32[]{:S(2)}) %collective-permute-start.36) | collective-permute-done | bytes 262176 | tf_op jit(solution)/shard_map/ppermute | solution.py:287
  203.8 6.0 %collective-permute-done.42.g2 = bf16[128,1024]{1,0:T(8,128)(2,1)S(1)} collective-permute-done((bf16[128,1024]{1,0:T(8,128)(2,1)}, bf16[128,1024]{1,0:T(8,128)(2,1)S(1)}, u32[]{:S(2)}, u32[]{:S(2)}) %collective-permute-start.42) | collective-permute-done | bytes 262176 | tf_op jit(solution)/shard_map/ppermute | solution.py:287
  209.7 5.3 %collective-permute-done.44.g4 = bf16[128,1024]{1,0:T(8,128)(2,1)S(1)} collective-permute-done((bf16[128,1024]{1,0:T(8,128)(2,1)}, bf16[128,1024]{1,0:T(8,128)(2,1)S(1)}, u32[]{:S(2)}, u32[]{:S(2)}) %collective-permute-start.44) | collective-permute-done | bytes 262176 | tf_op jit(solution)/shard_map/ppermute | solution.py:287
  219.3 16.5 %shard_map.273 = (bf16[1024,384]{1,0:T(8,128)(2,1)}, f32[1,384]{1,0:T(1,128)}, bf16[2,2,128,1024]{3,2,1,0:T(8,128)(2,1)}, bf16[2,2,128,1024]{3,2,1,0:T(8,128)(2,1)}) custom-call(s32[2]{0:T(128)} %pad_add_fusion.lens_ref, f32[2]{0:T(128)} %multiply_exponential_fusion.slopes_ref, bf16[128,1024]{1,0:T(8,128)(2,1)} %get-tuple-element.139.g0, ...), custom_call_target="tpu_custom_call" | custom-call | flops 2415919104 | bytes 8388608 | tf_op jit(solution)/shard_map/pallas_call | solution.py:471
  240.7 6.3 %collective-permute-done.40 = bf16[128,1024]{1,0:T(8,128)(2,1)S(1)} collective-permute-done((bf16[128,1024]{1,0:T(8,128)(2,1)}, bf16[128,1024]{1,0:T(8,128)(2,1)S(1)}, u32[]{:S(2)}, u32[]{:S(2)}) %collective-permute-start.40) | collective-permute-done | bytes 262176 | tf_op jit(solution)/shard_map/ppermute | solution.py:287
  247.0 4.7 %collective-permute-done.39 = bf16[128,1024]{1,0:T(8,128)(2,1)S(1)} collective-permute-done((bf16[128,1024]{1,0:T(8,128)(2,1)}, bf16[128,1024]{1,0:T(8,128)(2,1)S(1)}, u32[]{:S(2)}, u32[]{:S(2)}) %collective-permute-start.39) | collective-permute-done | bytes 262176 | tf_op jit(solution)/shard_map/ppermute | solution.py:287
  259.2 6.7 %shard_map.275 = (bf16[8,32,384]{2,1,0:T(8,128)(2,1)}, bf16[8,32,384]{2,1,0:T(8,128)(2,1)}, bf16[8,32,384]{2,1,0:T(8,128)(2,1)}, bf16[8,32,384]{2,1,0:T(8,128)(2,1)}, bf16[4,32,1024]{2,1,0:T(8,128)(2,1)}) custom-call(bf16[128,1024]{1,0:T(8,128)(2,1)} %get-tuple-element.96.n0, bf16[128,1024]{1,0:T(8,128)(2,1)} %copy-done.11, bf16[128,1024]{1,0:T(8,128)(2,1)} %copy-done.8, ...), custom_call_target="tpu_custom_call" | custom-call | flops 1073741824 | bytes 8388608 | tf_op jit(solution)/shard_map/pallas_call | solution.py:471
  268.4 4.3 %collective-permute-start.55 = (bf16[8,32,384]{2,1,0:T(8,128)(2,1)}, bf16[8,32,384]{2,1,0:T(8,128)(2,1)S(1)}, u32[]{:S(2)}, u32[]{:S(2)}) collective-permute-start(bf16[8,32,384]{2,1,0:T(8,128)(2,1)} %get-tuple-element.161), channel_id=1, source_target_pairs={{0,2},{1,3},{2,0},{3,1},{4,6},{5,7},{6,4},{7,5},{8,10},{9,11},{10,... | collective-permute-start | bytes 589832 | tf_op jit(solution)/shard_map/ppermute | solution.py:291
  284.7 11.2 %all-to-all-start = ((bf16[32,2,192]{2,1,0:T(2,128)(2,1)}), bf16[32,2,192]{2,1,0:T(2,128)(2,1)S(1)}, u32[]{:S(2)}, u32[]{:S(2)}) async-start(bf16[32,2,192]{2,1,0:T(2,128)(2,1)} %reshape.250), calls=%async_computation | async-start | bytes 65536 | tf_op jit(solution)/shard_map/all_to_all | solution.py:1116
  296.0 8.1 %collective-permute-done.55 = bf16[8,32,384]{2,1,0:T(8,128)(2,1)S(1)} collective-permute-done((bf16[8,32,384]{2,1,0:T(8,128)(2,1)}, bf16[8,32,384]{2,1,0:T(8,128)(2,1)S(1)}, u32[]{:S(2)}, u32[]{:S(2)}) %collective-permute-start.55) | collective-permute-done | bytes 196640 | tf_op jit(solution)/shard_map/ppermute | solution.py:291
  308.8 5.6 %all-to-all-done = bf16[32,2,192]{2,1,0:T(2,128)(2,1)S(1)} async-done(((bf16[32,2,192]{2,1,0:T(2,128)(2,1)}), bf16[32,2,192]{2,1,0:T(2,128)(2,1)S(1)}, u32[]{:S(2)}, u32[]{:S(2)}) %all-to-all-start) | async-done | bytes 24608 | tf_op jit(solution)/shard_map/all_to_all | solution.py:1116
  319.7 4.2 %all-to-all-done.1 = bf16[8,32,384]{2,1,0:T(8,128)(2,1)S(1)} async-done(((bf16[8,32,384]{2,1,0:T(8,128)(2,1)}), bf16[8,32,384]{2,1,0:T(8,128)(2,1)S(1)}, u32[]{:S(2)}, u32[]{:S(2)}) %all-to-all-start.1) | async-done | bytes 196640 | tf_op jit(solution)/shard_map/all_to_all | solution.py:377
  (295 shorter events, 132.1 us)
Async XLA Ops:
  7.2 148.1 %all-gather.4.cloned.1.call-start = ((), (), s32[]{:S(2)}) async-start(), calls=%async_computation.6 | async-start | bytes 1310720 | tf_op jit(solution)/shard_map/all_gather | solution.py:1046
  31.4 125.5 %all-gather.6.cloned.1.call-start = ((), (), s32[]{:S(2)}) async-start(), calls=%async_computation.10 | async-start | bytes 2359296 | tf_op jit(solution)/shard_map/all_gather | solution.py:1045
  32.1 240.5 %reduce-scatter.6.cloned.1.call-start = ((), (), s32[]{:S(2)}) async-start(), calls=%async_computation.8 | async-start | bytes 1310720 | tf_op jit(solution)/shard_map/reduce_scatter | solution.py:367
  32.2 24.1 %collective-permute-start.13 = (bf16[256,384]{1,0:T(8,128)(2,1)}, bf16[256,384]{1,0:T(8,128)(2,1)S(1)}, u32[]{:S(2)}, u32[]{:S(2)}) collective-permute-start(bf16[256,384]{1,0:T(8,128)(2,1)} %get-tuple-element.103.w0), channel_id=1, source_target_pairs={{0,1},{1,2},{2,3},{3,0},{4,5},{5,6},{6,7},{7,4},{8,9},{9,10},{10,1... | collective-permute-start | bytes 589832 | tf_op jit(solution)/shard_map/ppermute | solution.py:291
  47.6 20.7 %collective-permute-start.14 = (bf16[256,384]{1,0:T(8,128)(2,1)}, bf16[256,384]{1,0:T(8,128)(2,1)S(1)}, u32[]{:S(2)}, u32[]{:S(2)}) collective-permute-start(bf16[256,384]{1,0:T(8,128)(2,1)} %get-tuple-element.103.w0), channel_id=1, source_target_pairs={{0,2},{1,3},{2,0},{3,1},{4,6},{5,7},{6,4},{7,5},{8,10},{9,11},{10,... | collective-permute-start | bytes 589832 | tf_op jit(solution)/shard_map/ppermute | solution.py:291
  48.1 20.2 %collective-permute-start.15 = (bf16[256,384]{1,0:T(8,128)(2,1)}, bf16[256,384]{1,0:T(8,128)(2,1)S(1)}, u32[]{:S(2)}, u32[]{:S(2)}) collective-permute-start(bf16[256,384]{1,0:T(8,128)(2,1)} %get-tuple-element.103.w0), channel_id=1, source_target_pairs={{0,3},{1,0},{2,1},{3,2},{4,7},{5,4},{6,5},{7,6},{8,11},{9,8},{10,9... | collective-permute-start | bytes 589832 | tf_op jit(solution)/shard_map/ppermute | solution.py:291
  50.0 31.8 %collective-permute-start.7 = (bf16[128,1024]{1,0:T(8,128)(2,1)S(1)}, bf16[128,1024]{1,0:T(8,128)(2,1)S(1)}, u32[]{:S(2)}, u32[]{:S(2)}) collective-permute-start(bf16[128,1024]{1,0:T(8,128)(2,1)S(1)} %copy-done.7), channel_id=1, source_target_pairs={{0,8},{4,12},{8,0},{12,4},{16,24},{20,28},{24,16},{28,20},{1,9},{5... | collective-permute-start | bytes 786440 | tf_op jit(solution)/shard_map/ppermute | solution.py:287
  53.0 37.5 %collective-permute-start.9 = (bf16[128,1024]{1,0:T(8,128)(2,1)S(1)}, bf16[128,1024]{1,0:T(8,128)(2,1)S(1)}, u32[]{:S(2)}, u32[]{:S(2)}) collective-permute-start(bf16[128,1024]{1,0:T(8,128)(2,1)S(1)} %copy-done.7), channel_id=1, source_target_pairs={{0,16},{4,20},{8,24},{12,28},{16,0},{20,4},{24,8},{28,12},{1,17},{... | collective-permute-start | bytes 786440 | tf_op jit(solution)/shard_map/ppermute | solution.py:287
  56.3 34.3 %collective-permute-start.11 = (bf16[128,1024]{1,0:T(8,128)(2,1)S(1)}, bf16[128,1024]{1,0:T(8,128)(2,1)S(1)}, u32[]{:S(2)}, u32[]{:S(2)}) collective-permute-start(bf16[128,1024]{1,0:T(8,128)(2,1)S(1)} %copy-done.7), channel_id=1, source_target_pairs={{0,24},{4,28},{8,16},{12,20},{16,8},{20,12},{24,0},{28,4},{1,25},{... | collective-permute-start | bytes 786440 | tf_op jit(solution)/shard_map/ppermute | solution.py:287
  68.3 22.8 %collective-permute-start.18 = (bf16[128,1024]{1,0:T(8,128)(2,1)}, bf16[128,1024]{1,0:T(8,128)(2,1)S(1)}, u32[]{:S(2)}, u32[]{:S(2)}) collective-permute-start(bf16[128,1024]{1,0:T(8,128)(2,1)} %get-tuple-element.105), channel_id=1, source_target_pairs={{0,3},{4,7},{9,8},{13,12},{18,17},{22,21},{27,26},{31,30}} | collective-permute-start | bytes 786440 | tf_op jit(solution)/shard_map/ppermute | solution.py:296
  113.3 20.4 %collective-permute-start.24 = (bf16[256,512]{1,0:T(8,128)(2,1)S(1)}, bf16[256,512]{1,0:T(8,128)(2,1)S(1)}, u32[]{:S(2)}, u32[]{:S(2)}) collective-permute-start(bf16[256,512]{1,0:T(8,128)(2,1)S(1)} %copy-done.34), channel_id=1, source_target_pairs={{0,2},{1,3},{2,0},{3,1},{4,6},{5,7},{6,4},{7,5},{8,10},{9,11},{10,... | collective-permute-start | bytes 786440 | tf_op jit(solution)/shard_map/ppermute | solution.py:291
  113.3 20.4 %collective-permute-start.25 = (bf16[256,512]{1,0:T(8,128)(2,1)S(1)}, bf16[256,512]{1,0:T(8,128)(2,1)S(1)}, u32[]{:S(2)}, u32[]{:S(2)}) collective-permute-start(bf16[256,512]{1,0:T(8,128)(2,1)S(1)} %copy-done.34), channel_id=1, source_target_pairs={{0,3},{1,0},{2,1},{3,2},{4,7},{5,4},{6,5},{7,6},{8,11},{9,8},{10,9... | collective-permute-start | bytes 786440 | tf_op jit(solution)/shard_map/ppermute | solution.py:291
  181.1 95.6 %reduce-scatter.8.cloned.1.call-start = ((), (), s32[]{:S(2)}) async-start(), calls=%async_computation.9 | async-start | bytes 1310720 | tf_op jit(solution)/shard_map/reduce_scatter | solution.py:367
  255.5 20.6 %collective-permute-start.50 = (bf16[128,1024]{1,0:T(8,128)(2,1)}, bf16[128,1024]{1,0:T(8,128)(2,1)S(1)}, u32[]{:S(2)}, u32[]{:S(2)}) collective-permute-start(bf16[128,1024]{1,0:T(8,128)(2,1)} %get-tuple-element.151), channel_id=1, source_target_pairs={{0,8},{4,12},{8,0},{12,4},{16,24},{20,28},{24,16},{28,20},{1,9},{5... | collective-permute-start | bytes 786440 | tf_op jit(solution)/shard_map/ppermute | solution.py:287
  256.6 20.1 %collective-permute-start.51 = (bf16[128,1024]{1,0:T(8,128)(2,1)}, bf16[128,1024]{1,0:T(8,128)(2,1)S(1)}, u32[]{:S(2)}, u32[]{:S(2)}) collective-permute-start(bf16[128,1024]{1,0:T(8,128)(2,1)} %get-tuple-element.152), channel_id=1, source_target_pairs={{0,16},{4,20},{8,24},{12,28},{16,0},{20,4},{24,8},{28,12},{1,17},{... | collective-permute-start | bytes 786440 | tf_op jit(solution)/shard_map/ppermute | solution.py:287
  257.4 20.0 %collective-permute-start.52 = (bf16[128,1024]{1,0:T(8,128)(2,1)}, bf16[128,1024]{1,0:T(8,128)(2,1)S(1)}, u32[]{:S(2)}, u32[]{:S(2)}) collective-permute-start(bf16[128,1024]{1,0:T(8,128)(2,1)} %get-tuple-element.153), channel_id=1, source_target_pairs={{0,24},{4,28},{8,16},{12,20},{16,8},{20,12},{24,0},{28,4},{1,25},{... | collective-permute-start | bytes 786440 | tf_op jit(solution)/shard_map/ppermute | solution.py:287
  265.9 30.0 %collective-permute-start.56 = (bf16[8,32,384]{2,1,0:T(8,128)(2,1)}, bf16[8,32,384]{2,1,0:T(8,128)(2,1)S(1)}, u32[]{:S(2)}, u32[]{:S(2)}) collective-permute-start(bf16[8,32,384]{2,1,0:T(8,128)(2,1)} %get-tuple-element.162), channel_id=1, source_target_pairs={{0,3},{1,0},{2,1},{3,2},{4,7},{5,4},{6,5},{7,6},{8,11},{9,8},{10,9... | collective-permute-start | bytes 589832 | tf_op jit(solution)/shard_map/ppermute | solution.py:291
  268.4 35.7 %collective-permute-start.55 = (bf16[8,32,384]{2,1,0:T(8,128)(2,1)}, bf16[8,32,384]{2,1,0:T(8,128)(2,1)S(1)}, u32[]{:S(2)}, u32[]{:S(2)}) collective-permute-start(bf16[8,32,384]{2,1,0:T(8,128)(2,1)} %get-tuple-element.161), channel_id=1, source_target_pairs={{0,2},{1,3},{2,0},{3,1},{4,6},{5,7},{6,4},{7,5},{8,10},{9,11},{10,... | collective-permute-start | bytes 589832 | tf_op jit(solution)/shard_map/ppermute | solution.py:291
  276.1 49.9 %reduce-scatter.4.cloned.1.call-start = ((), (), s32[]{:S(2)}) async-start(), calls=%async_computation.7 | async-start | bytes 327680 | tf_op jit(solution)/shard_map/reduce_scatter | solution.py:367
  276.1 27.9 %collective-permute-start.54 = (bf16[8,32,384]{2,1,0:T(8,128)(2,1)}, bf16[8,32,384]{2,1,0:T(8,128)(2,1)S(1)}, u32[]{:S(2)}, u32[]{:S(2)}) collective-permute-start(bf16[8,32,384]{2,1,0:T(8,128)(2,1)} %get-tuple-element.160), channel_id=1, source_target_pairs={{0,1},{1,2},{2,3},{3,0},{4,5},{5,6},{6,7},{7,4},{8,9},{9,10},{10,1... | collective-permute-start | bytes 589832 | tf_op jit(solution)/shard_map/ppermute | solution.py:291
  276.7 30.4 %collective-permute-start.49 = (bf16[128,1024]{1,0:T(8,128)(2,1)S(1)}, bf16[128,1024]{1,0:T(8,128)(2,1)S(1)}, u32[]{:S(2)}, u32[]{:S(2)}) collective-permute-start(bf16[128,1024]{1,0:T(8,128)(2,1)S(1)} %add_convert_fusion), channel_id=1, source_target_pairs={{0,0},{1,16},{2,4},{3,20},{4,2},{5,18},{6,6},{7,22},{8,1},{9,17},{... | collective-permute-start | bytes 786440 | tf_op jit(solution)/shard_map/ppermute | solution.py:296
  277.4 30.6 %collective-permute-start.57 = (bf16[128,1024]{1,0:T(8,128)(2,1)}, bf16[128,1024]{1,0:T(8,128)(2,1)S(1)}, u32[]{:S(2)}, u32[]{:S(2)}) collective-permute-start(bf16[128,1024]{1,0:T(8,128)(2,1)} %bitcast.47), channel_id=1, source_target_pairs={{0,0},{1,8},{2,16},{3,24},{4,1},{5,9},{6,17},{7,25},{8,2},{9,10},{... | collective-permute-start | bytes 786440 | tf_op jit(solution)/shard_map/ppermute | solution.py:296
  284.7 29.6 %all-to-all-start = ((bf16[32,2,192]{2,1,0:T(2,128)(2,1)}), bf16[32,2,192]{2,1,0:T(2,128)(2,1)S(1)}, u32[]{:S(2)}, u32[]{:S(2)}) async-start(bf16[32,2,192]{2,1,0:T(2,128)(2,1)} %reshape.250), calls=%async_computation | async-start | bytes 65536 | tf_op jit(solution)/shard_map/all_to_all | solution.py:1116
  306.4 18.7 %collective-permute-start.53 = (bf16[128,1024]{1,0:T(8,128)(2,1)S(1)}, bf16[128,1024]{1,0:T(8,128)(2,1)S(1)}, u32[]{:S(2)}, u32[]{:S(2)}) collective-permute-start(bf16[128,1024]{1,0:T(8,128)(2,1)S(1)} %copy-done.38), channel_id=1, source_target_pairs={{0,0},{1,16},{2,4},{3,20},{4,2},{5,18},{6,6},{7,22},{8,1},{9,17},{... | collective-permute-start | bytes 786440 | tf_op jit(solution)/shard_map/ppermute | solution.py:296
  (100 other events, 945.4 us)
Sparse Core Ops, SparseCore 0:
  31.5 49.9 all-gather.3
  83.4 36.5 all-gather.5
  181.2 29.5 reduce-scatter.5
  215.7 28.7 reduce-scatter.7
  278.9 22.7 reduce-scatter.3

commit v4 on v3

--- a/solution.py
+++ b/solution.py
@@ -317,9 +317,9 @@
     return lax.optimization_barrier((value, *earlier))[0]
 
 
-def gather_plane(rows):
+def gather_plane(rows, earlier=()):
     near = over_rep(rows, 1)
-    two, four, six = (over_rep(rows, flip) for flip in (2, 4, 6))
+    two, four, six = after(tuple(over_rep(rows, flip) for flip in (2, 4, 6)), earlier)
     return [rows, near, two, over_rep(two, 1), four, over_rep(four, 1), six, over_rep(six, 1)]
 
 
@@ -373,10 +373,10 @@
     )
 
 
-def columns_to_rows(parts):
-    arrived = lax.all_to_all(parts, "rep", 0, 0, tiled=True)
-    spread = arrived.reshape(PLANE, parts.shape[1], -1, 128)
-    return jnp.transpose(spread, (1, 2, 0, 3)).reshape(parts.shape[1], -1).astype(jnp.float32)
+def spread_columns(arrived):
+    count = arrived.shape[1]
+    parts = arrived.reshape(PLANE, count, -1, 128)
+    return jnp.transpose(parts, (1, 2, 0, 3)).reshape(count, -1).astype(jnp.float32)
 
 
 def dot_nn(left, right):
@@ -417,11 +417,12 @@
 
 
 def load_blocks(blocks, whole, sems):
-    count = blocks[0].shape[0]
+    count = whole.shape[0] // PLANE
     copies = []
     for place, k in enumerate(ORDER):
         at = pl.ds(place * count, count)
-        copies.append(pltpu.make_async_copy(blocks[k], whole.at[at], sems.at[place]))
+        block = blocks[k].at[pl.ds(0, count)]
+        copies.append(pltpu.make_async_copy(block, whole.at[at], sems.at[place]))
         copies[-1].start()
     return copies
 
@@ -480,17 +481,29 @@
 
 
 def own_eighths(qkv_weight, out_weight, up_weight, down_weight):
-    def kernel(qkv_ref, out_ref, up_ref, down_ref, qkv_own, out_own, up_own, down_own, sems):
+    height, features = qkv_weight.shape[0], out_weight.shape[1]
+    units = up_weight.shape[1] // PLANE
+    half = features // 2
+
+    def kernel(qkv_ref, out_ref, up_ref, down_ref, qkv_own, out_own, wide_own, sems):
         rep = lax.axis_index("rep")
         moves = []
-        for ref, own_ref in ((qkv_ref, qkv_own), (up_ref, up_own)):
-            for j in range(own_ref.shape[1] // 128):
+        for ref, own_ref in ((qkv_ref, qkv_own), (up_ref, wide_own)):
+            for j in range(ref.shape[1] // (128 * PLANE)):
                 at = pl.ds(pl.multiple_of(1024 * j + 128 * rep, 128), 128)
                 moves.append((ref.at[:, at], own_ref.at[:, pl.ds(128 * j, 128)]))
-        for ref, own_ref, index in ((out_ref, out_own, rep & 1), (down_ref, down_own, rep)):
-            count = own_ref.shape[0]
-            at = pl.ds(pl.multiple_of(index * count, count), count)
-            moves.append((ref.at[at, :], own_ref))
+        count = out_own.shape[0]
+        at = pl.ds(pl.multiple_of((rep & 1) * count, count), count)
+        moves.append((out_ref.at[at, :], out_own))
+        count = down_ref.shape[0] // PLANE
+        at = pl.ds(pl.multiple_of(rep * count, count), count)
+        for j in range(2):
+            moves.append(
+                (
+                    down_ref.at[at, pl.ds(j * half, half)],
+                    wide_own.at[pl.ds(j * count, count), pl.ds(units, half)],
+                )
+            )
         copies = [
             pltpu.make_async_copy(src, dst, sems.at[i]) for i, (src, dst) in enumerate(moves)
         ]
@@ -498,7 +511,6 @@
             copy.start()
         wait_all(copies)
 
-    height, features = qkv_weight.shape[0], out_weight.shape[1]
     low = jnp.bfloat16
     return kernel_call(
         kernel,
@@ -506,17 +518,18 @@
         [
             sds((height, qkv_weight.shape[1] // PLANE), low),
             sds((features // PLANE, features), low),
-            sds((height, up_weight.shape[1] // PLANE), low),
-            sds((down_weight.shape[0] // PLANE, features), low),
+            sds((height, units + half), low),
         ],
-        [pltpu.SemaphoreType.DMA((9,))],
+        [pltpu.SemaphoreType.DMA((10,))],
         0,
         (qkv_weight, out_weight, up_weight, down_weight),
     )
 
 
-def first_norm(tokens, packs):
-    def kernel(tokens_ref, p0, p1, p2, p3, vectors_ref, normed_ref):
+def first_norm(moved, packs):
+    count, features = moved.shape[0] // 2, moved.shape[1]
+
+    def kernel(moved_ref, p0, p1, p2, p3, vectors_ref, normed_ref, tokens_ref):
         z = lax.axis_index("shard")
         packs = [ref[...].astype(jnp.float32) for ref in (p0, p1, p2, p3)]
         vectors_ref[...] = jnp.zeros_like(vectors_ref)
@@ -534,17 +547,19 @@
                         start + i : start + i + 1
                     ]
                 start += size // 128
-        xhat, unused = unit_rows(tokens_ref[...].astype(jnp.float32))
+        tokens = moved_ref[:count]
+        tokens_ref[...] = tokens
+        xhat, unused = unit_rows(tokens.astype(jnp.float32))
         normed = xhat * vectors_ref[0:1, :] + vectors_ref[1:2, :]
         normed_ref[...] = normed.astype(jnp.bfloat16)
 
     return kernel_call(
         kernel,
         [LOCAL] * 5,
-        [sds((16, tokens.shape[1]), jnp.float32), sds(tokens.shape, jnp.bfloat16)],
+        [sds((16, features), jnp.float32), *[sds((count, features), jnp.bfloat16)] * 2],
         [],
         0,
-        (tokens, *packs),
+        (moved, *packs),
     )
 
 
@@ -567,17 +582,14 @@
     )
 
 
-def second_norm_back(lens, vectors, middle, cotangent, parts):
+def second_norm_back(vectors, middle, seed_low, parts):
     rows, features = middle.shape
 
     def kernel(
-        lens_ref, vectors_ref, middle_ref, cotangent_ref, own, two, four, six,
+        vectors_ref, middle_ref, seed_ref, own, two, four, six,
         grad_ref, low_ref, sums_ref,
     ):
-        first = quarter_of(lax.axis_index("rep")) * rows
-        position = lax.broadcasted_iota(jnp.int32, (rows, 1), 0) + first
-        seed = cotangent_ref[...].astype(jnp.float32)
-        seed = jnp.where(position < lens_ref[0], seed, 0.0)
+        seed = seed_ref[...].astype(jnp.float32)
         grad = total_of((own, two, four, six))
         xhat, rstd = unit_rows(middle_ref[...])
         total = seed + norm_back(grad, xhat, rstd, vectors_ref[3:4, :])
@@ -591,7 +603,7 @@
 
     return kernel_call(
         kernel,
-        [SCALARS] + [LOCAL] * 7,
+        [LOCAL] * 7,
         [
             sds((rows, features), jnp.float32),
             sds((rows, features), jnp.bfloat16),
@@ -599,7 +611,7 @@
         ],
         [],
         0,
-        (lens, vectors, middle, cotangent, *parts),
+        (vectors, middle, seed_low, *parts),
     )
 
 
@@ -624,7 +636,7 @@
     )
 
 
-def attention_forward(lens, slopes, blocks, weights, out_part, vectors):
+def attention_forward(lens, slopes, blocks, weights, vectors):
     rows, features = PLANE * blocks[0].shape[0], blocks[0].shape[1]
     span = rows // 2
     width = weights[0].shape[1]
@@ -634,13 +646,12 @@
     step_rows = span // QUARTERS
 
     def kernel(
-        lens_ref, slopes_ref, n0, n1, n2, n3, n4, n5, n6, n7, w0, w1, w2, w3, out_ref, vectors_ref,
-        joint_ref, mixed_ref, keep_ref, give_ref, weight_ref, normed_ref, out_all, sems, more_sems,
+        own_length, other_length, slopes_ref, n0, n1, n2, n3, n4, n5, n6, n7, w0, w1, w2, w3,
+        vectors_ref, joint_ref, mixed_ref, weight_ref, normed_ref, sems, more_sems,
     ):
         rep = lax.axis_index("rep")
         weight_copies = place_pieces((w0, w1, w2, w3), weight_ref, sems)
         copies = load_blocks((n0, n1, n2, n3, n4, n5, n6, n7), normed_ref, more_sems)
-        out_copy = load(out_ref, out_all, sems.at[DEPTH])
         mine = pl.ds(pl.multiple_of(rep * own, own), own)
         bias_q, bias_v = vectors_ref[6:7, mine], vectors_ref[7:8, mine]
         wait_all(weight_copies)
@@ -657,13 +668,15 @@
         for s in range(2):
             keys = joint_ref[pl.ds(s * span, span), own : 2 * own]
             values = joint_ref[pl.ds(s * span, span), 2 * own :]
+            length = (own_length, other_length)[s][0:1, 0:1]
+            inside = key_pos.astype(jnp.float32) < length
 
             @pl.loop(0, QUARTERS)
             def _(i):
                 first = pl.multiple_of(i * step_rows, step_rows)
                 at = pl.ds(s * span + first, step_rows)
                 query_pos = row_positions((step_rows, 1), 0, rep, first)
-                allowed = (key_pos <= query_pos) & (key_pos < lens_ref[s])
+                allowed = (key_pos <= query_pos) & inside
                 distance = (query_pos - key_pos).astype(jnp.float32)
                 query = joint_ref[at, :own]
                 mixed = jnp.zeros((step_rows, own), jnp.float32)
@@ -677,27 +690,35 @@
                     mixed = jnp.where(mine, dot_nn(probs.astype(jnp.bfloat16), values), mixed)
                 mixed_ref[at, :] = mixed.astype(jnp.bfloat16)
 
-            if s == 0:
-                out_copy.wait()
-            for c, part_ref in enumerate((keep_ref, give_ref)):
-                at = pl.ds((2 * s + c) * (span // 2), span // 2)
-                part = dot_nn(mixed_ref[at, :], out_all[...]).astype(jnp.bfloat16)
-                part_ref[s] = part.reshape(2, span // 4, features)
-
-    half = sds((2, 2, span // 4, features), jnp.bfloat16)
     return kernel_call(
         kernel,
-        [SCALARS] * 2 + [ANYWHERE] * 13 + [LOCAL],
-        [sds((rows, width), jnp.bfloat16), sds((rows, own), jnp.bfloat16), half, half],
+        [LOCAL] * 2 + [SCALARS] + [ANYWHERE] * 12 + [LOCAL],
+        [sds((rows, width), jnp.bfloat16), sds((rows, own), jnp.bfloat16)],
         [
             pltpu.VMEM((features, width), jnp.bfloat16),
             pltpu.VMEM((rows, features), jnp.bfloat16),
-            pltpu.VMEM((own, features), jnp.bfloat16),
-            pltpu.SemaphoreType.DMA((DEPTH + 1,)),
+            pltpu.SemaphoreType.DMA((DEPTH,)),
             pltpu.SemaphoreType.DMA((PLANE,)),
         ],
-        2 * rows * features * (width + own) + 8 * rows * span * own,
-        (lens, slopes, *blocks, *weights, out_part, vectors),
+        2 * rows * features * width + 8 * rows * span * own,
+        (*lens, slopes, *blocks, *weights, vectors),
+    )
+
+
+def out_projection(mixed, out_part):
+    rows, features = mixed.shape[0], out_part.shape[1]
+    tile = rows // 4
+
+    def kernel(mixed_ref, out_ref, keep_ref, give_ref):
+        for s in range(2):
+            for c, part_ref in enumerate((keep_ref, give_ref)):
+                at = pl.ds((2 * s + c) * tile, tile)
+                part = dot_nn(mixed_ref[at, :], out_ref[...]).astype(jnp.bfloat16)
+                part_ref[s] = part.reshape(2, tile // 2, features)
+
+    half = sds((2, 2, tile // 2, features), jnp.bfloat16)
+    return kernel_call(
+        kernel, [LOCAL] * 2, [half, half], [], 2 * rows * features * mixed.shape[1], (mixed, out_part)
     )
 
 
@@ -711,7 +732,8 @@
     step_rows = span // QUARTERS
 
     def kernel(
-        lens_ref, slopes_ref, g0, g1, g2, g3, g4, g5, g6, g7, joint_hbm, w0, w1, w2, w3, out_ref,
+        own_length, other_length, slopes_ref, g0, g1, g2, g3, g4, g5, g6, g7,
+        joint_hbm, w0, w1, w2, w3, out_ref,
         joint_grad_ref, sums_ref, keep_ref, give_ref,
         weight_ref, mixed_grad_ref, key_acc, value_acc, joint_ref, grad_ref, out_all, sems, more_sems,
     ):
@@ -734,6 +756,8 @@
         for s in range(2):
             keys = joint_ref[pl.ds(s * span, span), own : 2 * own]
             values = joint_ref[pl.ds(s * span, span), 2 * own :]
+            length = (own_length, other_length)[s][0:1, 0:1]
+            inside = key_pos.astype(jnp.float32) < length
             key_acc[...] = jnp.zeros_like(key_acc)
             value_acc[...] = jnp.zeros_like(value_acc)
 
@@ -742,7 +766,7 @@
                 first = pl.multiple_of(i * step_rows, step_rows)
                 at = pl.ds(s * span + first, step_rows)
                 query_pos = row_positions((step_rows, 1), 0, rep, first)
-                allowed = (key_pos <= query_pos) & (key_pos < lens_ref[s])
+                allowed = (key_pos <= query_pos) & inside
                 distance = (query_pos - key_pos).astype(jnp.float32)
                 query = joint_ref[at, :own]
                 mixed_grad = mixed_grad_ref[at, :]
@@ -780,7 +804,7 @@
     half = sds((2, 2, span // 4, features), jnp.bfloat16)
     return kernel_call(
         kernel,
-        [SCALARS] * 2 + [ANYWHERE] * 14,
+        [LOCAL] * 2 + [SCALARS] + [ANYWHERE] * 14,
         [sds((rows, width), jnp.bfloat16), sds((1, width), jnp.float32), half, half],
         [
             pltpu.VMEM((features, width), jnp.bfloat16),
@@ -794,34 +818,39 @@
             pltpu.SemaphoreType.DMA((PLANE,)),
         ],
         2 * rows * features * (width + own) + 20 * rows * span * own,
-        (lens, slopes, *blocks, joint, *weights, out_part),
-    )
-
-
-def feed_forward(blocks, grad, ups, down, vectors):
+        (*lens, slopes, *blocks, joint, *weights, out_part),
+    )
+
+
+def feed_forward(blocks, grads, wide, vectors):
     count, features = blocks[0].shape
     rows = PLANE * count
-    units = ups[0].shape[1]
+    half_width = features // 2
+    units = wide.shape[1] - half_width
     tile = 2 * count
     root = math.sqrt(2.0 / math.pi)
     bend = 0.044715
 
     def kernel(
-        n0, n1, n2, n3, n4, n5, n6, n7, grad_hbm, u0, u1, u2, u3, down_hbm, vectors_ref,
+        n0, n1, n2, n3, n4, n5, n6, n7, g0, g1, g2, g3, g4, g5, g6, g7, wide_hbm, vectors_ref,
         active_ref, hidden_grad_ref, sums_ref, branch_keep_ref, branch_give_ref, keep_ref, give_ref,
-        up_ref, down_ref, normed_ref, grad_ref, sems, more_sems,
+        up_ref, down_ref, normed_ref, grad_ref, sems, grad_sems, more_sems,
     ):
         rep = lax.axis_index("rep")
-        up_copies = place_pieces((u0, u1, u2, u3), up_ref, more_sems)
+        up_copies = [load(wide_hbm.at[:, pl.ds(0, units)], up_ref, more_sems.at[0])]
         copies = load_blocks((n0, n1, n2, n3, n4, n5, n6, n7), normed_ref, sems)
-        down_copy = load(down_hbm, down_ref, more_sems.at[DEPTH])
-        grad_copy = load(grad_hbm, grad_ref, more_sems.at[DEPTH + 1])
+        grad_copies = load_blocks((g0, g1, g2, g3, g4, g5, g6, g7), grad_ref, grad_sems)
+        down_copies = []
+        for p in range(DEPTH):
+            for j in range(2):
+                source = wide_hbm.at[pl.ds((2 * p + j) * 128, 128), pl.ds(units, half_width)]
+                to = down_ref.at[pl.ds(p * 128, 128), pl.ds(j * half_width, half_width)]
+                down_copies.append(load(source, to, more_sems.at[2 + 2 * p + j]))
         mine = pl.ds(pl.multiple_of(rep * 128, 128), 128)
         bias = jnp.concatenate([vectors_ref[8 + p : 9 + p, mine] for p in range(DEPTH)], 1)
         total = jnp.zeros((1, units), jnp.float32)
         for s in range(2):
             for c in range(2):
-                sources = [rep ^ (4 * s + 2 * x + c) for x in range(2)]
                 at = pl.ds((2 * s + c) * tile, tile)
                 if (s, c) == (0, 0):
                     wait_all(up_copies)
@@ -833,26 +862,24 @@
                 active = (v * half).astype(jnp.bfloat16)
                 slope = half + (0.5 * root) * v * (1.0 - t * t) * (1.0 + 3.0 * bend * square)
                 if (s, c) == (0, 0):
-                    grad_copy.wait()
-                    down_copy.wait()
-                grad = jnp.concatenate([grad_ref[source] for source in sources], 0)
-                hidden_grad = (dot_nt(grad, down_ref[...]) * slope).astype(jnp.bfloat16)
+                    wait_all(grad_copies)
+                    wait_all(down_copies)
+                hidden_grad = (dot_nt(grad_ref[at, :], down_ref[...]) * slope).astype(jnp.bfloat16)
                 hidden_grad_ref[at, :] = hidden_grad
                 total = total + jnp.sum(hidden_grad.astype(jnp.float32), 0, keepdims=True)
                 back = dot_nt(hidden_grad, up_ref[...]).astype(jnp.bfloat16)
                 (keep_ref, give_ref)[c][s] = back.reshape(2, count, features)
                 branch = dot_nn(active, down_ref[...]).astype(jnp.bfloat16)
+                active_ref[at, :] = active
                 (branch_keep_ref, branch_give_ref)[c][s] = branch.reshape(2, count, features)
-                for x, source in enumerate(sources):
-                    active_ref[source] = active[x * count : (x + 1) * count]
         sums_ref[...] = total
 
     half = sds((2, 2, count, features), jnp.bfloat16)
     return kernel_call(
         kernel,
-        [ANYWHERE] * 14 + [LOCAL],
+        [ANYWHERE] * 17 + [LOCAL],
         [
-            sds((PLANE, count, units), jnp.bfloat16),
+            sds((rows, units), jnp.bfloat16),
             sds((rows, units), jnp.bfloat16),
             sds((1, units), jnp.float32),
             half,
@@ -862,73 +889,72 @@
         ],
         [
             pltpu.VMEM((features, units), jnp.bfloat16),
-            pltpu.VMEM(down.shape, jnp.bfloat16),
+            pltpu.VMEM((units, features), jnp.bfloat16),
             pltpu.VMEM((rows, features), jnp.bfloat16),
-            pltpu.VMEM(grad.shape, jnp.bfloat16),
+            pltpu.VMEM((rows, features), jnp.bfloat16),
             pltpu.SemaphoreType.DMA((PLANE,)),
-            pltpu.SemaphoreType.DMA((DEPTH + 2,)),
+            pltpu.SemaphoreType.DMA((PLANE,)),
+            pltpu.SemaphoreType.DMA((2 + 2 * DEPTH,)),
         ],
         8 * rows * features * units,
-        (*blocks, grad, *ups, down, vectors),
-    )
-
-
-def feed_forward_weights(blocks, hidden_grad, active, grad):
+        (*blocks, *grads, wide, vectors),
+    )
+
+
+def feed_forward_weights(blocks, hidden_grad, active, grads):
     count, features = blocks[0].shape
     rows, units = hidden_grad.shape
 
     def kernel(
-        n0, n1, n2, n3, n4, n5, n6, n7, hidden_grad_hbm, active_hbm, grad_hbm, up_ref, down_ref,
-        normed_ref, hidden_grad_ref, active_ref, grad_ref, sems, more_sems,
+        n0, n1, n2, n3, n4, n5, n6, n7, g0, g1, g2, g3, g4, g5, g6, g7, hidden_grad_hbm, active_hbm,
+        wide_ref, normed_ref, hidden_grad_ref, active_ref, grad_ref, sems, grad_sems, more_sems,
     ):
-        active_copies = [
-            load(active_hbm, active_ref, more_sems.at[0]),
-            load(grad_hbm, grad_ref, more_sems.at[1]),
-        ]
-        copies = [load(hidden_grad_hbm, hidden_grad_ref, more_sems.at[2])]
+        active_copies = [load(active_hbm, active_ref, more_sems.at[0])]
+        active_copies += load_blocks((g0, g1, g2, g3, g4, g5, g6, g7), grad_ref, grad_sems)
+        copies = [load(hidden_grad_hbm, hidden_grad_ref, more_sems.at[1])]
         copies += load_blocks((n0, n1, n2, n3, n4, n5, n6, n7), normed_ref, sems)
         wait_all(active_copies)
-        grad = grad_ref[...].reshape(rows, features)
         for p in range(DEPTH):
-            part = active_ref[:, :, p * 128 : (p + 1) * 128].reshape(rows, 128)
-            down_ref[p] = outer(part, grad).astype(jnp.bfloat16)
+            part = active_ref[:, p * 128 : (p + 1) * 128]
+            down = outer(part, grad_ref[...]).astype(jnp.bfloat16)
+            wide_ref[p, :128, units:] = down[:, : features // 2]
+            wide_ref[p, 128:, units:] = down[:, features // 2 :]
         wait_all(copies)
         for r in range(PLANE):
             part = outer(normed_ref[:, r * 128 : (r + 1) * 128], hidden_grad_ref[...])
-            up_ref[:, r] = part.astype(jnp.bfloat16).reshape(DEPTH, 32, units)
+            part = part.astype(jnp.bfloat16).reshape(DEPTH, 32, units)
+            wide_ref[:, r * 32 : (r + 1) * 32, :units] = part
 
     low = jnp.bfloat16
     return kernel_call(
         kernel,
-        [ANYWHERE] * 11,
-        [sds((DEPTH, PLANE, 32, units), low), sds((DEPTH, units // DEPTH, features), low)],
+        [ANYWHERE] * 18,
+        [sds((DEPTH, PLANE * 32, units + features // 2), low)],
         [
             pltpu.VMEM((rows, features), low),
             pltpu.VMEM((rows, units), low),
-            pltpu.VMEM(active.shape, low),
-            pltpu.VMEM(grad.shape, low),
+            pltpu.VMEM((rows, units), low),
+            pltpu.VMEM((rows, features), low),
             pltpu.SemaphoreType.DMA((PLANE,)),
-            pltpu.SemaphoreType.DMA((3,)),
+            pltpu.SemaphoreType.DMA((PLANE,)),
+            pltpu.SemaphoreType.DMA((2,)),
         ],
         4 * rows * features * units,
-        (*blocks, hidden_grad, active, grad),
-    )
-
-
-def attention_weights(blocks, joint_grad, mixed, grads):
-    count, features = blocks[0].shape
+        (*blocks, *grads, hidden_grad, active),
+    )[0]
+
+
+def qkv_weights(blocks, joint_grad):
+    features = blocks[0].shape[1]
     rows, width = joint_grad.shape
-    own = mixed.shape[1]
 
     def kernel(
-        n0, n1, n2, n3, n4, n5, n6, n7, joint_grad_hbm, mixed_hbm, g0, g1, g2, g3, g4, g5, g6, g7,
-        q0, q1, q2, q3, out_ref, normed_ref, joint_grad_ref, mixed_ref, grad_ref, sems, more_sems,
+        n0, n1, n2, n3, n4, n5, n6, n7, joint_grad_hbm,
+        q0, q1, q2, q3, normed_ref, joint_grad_ref, sems, more_sems,
     ):
         z = lax.axis_index("shard")
         copies = [load(joint_grad_hbm, joint_grad_ref, more_sems.at[0])]
-        copies += load_blocks((n0, n1, n2, n3, n4, n5, n6, n7), normed_ref, sems.at[0])
-        out_copies = [load(mixed_hbm, mixed_ref, more_sems.at[1])]
-        out_copies += load_blocks((g0, g1, g2, g3, g4, g5, g6, g7), grad_ref, sems.at[1])
+        copies += load_blocks((n0, n1, n2, n3, n4, n5, n6, n7), normed_ref, sems)
         wait_all(copies)
         for r in range(PLANE):
             part = outer(normed_ref[:, r * 128 : (r + 1) * 128], joint_grad_ref[...])
@@ -940,26 +966,39 @@
                     def _():
                         ref[r] = part[p]
 
-        wait_all(out_copies)
-        part = outer(mixed_ref[...], grad_ref[...])
-        out_ref[...] = part.astype(jnp.bfloat16).reshape(DEPTH, own // DEPTH, features)
-
     low = jnp.bfloat16
     return kernel_call(
         kernel,
-        [ANYWHERE] * 18,
-        [sds((PLANE, 32, width), low)] * 4 + [sds((DEPTH, own // DEPTH, features), low)],
+        [ANYWHERE] * 9,
+        [sds((PLANE, 32, width), low)] * 4,
         [
             pltpu.VMEM((rows, features), low),
             pltpu.VMEM((rows, width), low),
-            pltpu.VMEM((rows, own), low),
-            pltpu.VMEM((rows, features), low),
-            pltpu.SemaphoreType.DMA((2, PLANE)),
-            pltpu.SemaphoreType.DMA((2,)),
+            pltpu.SemaphoreType.DMA((PLANE,)),
+            pltpu.SemaphoreType.DMA((1,)),
         ],
-        2 * rows * features * (width + own),
-        (*blocks, joint_grad, mixed, *grads),
-    )
+        2 * rows * features * width,
+        (*blocks, joint_grad),
+    )
+
+
+def out_weights(mixed, grads):
+    count, features = grads[0].shape
+    rows, own = mixed.shape
+
+    def kernel(mixed_ref, g0, g1, g2, g3, g4, g5, g6, g7, out_ref, grad_ref, sems):
+        wait_all(load_blocks((g0, g1, g2, g3, g4, g5, g6, g7), grad_ref, sems))
+        part = outer(mixed_ref[...], grad_ref[...])
+        out_ref[...] = part.astype(jnp.bfloat16).reshape(DEPTH, own // DEPTH, features)
+
+    return kernel_call(
+        kernel,
+        [LOCAL] + [ANYWHERE] * 8,
+        [sds((DEPTH, own // DEPTH, features), jnp.bfloat16)],
+        [pltpu.VMEM((rows, features), jnp.bfloat16), pltpu.SemaphoreType.DMA((PLANE,))],
+        2 * rows * features * own,
+        (mixed, *grads),
+    )[0]
 
 
 def body_planes(
@@ -1004,95 +1043,93 @@
         start += item.shape[0]
     packed = packed.reshape(-1, 128)
     packs = [packed] + [over_z(packed, step) for step in (1, 2, 3)]
-    tokens = to_home(tokens)
-
-    weights = after((qkv_weight, out_weight, up_weight, down_weight), tokens, packs)
-    qkv_own, out_own, up_own, down_own = own_eighths(*weights)
-    vectors, normed = first_norm(tokens, packs)
-    normed_blocks = gather_plane(normed)
+    moved = to_home(jnp.concatenate([tokens, cotangent], 0))
+    own_length = jnp.sum(jnp.where(jnp.arange(lengths.shape[0]) == assign[0], lengths, 0))
+    length = to_home(jnp.full((8, 128), own_length.astype(jnp.float32)))
+    lens = (length, over_rep(length, 4))
+
+    weights = after((qkv_weight, out_weight, up_weight, down_weight), moved, packs, lens)
+    qkv_own, out_own, wide_own = own_eighths(*weights)
+    vectors, normed, tokens = first_norm(moved, packs)
     qkv_own = after(qkv_own, normed)
     qkv_parts = [qkv_own] + [over_z(qkv_own, step) for step in (1, 2, 3)]
-    out_own = after(out_own, qkv_parts)
-    out_part = jnp.where(z == rep >> 1, out_own, jnp.zeros_like(out_own))
-    for step in (1, 2, 3):
-        out_part = out_part + over_all(
-            out_own,
+    normed_blocks = gather_plane(normed, qkv_parts)
+    cotangent = after(moved, normed_blocks)[row_count:]
+    position = quarter_of(rep) * row_count + jnp.arange(row_count)
+    valid = position.astype(jnp.float32) < length[0, 0]
+    branch_grad = jnp.where(valid[:, None], cotangent, jnp.zeros_like(cotangent))
+    branch_near = [over_rep(branch_grad, flip) for flip in (1, 2, 4, 6)]
+    heads = (2 * rep + jnp.arange(2)).astype(jnp.float32)
+    slopes = jnp.exp2(-8.0 * (heads + 1.0) / HEADS)
+    joint, mixed = attention_forward(lens, slopes, normed_blocks, qkv_parts, vectors)
+    out_moved = [
+        over_all(
+            after(out_own, qkv_parts),
             lambda i, step=step: (
                 i - i % DEPTH + (i % DEPTH + step) % DEPTH if i % DEPTH == i // 8 else None
             ),
         )
-    up_own = after(up_own, out_part)
-    up_parts = [up_own] + [over_z(up_own, step) for step in (1, 2, 3)]
-
-    own_length = jnp.sum(jnp.where(jnp.arange(lengths.shape[0]) == assign[0], lengths, 0))
-    ones = jnp.ones((16, feature_count), jnp.float32)
-    length_rows = jnp.where(
-        jnp.arange(16)[:, None] == 0, ones * (own_length // 16), ones * (own_length % 16)
-    )
-    moved = to_home(
-        after(jnp.concatenate([cotangent, length_rows.astype(jnp.bfloat16)], 0), normed)
-    )
-    cotangent = moved[:row_count]
-    length_parts = moved[row_count : row_count + 2, 0].astype(jnp.int32)
-    seq_length = 16 * length_parts[0] + length_parts[1]
-    other_length = over_rep(seq_length.astype(jnp.float32).reshape(1, 1), 4)
-    lens = jnp.stack([seq_length, other_length.astype(jnp.int32)[0, 0]])
-    heads = (2 * rep + jnp.arange(2)).astype(jnp.float32)
-    slopes = jnp.exp2(-8.0 * (heads + 1.0) / HEADS)
-    position = quarter_of(rep) * row_count + jnp.arange(row_count)
-    branch_grad = jnp.where((position < seq_length)[:, None], cotangent, jnp.zeros_like(cotangent))
-
-    branch_grad_plane = lax.all_gather(branch_grad, "rep", axis=0, tiled=False)
-    down_all = lax.all_gather(after(down_own, branch_grad), "shard", axis=0, tiled=True)
-    joint, mixed, keep, give = attention_forward(
-        lens, slopes, normed_blocks, qkv_parts, out_part, vectors
-    )
+        for step in (1, 2, 3)
+    ]
+    out_part = jnp.where(z == rep >> 1, out_own, jnp.zeros_like(out_own))
+    out_moved, branch_near = after((out_moved, branch_near), mixed)
+    for piece in out_moved:
+        out_part = out_part + piece
+    branch_blocks = [branch_grad, branch_near[0]]
+    for block in branch_near[1:]:
+        branch_blocks += [block, over_rep(block, 1)]
+    wide_all = lax.all_gather(after(wide_own, out_part), "shard", axis=0, tiled=True)
+    keep, give = out_projection(mixed, out_part)
     parts = send_parts(add_halves(keep, over_rep(give, 1)))
-    middle, normed_two = second_norm(tokens, vectors, after(parts, up_parts))
+    middle, normed_two = second_norm(tokens, vectors, parts)
     normed_two_blocks = gather_plane(normed_two)
     active, hidden_grad, hidden_sums, branch_keep, branch_give, keep, give = feed_forward(
-        normed_two_blocks, branch_grad_plane, up_parts, down_all, vectors
+        normed_two_blocks, branch_blocks, wide_all, vectors
     )
     received = over_rep(give, 1)
+    parts = send_parts(add_halves(keep, received))
     branch_received = over_rep(after(branch_give, received), 1)
-    halves = add_halves(keep, received)
-    up_slice, down_slice = feed_forward_weights(
-        normed_two_blocks, after(hidden_grad, halves), active, branch_grad_plane
-    )
-    up_summed = scattered_over_z(up_slice)
-    down_summed = scattered_over_z(down_slice)
-    parts = after(send_parts(halves), up_slice, branch_received)
+    branch_halves = add_halves(branch_keep, after(branch_received, parts[0]))
+    wide_slice = feed_forward_weights(
+        normed_two_blocks, after(hidden_grad, parts[0]), active, branch_blocks
+    )
     middle_grad, attended_grad, second_sums = second_norm_back(
-        lens, vectors, middle, cotangent, parts
-    )
+        vectors, middle, branch_grad, after(parts, wide_slice, branch_halves)
+    )
+    wide_summed = scattered_over_z(after(wide_slice, attended_grad))
     attended_blocks = gather_plane(attended_grad)
-    branch_halves = add_halves(branch_keep, after(branch_received, attended_grad))
+    branch_own, *branch_rest = send_parts(branch_halves)
     joint_grad, joint_sums, keep, give = attention_backward(
-        after(lens, branch_halves), slopes, attended_blocks, joint, qkv_parts, out_part
-    )
-    branch_own, *branch_rest = send_parts(branch_halves)
-    received = after(over_rep(give, 1), branch_rest)
-    halves = add_halves(keep, received)
-    *qkv_slices, out_slice = attention_weights(
-        normed_blocks, after(joint_grad, halves), mixed, attended_blocks
-    )
-    parts = after(send_parts(halves), qkv_slices)
-    tokens_grad, first_sums = first_norm_back(tokens, vectors, middle_grad, parts)
-    tokens_grad = from_home(tokens_grad).astype(jnp.float32)
+        lens, slopes, attended_blocks, joint, qkv_parts, out_part
+    )
+    received = over_rep(after(give, branch_rest), 1)
+    qkv_slices = qkv_weights(normed_blocks, joint_grad)
+    parts = send_parts(add_halves(keep, after(received, qkv_slices)))
+    qkv_slices = [qkv_slices[0]] + [over_z(qkv_slices[step], step) for step in (1, 2, 3)]
+    out_slice = out_weights(after(mixed, parts[0]), attended_blocks)
+    tokens_grad, first_sums = first_norm_back(
+        tokens, vectors, middle_grad, after(parts, out_slice, qkv_slices)
+    )
+    tokens_grad = from_home(tokens_grad)
+    units = wide_summed.shape[1] - feature_count // 2
+    wide_summed, qkv_slices = after((wide_summed, qkv_slices), first_sums)
+    up_summed = wide_summed[:, :units].reshape(PLANE, -1, units)
     qkv_summed = qkv_slices[0].astype(jnp.float32)
     for step in (1, 2, 3):
-        qkv_summed = qkv_summed + over_z(qkv_slices[step], step).astype(jnp.float32)
-    qkv_grad = columns_to_rows(qkv_summed.astype(jnp.bfloat16))
+        qkv_summed = qkv_summed + qkv_slices[step].astype(jnp.float32)
+    both = jnp.concatenate([up_summed, qkv_summed.astype(jnp.bfloat16)], 2)
+    arrived = lax.all_to_all(both, "rep", 0, 0, tiled=True)
+    up_grad = spread_columns(arrived[:, :, :units])
+    qkv_grad = spread_columns(arrived[:, :, units:])
     out_grad = scattered_over_z(out_slice).astype(jnp.float32)
-
+    down_summed = jnp.concatenate([wide_summed[:128, units:], wide_summed[128:, units:]], 1)
+    down_grad = over_all(
+        down_summed,
+        lambda i: (2 * (i % DEPTH) + i // 16) * DEPTH + (i // DEPTH) % DEPTH,
+    )
     branch = branch_own + sum(part.astype(jnp.float32) for part in branch_rest)
     layer_low = (middle + branch + vectors[5:6]).astype(jnp.bfloat16)
-    layer_out = from_home(after(layer_low, halves)).astype(jnp.float32)
-    down_grad = over_all(
-        after(down_summed, halves),
-        lambda i: (2 * (i % DEPTH) + i // 16) * DEPTH + (i // DEPTH) % DEPTH,
-    ).astype(jnp.float32)
-    up_grad = columns_to_rows(after(up_summed, halves))
+    layer_out = from_home(after(layer_low, parts[0]))
 
     at_rep = (jnp.arange(PLANE) == rep)[None, :, None]
 
@@ -1113,7 +1150,11 @@
     small_packed = jnp.concatenate(
         [g.reshape(devices, g.shape[0] // devices) for g in small_grads], 1
     ).astype(jnp.bfloat16)
-    small_arrived = lax.all_to_all(small_packed, ("rep", "shard"), 0, 0, tiled=True)
+    small_arrived = lax.all_to_all(after(small_packed, arrived), ("rep", "shard"), 0, 0, tiled=True)
+    layer_out, tokens_grad, down_grad = (
+        moved_back.astype(jnp.float32)
+        for moved_back in after((layer_out, tokens_grad, down_grad), small_arrived)
+    )
     small_sums = jnp.sum(small_arrived.astype(jnp.float32), 0)
     sums = []
     start = 0

time: 335 us -> 297 us (0.89)
  starting transfers between devices: 117 us -> 79.7 us
  Pallas kernels: 76.7 us -> 81.7 us
  between operations: 20 us -> 16.1 us
    ppermute x12 -> x9, starting transfers between devices: 35.5 us -> 21.1 us  [over_z(): lax.ppermute(value, 'shard', [(i, (i + step) % DEPTH) for i in range(DEPT...]
    ppermute x38 -> x45, waiting for transfers between devices: 54.9 us -> 42.3 us  [over_rep(): return lax.ppermute(value, 'rep', [(i, i ^ flip) for i in range(PLANE)])]
    ppermute x8, starting transfers between devices: 22.6 us -> 10.6 us  [over_all(): return lax.ppermute(value, ('rep', 'shard'), pairs)]
    ppermute x38 -> x45, starting transfers between devices: 40 us -> 31 us  [over_rep(): return lax.ppermute(value, 'rep', [(i, i ^ flip) for i in range(PLANE)])]
    pallas_call x14 -> x16, Pallas kernels: 76.7 us -> 81.7 us  [kernel_call(): pl.pallas_call(kernel, out_shape=outs, in_specs=ins, out_specs=[LOCAL] *...]
    ppermute x8, waiting for transfers between devices: 3.71 us -> 7.1 us  [over_all(): return lax.ppermute(value, ('rep', 'shard'), pairs)]
    ppermute x12 -> x9, waiting for transfers between devices: 21.4 us -> 23.8 us  [over_z(): lax.ppermute(value, 'shard', [(i, (i + step) % DEPTH) for i in range(DEPT...]
    all_to_all x3 -> x2, starting transfers between devices: 18 us -> 16.6 us  [the longest x1 10.6 us: body_planes(): arrived = lax.all_to_all(both, 'rep', 0, 0, tiled=True)]
  transfers between devices with their start and end apart: 66 -> 67, of which waited for: 20 -> 25; matrix products, arithmetic and copies ran while one was open for 5% -> 6% of each run, Pallas kernels for 17% -> 21%
where the time goes in v4:
time: 297 us; the launch traced here: 296 us
  waiting for transfers between devices  87.5 us (29%)
  Pallas kernels  81.7 us (28%)
  starting transfers between devices  79.7 us (27%)
  local copies, waits for them, and re-layouts  17.6 us (6%)
  between operations  16.1 us (5%)
  other arithmetic  13.1 us (4%)
    pallas_call x16, Pallas kernels, kernel_call(): pl.pallas_call(kernel, out_shape=outs, in_specs=ins, out_specs=[LOCAL] *...  81.7 us
    ppermute x45, waiting for transfers between devices, over_rep(): return lax.ppermute(value, 'rep', [(i, i ^ flip) for i in range(PLANE)])  42.3 us
    ppermute x45, starting transfers between devices, over_rep(): return lax.ppermute(value, 'rep', [(i, i ^ flip) for i in range(PLANE)])  31 us
    ppermute x9, waiting for transfers between devices, over_z(): lax.ppermute(value, 'shard', [(i, (i + step) % DEPTH) for i in range(DEPT...  23.8 us
    ppermute x9, starting transfers between devices, over_z(): lax.ppermute(value, 'shard', [(i, (i + step) % DEPTH) for i in range(DEPT...  21.1 us
    unnamed x128, local copies, waits for them, and re-layouts  11.3 us
    all_to_all x1, starting transfers between devices, body_planes(): arrived = lax.all_to_all(both, 'rep', 0, 0, tiled=True)  10.6 us
    ppermute x8, starting transfers between devices, over_all(): return lax.ppermute(value, ('rep', 'shard'), pairs)  10.6 us
  transfers between devices with their start and end apart: 67, of which 25 were waited for; matrix products, arithmetic and copies ran while one was open for 6% of the time, Pallas kernels for 21%

profile of v4, /device:TPU:0, one launch (start us, length us, event | category | flops | bytes accessed | tf_op | source)
XLA Modules:
  0.0 295.7 jit_solution(16480453948218109621)
XLA Ops:
  13.1 8.4 %collective-permute-start.1 = (bf16[24,128]{1,0:T(8,128)(2,1)S(1)}, bf16[24,128]{1,0:T(8,128)(2,1)S(1)}, u32[]{:S(2)}, u32[]{:S(2)}) collective-permute-start(bf16[24,128]{1,0:T(8,128)(2,1)S(1)} %add_bitcast_fusion.p0), channel_id=1, source_target_pairs={{0,1},{1,2},{2,3},{3,0},{4,5},{5,6},{6,7},{7,4},{8,9},{9,10},{10,1... | collective-permute-start | bytes 18440 | tf_op jit(solution)/shard_map/ppermute | solution.py:291
  21.5 4.1 %collective-permute-start.2 = (bf16[24,128]{1,0:T(8,128)(2,1)S(1)}, bf16[24,128]{1,0:T(8,128)(2,1)S(1)}, u32[]{:S(2)}, u32[]{:S(2)}) collective-permute-start(bf16[24,128]{1,0:T(8,128)(2,1)S(1)} %add_bitcast_fusion.p0), channel_id=1, source_target_pairs={{0,2},{1,3},{2,0},{3,1},{4,6},{5,7},{6,4},{7,5},{8,10},{9,11},{10,... | collective-permute-start | bytes 18440 | tf_op jit(solution)/shard_map/ppermute | solution.py:291
  28.6 4.5 %collective-permute-done.3.p3 = bf16[24,128]{1,0:T(8,128)(2,1)S(1)} collective-permute-done((bf16[24,128]{1,0:T(8,128)(2,1)S(1)}, bf16[24,128]{1,0:T(8,128)(2,1)S(1)}, u32[]{:S(2)}, u32[]{:S(2)}) %collective-permute-start.3) | collective-permute-done | bytes 6176 | tf_op jit(solution)/shard_map/ppermute | solution.py:291
  48.7 7.6 %collective-permute-done.11.w2 = bf16[256,384]{1,0:T(8,128)(2,1)S(1)} collective-permute-done((bf16[256,384]{1,0:T(8,128)(2,1)}, bf16[256,384]{1,0:T(8,128)(2,1)S(1)}, u32[]{:S(2)}, u32[]{:S(2)}) %collective-permute-start.11) | collective-permute-done | bytes 196640 | tf_op jit(solution)/shard_map/ppermute | solution.py:291
  60.4 3.7 %collective-permute-start.16 = (bf16[128,1024]{1,0:T(8,128)(2,1)}, bf16[128,1024]{1,0:T(8,128)(2,1)S(1)}, u32[]{:S(2)}, u32[]{:S(2)}) collective-permute-start(bf16[128,1024]{1,0:T(8,128)(2,1)} %get-tuple-element.125), channel_id=1, source_target_pairs={{0,1},{4,5},{9,10},{13,14},{18,19},{22,23},{27,24},{31,28}} | collective-permute-start | bytes 786440 | tf_op jit(solution)/shard_map/ppermute | solution.py:296
  71.0 5.6 %collective-permute-done.17 = bf16[128,1024]{1,0:T(8,128)(2,1)S(1)} collective-permute-done((bf16[128,1024]{1,0:T(8,128)(2,1)}, bf16[128,1024]{1,0:T(8,128)(2,1)S(1)}, u32[]{:S(2)}, u32[]{:S(2)}) %collective-permute-start.17) | collective-permute-done | bytes 262176 | tf_op jit(solution)/shard_map/ppermute | solution.py:296
  77.2 12.2 %shard_map.265 = (bf16[1024,384]{1,0:T(8,128)(2,1)}, bf16[1024,128]{1,0:T(8,128)(2,1)}) custom-call(f32[8,128]{1,0:T(8,128)} %copy-done.60, f32[8,128]{1,0:T(8,128)} %copy-done.61, f32[2]{0:T(128)} %multiply_exponential_fusion.slopes_ref, bf16[128,1024]{1,0:T(8,128)(2,1)} %get-tuple-element.113.n0, bf16[128,1024]{1,0:T(8,128)(2,1)} %copy-done.46, ...), custom_call_target="tpu_custom_call" | custom-call | flops 1342177280 | bytes 8388608 | tf_op jit(solution)/shard_map/pallas_call | solution.py:472
  100.2 3.5 %collective-permute-start.25 = (bf16[128,1024]{1,0:T(8,128)(2,1)}, bf16[128,1024]{1,0:T(8,128)(2,1)S(1)}, u32[]{:S(2)}, u32[]{:S(2)}) collective-permute-start(bf16[128,1024]{1,0:T(8,128)(2,1)} %get-tuple-element.134), channel_id=1, source_target_pairs={{0,16},{4,20},{8,24},{12,28},{16,0},{20,4},{24,8},{28,12},{1,17},{... | collective-permute-start | bytes 786440 | tf_op jit(solution)/shard_map/ppermute | solution.py:287
  103.6 5.9 %collective-permute-done.24.two = bf16[128,1024]{1,0:T(8,128)(2,1)S(1)} collective-permute-done((bf16[128,1024]{1,0:T(8,128)(2,1)}, bf16[128,1024]{1,0:T(8,128)(2,1)S(1)}, u32[]{:S(2)}, u32[]{:S(2)}) %collective-permute-start.24) | collective-permute-done | bytes 262176 | tf_op jit(solution)/shard_map/ppermute | solution.py:287
  109.5 6.3 %collective-permute-done.25.four = bf16[128,1024]{1,0:T(8,128)(2,1)S(1)} collective-permute-done((bf16[128,1024]{1,0:T(8,128)(2,1)}, bf16[128,1024]{1,0:T(8,128)(2,1)S(1)}, u32[]{:S(2)}, u32[]{:S(2)}) %collective-permute-start.25) | collective-permute-done | bytes 262176 | tf_op jit(solution)/shard_map/ppermute | solution.py:287
  123.0 5.4 %collective-permute-done.28.n2 = bf16[128,1024]{1,0:T(8,128)(2,1)S(1)} collective-permute-done((bf16[128,1024]{1,0:T(8,128)(2,1)}, bf16[128,1024]{1,0:T(8,128)(2,1)S(1)}, u32[]{:S(2)}, u32[]{:S(2)}) %collective-permute-start.28) | collective-permute-done | bytes 262176 | tf_op jit(solution)/shard_map/ppermute | solution.py:287
  128.5 5.1 %collective-permute-done.29.n4 = bf16[128,1024]{1,0:T(8,128)(2,1)S(1)} collective-permute-done((bf16[128,1024]{1,0:T(8,128)(2,1)}, bf16[128,1024]{1,0:T(8,128)(2,1)S(1)}, u32[]{:S(2)}, u32[]{:S(2)}) %collective-permute-start.29) | collective-permute-done | bytes 262176 | tf_op jit(solution)/shard_map/ppermute | solution.py:287
  139.2 10.8 %shard_map.269 = (bf16[1024,512]{1,0:T(8,128)(2,1)}, bf16[1024,512]{1,0:T(8,128)(2,1)}, f32[1,512]{1,0:T(1,128)}, bf16[2,2,128,1024]{3,2,1,0:T(8,128)(2,1)}, bf1...) custom-call(bf16[128,1024]{1,0:T(8,128)(2,1)} %get-tuple-element.137.n0, ...), custom_call_target="tpu_custom_call" | custom-call | flops 4294967296 | bytes 8388608 | tf_op jit(solution)/shard_map/pallas_call | solution.py:472
  160.1 6.4 %shard_map.272 = bf16[4,256,1024]{2,1,0:T(8,128)(2,1)} custom-call(bf16[128,1024]{1,0:T(8,128)(2,1)} %get-tuple-element.137.n0, bf16[128,1024]{1,0:T(8,128)(2,1)} %copy-done.27, bf16[128,1024]{1,0:T(8,128)(2,1)} %copy-done.21, bf16[128,1024]{1,0:T(8,128)(2,1)} %copy-done.28, bf16[128,1024]{1,0:T(8,128)(2,1)} %copy-done.22, bf16[128,1024]{1,0:T(8,128)(2,1)} %copy-done.29, ...), custom_call_target="tpu_custom_call" | custom-call | flops 2147483648 | bytes 8388608 | tf_op jit(solution)/shard_map/pallas_call | solution.py:472
  180.2 5.7 %collective-permute-done.46.g2 = bf16[128,1024]{1,0:T(8,128)(2,1)S(1)} collective-permute-done((bf16[128,1024]{1,0:T(8,128)(2,1)S(1)}, bf16[128,1024]{1,0:T(8,128)(2,1)S(1)}, u32[]{:S(2)}, u32[]{:S(2)}) %collective-permute-start.46) | collective-permute-done | bytes 262176 | tf_op jit(solution)/shard_map/ppermute | solution.py:287
  185.9 4.7 %collective-permute-done.47.g4 = bf16[128,1024]{1,0:T(8,128)(2,1)S(1)} collective-permute-done((bf16[128,1024]{1,0:T(8,128)(2,1)S(1)}, bf16[128,1024]{1,0:T(8,128)(2,1)S(1)}, u32[]{:S(2)}, u32[]{:S(2)}) %collective-permute-start.47) | collective-permute-done | bytes 262176 | tf_op jit(solution)/shard_map/ppermute | solution.py:287
  195.6 16.5 %shard_map.274 = (bf16[1024,384]{1,0:T(8,128)(2,1)}, f32[1,384]{1,0:T(1,128)}, bf16[2,2,128,1024]{3,2,1,0:T(8,128)(2,1)}, bf16[2,2,128,1024]{3,2,1,0:T(8,128)(2,1)}) custom-call(f32[8,128]{1,0:T(8,128)} %copy-done.60, f32[8,128]{1,0:T(8,128)} %copy-done.61, f32[2]{0:T(128)} %multiply_exponential_fusion.slopes_ref, bf16[128,1024]{1,0:T(8,128)(2,1)} %get-tuple-element.168.g0, ...), custom_call_target="tpu_custom_call" | custom-call | flops 2415919104 | bytes 8388608 | tf_op jit(solution)/shard_map/pallas_call | solution.py:472
  213.8 5.8 %shard_map.275 = (bf16[8,32,384]{2,1,0:T(8,128)(2,1)}, bf16[8,32,384]{2,1,0:T(8,128)(2,1)}, bf16[8,32,384]{2,1,0:T(8,128)(2,1)}, bf16[8,32,384]{2,1,0:T(8,128)(2,1)}) custom-call(bf16[128,1024]{1,0:T(8,128)(2,1)} %get-tuple-element.113.n0, bf16[128,1024]{1,0:T(8,128)(2,1)} %copy-done.46, bf16[128,1024]{1,0:T(8,128)(2,1)} %copy-done.43, ...), custom_call_target="tpu_custom_call" | custom-call | flops 805306368 | bytes 8388608 | tf_op jit(solution)/shard_map/pallas_call | solution.py:472
  229.2 3.7 %shard_map.277 = bf16[4,32,1024]{2,1,0:T(8,128)(2,1)} custom-call(bf16[1024,128]{1,0:T(8,128)(2,1)} %get-tuple-element.188.mixed_ref, bf16[128,1024]{1,0:T(8,128)(2,1)} %get-tuple-element.168.g0, bf16[128,1024]{1,0:T(8,128)(2,1)} %copy-done.17, bf16[128,1024]{1,0:T(8,128)(2,1)} %copy-done.13, bf16[128,1024]{1,0:T(8,128)(2,1)} %copy-done.18, ...), custom_call_target="tpu_custom_call" | custom-call | flops 268435456 | bytes 8388608 | tf_op jit(solution)/shard_map/pallas_call | solution.py:472
  237.6 4.1 %collective-permute-done.59 = bf16[8,32,384]{2,1,0:T(8,128)(2,1)S(1)} collective-permute-done((bf16[8,32,384]{2,1,0:T(8,128)(2,1)S(1)}, bf16[8,32,384]{2,1,0:T(8,128)(2,1)S(1)}, u32[]{:S(2)}, u32[]{:S(2)}) %collective-permute-start.59) | collective-permute-done | bytes 196640 | tf_op jit(solution)/shard_map/ppermute | solution.py:291
  249.9 10.6 %all-to-all-start = ((bf16[8,32,896]{2,1,0:T(8,128)(2,1)}), bf16[8,32,896]{2,1,0:T(8,128)(2,1)S(1)}, u32[]{:S(2)}, u32[]{:S(2)}) async-start(bf16[8,32,896]{2,1,0:T(8,128)(2,1)} %pad_maximum_fusion.1), calls=%async_computation.1 | async-start | bytes 917504 | tf_op jit(solution)/shard_map/all_to_all | solution.py:1121
  262.8 6.8 %all-to-all-done = bf16[8,32,896]{2,1,0:T(8,128)(2,1)S(1)} async-done(((bf16[8,32,896]{2,1,0:T(8,128)(2,1)}), bf16[8,32,896]{2,1,0:T(8,128)(2,1)S(1)}, u32[]{:S(2)}, u32[]{:S(2)}) %all-to-all-start) | async-done | bytes 458784 | tf_op jit(solution)/shard_map/all_to_all | solution.py:1121
  271.5 6.0 %all-to-all-start.1 = ((bf16[32,2,192]{2,1,0:T(2,128)(2,1)}), bf16[32,2,192]{2,1,0:T(2,128)(2,1)S(1)}, u32[]{:S(2)}, u32[]{:S(2)}) async-start(bf16[32,2,192]{2,1,0:T(2,128)(2,1)} %reshape.87), calls=%async_computation.2 | async-start | bytes 65536 | tf_op jit(solution)/shard_map/all_to_all | solution.py:1153
  280.4 4.4 %all-to-all-done.1 = bf16[32,2,192]{2,1,0:T(2,128)(2,1)S(1)} async-done(((bf16[32,2,192]{2,1,0:T(2,128)(2,1)}), bf16[32,2,192]{2,1,0:T(2,128)(2,1)S(1)}, u32[]{:S(2)}, u32[]{:S(2)}) %all-to-all-start.1) | async-done | bytes 24608 | tf_op jit(solution)/shard_map/all_to_all | solution.py:1153
  (308 shorter events, 121.9 us)
Async XLA Ops:
  7.2 132.0 %all-gather.2.cloned.1.call-start = ((), (), s32[]{:S(2)}) async-start(), calls=%async_computation.4 | async-start | bytes 2621440 | tf_op jit(solution)/shard_map/all_gather | solution.py:1081
  8.3 24.9 %collective-permute-start = (bf16[256,1024]{1,0:T(8,128)(2,1)S(1)}, bf16[256,1024]{1,0:T(8,128)(2,1)S(1)}, u32[]{:S(2)}, u32[]{:S(2)}) collective-permute-start(bf16[256,1024]{1,0:T(8,128)(2,1)S(1)} %pad_maximum_fusion), channel_id=1, source_target_pairs={{0,0},{1,8},{2,4},{3,12},{4,2},{5,10},{6,6},{7,14},{8,16},{9,24},{... | collective-permute-start | bytes 1572872 | tf_op jit(solution)/shard_map/ppermute | solution.py:296
  13.1 15.5 %collective-permute-start.1 = (bf16[24,128]{1,0:T(8,128)(2,1)S(1)}, bf16[24,128]{1,0:T(8,128)(2,1)S(1)}, u32[]{:S(2)}, u32[]{:S(2)}) collective-permute-start(bf16[24,128]{1,0:T(8,128)(2,1)S(1)} %add_bitcast_fusion.p0), channel_id=1, source_target_pairs={{0,1},{1,2},{2,3},{3,0},{4,5},{5,6},{6,7},{7,4},{8,9},{9,10},{10,1... | collective-permute-start | bytes 18440 | tf_op jit(solution)/shard_map/ppermute | solution.py:291
  40.9 15.3 %collective-permute-start.11 = (bf16[256,384]{1,0:T(8,128)(2,1)}, bf16[256,384]{1,0:T(8,128)(2,1)S(1)}, u32[]{:S(2)}, u32[]{:S(2)}) collective-permute-start(bf16[256,384]{1,0:T(8,128)(2,1)} %get-tuple-element.119.w0), channel_id=1, source_target_pairs={{0,2},{1,3},{2,0},{3,1},{4,6},{5,7},{6,4},{7,5},{8,10},{9,11},{10,... | collective-permute-start | bytes 589832 | tf_op jit(solution)/shard_map/ppermute | solution.py:291
  41.0 18.2 %collective-permute-start.7 = (bf16[128,1024]{1,0:T(8,128)(2,1)}, bf16[128,1024]{1,0:T(8,128)(2,1)S(1)}, u32[]{:S(2)}, u32[]{:S(2)}) collective-permute-start(bf16[128,1024]{1,0:T(8,128)(2,1)} %get-tuple-element.113.n0), channel_id=1, source_target_pairs={{0,8},{4,12},{8,0},{12,4},{16,24},{20,28},{24,16},{28,20},{1,9},{5... | collective-permute-start | bytes 786440 | tf_op jit(solution)/shard_map/ppermute | solution.py:287
  43.1 16.1 %collective-permute-start.8 = (bf16[128,1024]{1,0:T(8,128)(2,1)}, bf16[128,1024]{1,0:T(8,128)(2,1)S(1)}, u32[]{:S(2)}, u32[]{:S(2)}) collective-permute-start(bf16[128,1024]{1,0:T(8,128)(2,1)} %get-tuple-element.113.n0), channel_id=1, source_target_pairs={{0,16},{4,20},{8,24},{12,28},{16,0},{20,4},{24,8},{28,12},{1,17},{... | collective-permute-start | bytes 786440 | tf_op jit(solution)/shard_map/ppermute | solution.py:287
  44.9 14.3 %collective-permute-start.9 = (bf16[128,1024]{1,0:T(8,128)(2,1)}, bf16[128,1024]{1,0:T(8,128)(2,1)S(1)}, u32[]{:S(2)}, u32[]{:S(2)}) collective-permute-start(bf16[128,1024]{1,0:T(8,128)(2,1)} %get-tuple-element.113.n0), channel_id=1, source_target_pairs={{0,24},{4,28},{8,16},{12,20},{16,8},{20,12},{24,0},{28,4},{1,25},{... | collective-permute-start | bytes 786440 | tf_op jit(solution)/shard_map/ppermute | solution.py:287
  66.1 23.3 %collective-permute-start.18 = (bf16[128,1024]{1,0:T(8,128)(2,1)}, bf16[128,1024]{1,0:T(8,128)(2,1)S(1)}, u32[]{:S(2)}, u32[]{:S(2)}) collective-permute-start(bf16[128,1024]{1,0:T(8,128)(2,1)} %get-tuple-element.125), channel_id=1, source_target_pairs={{0,3},{4,7},{9,8},{13,12},{18,17},{22,21},{27,26},{31,30}} | collective-permute-start | bytes 786440 | tf_op jit(solution)/shard_map/ppermute | solution.py:296
  69.3 20.1 %collective-permute-start.19 = (bf16[128,1024]{1,0:T(8,128)(2,1)S(1)}, bf16[128,1024]{1,0:T(8,128)(2,1)S(1)}, u32[]{:S(2)}, u32[]{:S(2)}) collective-permute-start(bf16[128,1024]{1,0:T(8,128)(2,1)S(1)} %slice_select_fusion.g0.seed_ref), channel_id=1, source_target_pairs={{0,4},{4,0},{8,12},{12,8},{16,20},{20,16},{24,28},{28,24},{1,5},{5... | collective-permute-start | bytes 786440 | tf_op jit(solution)/shard_map/ppermute | solution.py:287
  69.5 19.9 %collective-permute-start.20 = (bf16[128,1024]{1,0:T(8,128)(2,1)S(1)}, bf16[128,1024]{1,0:T(8,128)(2,1)S(1)}, u32[]{:S(2)}, u32[]{:S(2)}) collective-permute-start(bf16[128,1024]{1,0:T(8,128)(2,1)S(1)} %slice_select_fusion.g0.seed_ref), channel_id=1, source_target_pairs={{0,8},{4,12},{8,0},{12,4},{16,24},{20,28},{24,16},{28,20},{1,9},{5... | collective-permute-start | bytes 786440 | tf_op jit(solution)/shard_map/ppermute | solution.py:287
  71.0 18.5 %collective-permute-start.21 = (bf16[128,1024]{1,0:T(8,128)(2,1)S(1)}, bf16[128,1024]{1,0:T(8,128)(2,1)S(1)}, u32[]{:S(2)}, u32[]{:S(2)}) collective-permute-start(bf16[128,1024]{1,0:T(8,128)(2,1)S(1)} %slice_select_fusion.g0.seed_ref), channel_id=1, source_target_pairs={{0,16},{4,20},{8,24},{12,28},{16,0},{20,4},{24,8},{28,12},{1,17},{... | collective-permute-start | bytes 786440 | tf_op jit(solution)/shard_map/ppermute | solution.py:287
  90.4 157.5 %reduce-scatter.3.cloned.1.call-start = ((), (), s32[]{:S(2)}) async-start(), calls=%async_computation.5 | async-start | bytes 2621440 | tf_op jit(solution)/shard_map/reduce_scatter | solution.py:367
  100.2 15.6 %collective-permute-start.25 = (bf16[128,1024]{1,0:T(8,128)(2,1)}, bf16[128,1024]{1,0:T(8,128)(2,1)S(1)}, u32[]{:S(2)}, u32[]{:S(2)}) collective-permute-start(bf16[128,1024]{1,0:T(8,128)(2,1)} %get-tuple-element.134), channel_id=1, source_target_pairs={{0,16},{4,20},{8,24},{12,28},{16,0},{20,4},{24,8},{28,12},{1,17},{... | collective-permute-start | bytes 786440 | tf_op jit(solution)/shard_map/ppermute | solution.py:287
  175.7 84.8 %reduce-scatter.5.cloned.1.call-start = ((), (), s32[]{:S(2)}) async-start(), calls=%async_computation.6 | async-start | bytes 327680 | tf_op jit(solution)/shard_map/reduce_scatter | solution.py:367
  191.3 20.9 %collective-permute-start.41 = (bf16[128,1024]{1,0:T(8,128)(2,1)}, bf16[128,1024]{1,0:T(8,128)(2,1)S(1)}, u32[]{:S(2)}, u32[]{:S(2)}) collective-permute-start(bf16[128,1024]{1,0:T(8,128)(2,1)} %get-tuple-element.157), channel_id=1, source_target_pairs={{0,24},{4,28},{8,16},{12,20},{16,8},{20,12},{24,0},{28,4},{1,25},{... | collective-permute-start | bytes 786440 | tf_op jit(solution)/shard_map/ppermute | solution.py:287
  192.3 19.8 %collective-permute-start.40 = (bf16[128,1024]{1,0:T(8,128)(2,1)}, bf16[128,1024]{1,0:T(8,128)(2,1)S(1)}, u32[]{:S(2)}, u32[]{:S(2)}) collective-permute-start(bf16[128,1024]{1,0:T(8,128)(2,1)} %get-tuple-element.156), channel_id=1, source_target_pairs={{0,16},{4,20},{8,24},{12,28},{16,0},{20,4},{24,8},{28,12},{1,17},{... | collective-permute-start | bytes 786440 | tf_op jit(solution)/shard_map/ppermute | solution.py:287
  193.4 18.8 %collective-permute-start.39 = (bf16[128,1024]{1,0:T(8,128)(2,1)}, bf16[128,1024]{1,0:T(8,128)(2,1)S(1)}, u32[]{:S(2)}, u32[]{:S(2)}) collective-permute-start(bf16[128,1024]{1,0:T(8,128)(2,1)} %get-tuple-element.155), channel_id=1, source_target_pairs={{0,8},{4,12},{8,0},{12,4},{16,24},{20,28},{24,16},{28,20},{1,9},{5... | collective-permute-start | bytes 786440 | tf_op jit(solution)/shard_map/ppermute | solution.py:287
  219.7 17.2 %collective-permute-start.58 = (bf16[8,32,384]{2,1,0:T(8,128)(2,1)}, bf16[8,32,384]{2,1,0:T(8,128)(2,1)S(1)}, u32[]{:S(2)}, u32[]{:S(2)}) collective-permute-start(bf16[8,32,384]{2,1,0:T(8,128)(2,1)} %get-tuple-element.179), channel_id=1, source_target_pairs={{0,2},{1,3},{2,0},{3,1},{4,6},{5,7},{6,4},{7,5},{8,10},{9,11},{10,... | collective-permute-start | bytes 589832 | tf_op jit(solution)/shard_map/ppermute | solution.py:291
  225.6 16.0 %collective-permute-start.54 = (bf16[128,1024]{1,0:T(8,128)(2,1)}, bf16[128,1024]{1,0:T(8,128)(2,1)S(1)}, u32[]{:S(2)}, u32[]{:S(2)}) collective-permute-start(bf16[128,1024]{1,0:T(8,128)(2,1)} %get-tuple-element.185), channel_id=1, source_target_pairs={{0,8},{4,12},{8,0},{12,4},{16,24},{20,28},{24,16},{28,20},{1,9},{5... | collective-permute-start | bytes 786440 | tf_op jit(solution)/shard_map/ppermute | solution.py:287
  227.0 14.6 %collective-permute-start.55 = (bf16[128,1024]{1,0:T(8,128)(2,1)}, bf16[128,1024]{1,0:T(8,128)(2,1)S(1)}, u32[]{:S(2)}, u32[]{:S(2)}) collective-permute-start(bf16[128,1024]{1,0:T(8,128)(2,1)} %get-tuple-element.186), channel_id=1, source_target_pairs={{0,16},{4,20},{8,24},{12,28},{16,0},{20,4},{24,8},{28,12},{1,17},{... | collective-permute-start | bytes 786440 | tf_op jit(solution)/shard_map/ppermute | solution.py:287
  236.9 49.8 %collective-permute-start.53 = (bf16[128,1024]{1,0:T(8,128)(2,1)S(1)}, bf16[128,1024]{1,0:T(8,128)(2,1)S(1)}, u32[]{:S(2)}, u32[]{:S(2)}) collective-permute-start(bf16[128,1024]{1,0:T(8,128)(2,1)S(1)} %add_convert_fusion), channel_id=1, source_target_pairs={{0,0},{1,16},{2,4},{3,20},{4,2},{5,18},{6,6},{7,22},{8,1},{9,17},{... | collective-permute-start | bytes 786440 | tf_op jit(solution)/shard_map/ppermute | solution.py:296
  245.3 41.4 %collective-permute-start.60 = (bf16[128,1024]{1,0:T(8,128)(2,1)}, bf16[128,1024]{1,0:T(8,128)(2,1)S(1)}, u32[]{:S(2)}, u32[]{:S(2)}) collective-permute-start(bf16[128,1024]{1,0:T(8,128)(2,1)} %get-tuple-element.193), channel_id=1, source_target_pairs={{0,0},{1,16},{2,4},{3,20},{4,2},{5,18},{6,6},{7,22},{8,1},{9,17},{... | collective-permute-start | bytes 786440 | tf_op jit(solution)/shard_map/ppermute | solution.py:296
  249.9 19.7 %all-to-all-start = ((bf16[8,32,896]{2,1,0:T(8,128)(2,1)}), bf16[8,32,896]{2,1,0:T(8,128)(2,1)S(1)}, u32[]{:S(2)}, u32[]{:S(2)}) async-start(bf16[8,32,896]{2,1,0:T(8,128)(2,1)} %pad_maximum_fusion.1), calls=%async_computation.1 | async-start | bytes 917504 | tf_op jit(solution)/shard_map/all_to_all | solution.py:1121
  262.1 24.6 %collective-permute-start.61 = (bf16[128,1024]{1,0:T(8,128)(2,1)S(1)}, bf16[128,1024]{1,0:T(8,128)(2,1)S(1)}, u32[]{:S(2)}, u32[]{:S(2)}) collective-permute-start(bf16[128,1024]{1,0:T(8,128)(2,1)S(1)} %pad_maximum_fusion.2), channel_id=1, source_target_pairs={{0,0},{1,8},{2,16},{3,24},{4,1},{5,9},{6,17},{7,25},{8,2},{9,10},{... | collective-permute-start | bytes 786440 | tf_op jit(solution)/shard_map/ppermute | solution.py:296
  (105 other events, 927.4 us)
Sparse Core Ops, SparseCore 0:
  90.5 48.5 all-gather.1
  175.9 42.9 reduce-scatter.2
  233.0 25.3 reduce-scatter.4

commit v5 on v4

--- a/solution.py
+++ b/solution.py
@@ -647,7 +647,7 @@
 
     def kernel(
         own_length, other_length, slopes_ref, n0, n1, n2, n3, n4, n5, n6, n7, w0, w1, w2, w3,
-        vectors_ref, joint_ref, mixed_ref, weight_ref, normed_ref, sems, more_sems,
+        vectors_ref, joint_ref, mixed_ref, probs_ref, weight_ref, normed_ref, sems, more_sems,
     ):
         rep = lax.axis_index("rep")
         weight_copies = place_pieces((w0, w1, w2, w3), weight_ref, sems)
@@ -686,14 +686,20 @@
                     scores = scores_of(masked, keys, slopes_ref[j], distance, allowed, scale)
                     top = jnp.max(scores, 1, keepdims=True)
                     exps = jnp.exp(scores - top)
-                    probs = exps / jnp.sum(exps, 1, keepdims=True)
-                    mixed = jnp.where(mine, dot_nn(probs.astype(jnp.bfloat16), values), mixed)
+                    probs = exps * (1.0 / jnp.sum(exps, 1, keepdims=True))
+                    probs_low = probs.astype(jnp.bfloat16)
+                    probs_ref[j, at, :] = probs_low
+                    mixed = jnp.where(mine, dot_nn(probs_low, values), mixed)
                 mixed_ref[at, :] = mixed.astype(jnp.bfloat16)
 
     return kernel_call(
         kernel,
         [LOCAL] * 2 + [SCALARS] + [ANYWHERE] * 12 + [LOCAL],
-        [sds((rows, width), jnp.bfloat16), sds((rows, own), jnp.bfloat16)],
+        [
+            sds((rows, width), jnp.bfloat16),
+            sds((rows, own), jnp.bfloat16),
+            sds((2, rows, span), jnp.bfloat16),
+        ],
         [
             pltpu.VMEM((features, width), jnp.bfloat16),
             pltpu.VMEM((rows, features), jnp.bfloat16),
@@ -722,7 +728,7 @@
     )
 
 
-def attention_backward(lens, slopes, blocks, joint, weights, out_part):
+def attention_backward(probs, blocks, joint, weights, out_part):
     rows, features = PLANE * blocks[0].shape[0], blocks[0].shape[1]
     span = rows // 2
     width = weights[0].shape[1]
@@ -732,15 +738,16 @@
     step_rows = span // QUARTERS
 
     def kernel(
-        own_length, other_length, slopes_ref, g0, g1, g2, g3, g4, g5, g6, g7,
+        probs_hbm, g0, g1, g2, g3, g4, g5, g6, g7,
         joint_hbm, w0, w1, w2, w3, out_ref,
         joint_grad_ref, sums_ref, keep_ref, give_ref,
-        weight_ref, mixed_grad_ref, key_acc, value_acc, joint_ref, grad_ref, out_all, sems, more_sems,
+        weight_ref, mixed_grad_ref, key_acc, value_acc, joint_ref, grad_ref, out_all, probs_ref, sems,
+        more_sems, probs_sem,
     ):
-        rep = lax.axis_index("rep")
         out_copy = load(out_ref, out_all, sems.at[DEPTH])
         grad_copies = load_blocks((g0, g1, g2, g3, g4, g5, g6, g7), grad_ref, more_sems)
         joint_copy = load(joint_hbm, joint_ref, sems.at[DEPTH + 1])
+        probs_copy = load(probs_hbm, probs_ref, probs_sem.at[0])
         copies = place_pieces((w0, w1, w2, w3), weight_ref, sems)
         out_copy.wait()
         for s in range(2):
@@ -750,14 +757,12 @@
                 mixed_grad = dot_nt(grad_ref[at, :], out_all[...])
                 mixed_grad_ref[at, :] = mixed_grad.astype(jnp.bfloat16)
         joint_copy.wait()
+        probs_copy.wait()
         lane = lax.broadcasted_iota(jnp.int32, (step_rows, own), 1)
         lane_all = lax.broadcasted_iota(jnp.int32, (span, own), 1)
-        key_pos = row_positions((1, span), 1, rep, 0)
         for s in range(2):
             keys = joint_ref[pl.ds(s * span, span), own : 2 * own]
             values = joint_ref[pl.ds(s * span, span), 2 * own :]
-            length = (own_length, other_length)[s][0:1, 0:1]
-            inside = key_pos.astype(jnp.float32) < length
             key_acc[...] = jnp.zeros_like(key_acc)
             value_acc[...] = jnp.zeros_like(value_acc)
 
@@ -765,9 +770,6 @@
             def _(i):
                 first = pl.multiple_of(i * step_rows, step_rows)
                 at = pl.ds(s * span + first, step_rows)
-                query_pos = row_positions((step_rows, 1), 0, rep, first)
-                allowed = (key_pos <= query_pos) & inside
-                distance = (query_pos - key_pos).astype(jnp.float32)
                 query = joint_ref[at, :own]
                 mixed_grad = mixed_grad_ref[at, :]
                 query_grad = jnp.zeros((step_rows, own), jnp.float32)
@@ -775,16 +777,14 @@
                     mine = (lane >= j * head_size) & (lane < (j + 1) * head_size)
                     masked = jnp.where(mine, query, jnp.zeros_like(query))
                     masked_grad = jnp.where(mine, mixed_grad, jnp.zeros_like(mixed_grad))
-                    scores = scores_of(masked, keys, slopes_ref[j], distance, allowed, scale)
-                    top = jnp.max(scores, 1, keepdims=True)
-                    exps = jnp.exp(scores - top)
-                    probs = exps / jnp.sum(exps, 1, keepdims=True)
+                    probs_low = probs_ref[j, at, :]
+                    probs = probs_low.astype(jnp.float32)
                     probs_grad = dot_nt(masked_grad, values)
                     row_dot = jnp.sum(probs * probs_grad, 1, keepdims=True)
                     score_grad = (probs * (probs_grad - row_dot)).astype(jnp.bfloat16)
                     query_grad = jnp.where(mine, dot_nn(score_grad, keys), query_grad)
                     key_acc[...] += outer(score_grad, masked)
-                    value_acc[...] += outer(probs.astype(jnp.bfloat16), masked_grad)
+                    value_acc[...] += outer(probs_low, masked_grad)
                 joint_grad_ref[at, :own] = (query_grad * scale).astype(jnp.bfloat16)
 
             at = pl.ds(s * span, span)
@@ -804,7 +804,7 @@
     half = sds((2, 2, span // 4, features), jnp.bfloat16)
     return kernel_call(
         kernel,
-        [LOCAL] * 2 + [SCALARS] + [ANYWHERE] * 14,
+        [ANYWHERE] * 15,
         [sds((rows, width), jnp.bfloat16), sds((1, width), jnp.float32), half, half],
         [
             pltpu.VMEM((features, width), jnp.bfloat16),
@@ -814,11 +814,13 @@
             pltpu.VMEM((rows, width), jnp.bfloat16),
             pltpu.VMEM((rows, features), jnp.bfloat16),
             pltpu.VMEM((own, features), jnp.bfloat16),
+            pltpu.VMEM(probs.shape, jnp.bfloat16),
             pltpu.SemaphoreType.DMA((DEPTH + 2,)),
             pltpu.SemaphoreType.DMA((PLANE,)),
+            pltpu.SemaphoreType.DMA((1,)),
         ],
         2 * rows * features * (width + own) + 20 * rows * span * own,
-        (*lens, slopes, *blocks, joint, *weights, out_part),
+        (probs, *blocks, joint, *weights, out_part),
     )
 
 
@@ -1061,7 +1063,7 @@
     branch_near = [over_rep(branch_grad, flip) for flip in (1, 2, 4, 6)]
     heads = (2 * rep + jnp.arange(2)).astype(jnp.float32)
     slopes = jnp.exp2(-8.0 * (heads + 1.0) / HEADS)
-    joint, mixed = attention_forward(lens, slopes, normed_blocks, qkv_parts, vectors)
+    joint, mixed, probs = attention_forward(lens, slopes, normed_blocks, qkv_parts, vectors)
     out_moved = [
         over_all(
             after(out_own, qkv_parts),
@@ -1100,7 +1102,7 @@
     attended_blocks = gather_plane(attended_grad)
     branch_own, *branch_rest = send_parts(branch_halves)
     joint_grad, joint_sums, keep, give = attention_backward(
-        lens, slopes, attended_blocks, joint, qkv_parts, out_part
+        probs, attended_blocks, joint, qkv_parts, out_part
     )
     received = over_rep(after(give, branch_rest), 1)
     qkv_slices = qkv_weights(normed_blocks, joint_grad)
@@ -1153,7 +1155,7 @@
     small_arrived = lax.all_to_all(after(small_packed, arrived), ("rep", "shard"), 0, 0, tiled=True)
     layer_out, tokens_grad, down_grad = (
         moved_back.astype(jnp.float32)
-        for moved_back in after((layer_out, tokens_grad, down_grad), small_arrived)
+        for moved_back in after((layer_out, tokens_grad, down_grad), arrived)
     )
     small_sums = jnp.sum(small_arrived.astype(jnp.float32), 0)
     sums = []

time: 297 us -> 291 us (0.980)
  Pallas kernels: 81.7 us -> 78.5 us
    pallas_call x16, Pallas kernels: 81.7 us -> 78.5 us  [kernel_call(): pl.pallas_call(kernel, out_shape=outs, in_specs=ins, out_specs=[LOCAL] *...]
where the time goes in v5:
time: 291 us; the launch traced here: 290 us
  waiting for transfers between devices  85.1 us (29%)
  starting transfers between devices  79.7 us (27%)
  Pallas kernels  78.5 us (27%)
  local copies, waits for them, and re-layouts  17.5 us (6%)
  between operations  16.1 us (6%)
  other arithmetic  13.2 us (5%)
    pallas_call x16, Pallas kernels, kernel_call(): pl.pallas_call(kernel, out_shape=outs, in_specs=ins, out_specs=[LOCAL] *...  78.5 us
    ppermute x45, waiting for transfers between devices, over_rep(): return lax.ppermute(value, 'rep', [(i, i ^ flip) for i in range(PLANE)])  42.3 us
    ppermute x45, starting transfers between devices, over_rep(): return lax.ppermute(value, 'rep', [(i, i ^ flip) for i in range(PLANE)])  31 us
    ppermute x9, waiting for transfers between devices, over_z(): lax.ppermute(value, 'shard', [(i, (i + step) % DEPTH) for i in range(DEPT...  23.9 us
    ppermute x9, starting transfers between devices, over_z(): lax.ppermute(value, 'shard', [(i, (i + step) % DEPTH) for i in range(DEPT...  21 us
    unnamed x128, local copies, waits for them, and re-layouts  11.1 us
    all_to_all x1, starting transfers between devices, body_planes(): arrived = lax.all_to_all(both, 'rep', 0, 0, tiled=True)  10.6 us
    ppermute x8, starting transfers between devices, over_all(): return lax.ppermute(value, ('rep', 'shard'), pairs)  10.6 us
  transfers between devices with their start and end apart: 67, of which 25 were waited for; matrix products, arithmetic and copies ran while one was open for 6% of the time, Pallas kernels for 21%

profile of v5, /device:TPU:0, one launch (start us, length us, event | category | flops | bytes accessed | tf_op | source)
XLA Modules:
  0.0 290.1 jit_solution(16065457776051110813)
XLA Ops:
  13.1 8.4 %collective-permute-start.1 = (bf16[24,128]{1,0:T(8,128)(2,1)S(1)}, bf16[24,128]{1,0:T(8,128)(2,1)S(1)}, u32[]{:S(2)}, u32[]{:S(2)}) collective-permute-start(bf16[24,128]{1,0:T(8,128)(2,1)S(1)} %add_bitcast_fusion.p0), channel_id=1, source_target_pairs={{0,1},{1,2},{2,3},{3,0},{4,5},{5,6},{6,7},{7,4},{8,9},{9,10},{10,1... | collective-permute-start | bytes 18440 | tf_op jit(solution)/shard_map/ppermute | solution.py:291
  21.5 4.1 %collective-permute-start.2 = (bf16[24,128]{1,0:T(8,128)(2,1)S(1)}, bf16[24,128]{1,0:T(8,128)(2,1)S(1)}, u32[]{:S(2)}, u32[]{:S(2)}) collective-permute-start(bf16[24,128]{1,0:T(8,128)(2,1)S(1)} %add_bitcast_fusion.p0), channel_id=1, source_target_pairs={{0,2},{1,3},{2,0},{3,1},{4,6},{5,7},{6,4},{7,5},{8,10},{9,11},{10,... | collective-permute-start | bytes 18440 | tf_op jit(solution)/shard_map/ppermute | solution.py:291
  28.6 4.5 %collective-permute-done.3.p3 = bf16[24,128]{1,0:T(8,128)(2,1)S(1)} collective-permute-done((bf16[24,128]{1,0:T(8,128)(2,1)S(1)}, bf16[24,128]{1,0:T(8,128)(2,1)S(1)}, u32[]{:S(2)}, u32[]{:S(2)}) %collective-permute-start.3) | collective-permute-done | bytes 6176 | tf_op jit(solution)/shard_map/ppermute | solution.py:291
  37.9 3.1 %collective-permute-start.10 = (bf16[256,384]{1,0:T(8,128)(2,1)}, bf16[256,384]{1,0:T(8,128)(2,1)S(1)}, u32[]{:S(2)}, u32[]{:S(2)}) collective-permute-start(bf16[256,384]{1,0:T(8,128)(2,1)} %get-tuple-element.120.w0), channel_id=1, source_target_pairs={{0,1},{1,2},{2,3},{3,0},{4,5},{5,6},{6,7},{7,4},{8,9},{9,10},{10,1... | collective-permute-start | bytes 589832 | tf_op jit(solution)/shard_map/ppermute | solution.py:291
  48.7 7.6 %collective-permute-done.11.w2 = bf16[256,384]{1,0:T(8,128)(2,1)S(1)} collective-permute-done((bf16[256,384]{1,0:T(8,128)(2,1)}, bf16[256,384]{1,0:T(8,128)(2,1)S(1)}, u32[]{:S(2)}, u32[]{:S(2)}) %collective-permute-start.11) | collective-permute-done | bytes 196640 | tf_op jit(solution)/shard_map/ppermute | solution.py:291
  60.4 3.7 %collective-permute-start.16 = (bf16[128,1024]{1,0:T(8,128)(2,1)}, bf16[128,1024]{1,0:T(8,128)(2,1)S(1)}, u32[]{:S(2)}, u32[]{:S(2)}) collective-permute-start(bf16[128,1024]{1,0:T(8,128)(2,1)} %get-tuple-element.126), channel_id=1, source_target_pairs={{0,1},{4,5},{9,10},{13,14},{18,19},{22,23},{27,24},{31,28}} | collective-permute-start | bytes 786440 | tf_op jit(solution)/shard_map/ppermute | solution.py:296
  71.0 5.6 %collective-permute-done.17 = bf16[128,1024]{1,0:T(8,128)(2,1)S(1)} collective-permute-done((bf16[128,1024]{1,0:T(8,128)(2,1)}, bf16[128,1024]{1,0:T(8,128)(2,1)S(1)}, u32[]{:S(2)}, u32[]{:S(2)}) %collective-permute-start.17) | collective-permute-done | bytes 262176 | tf_op jit(solution)/shard_map/ppermute | solution.py:296
  77.2 12.8 %shard_map.265 = (bf16[1024,384]{1,0:T(8,128)(2,1)}, bf16[1024,128]{1,0:T(8,128)(2,1)}, bf16[2,1024,512]{2,1,0:T(8,128)(2,1)}) custom-call(f32[8,128]{1,0:T(8,128)} %copy-done.60, f32[8,128]{1,0:T(8,128)} %copy-done.61, f32[2]{0:T(128)} %multiply_exponential_fusion.slopes_ref, bf16[128,1024]{1,0:T(8,128)(2,1)} %get-tuple-element.114.n0, ...), custom_call_target="tpu_custom_call" | custom-call | flops 1342177280 | bytes 8388608 | tf_op jit(solution)/shard_map/pallas_call | solution.py:472
  100.8 3.5 %collective-permute-start.25 = (bf16[128,1024]{1,0:T(8,128)(2,1)}, bf16[128,1024]{1,0:T(8,128)(2,1)S(1)}, u32[]{:S(2)}, u32[]{:S(2)}) collective-permute-start(bf16[128,1024]{1,0:T(8,128)(2,1)} %get-tuple-element.135), channel_id=1, source_target_pairs={{0,16},{4,20},{8,24},{12,28},{16,0},{20,4},{24,8},{28,12},{1,17},{... | collective-permute-start | bytes 786440 | tf_op jit(solution)/shard_map/ppermute | solution.py:287
  104.2 5.9 %collective-permute-done.24.two = bf16[128,1024]{1,0:T(8,128)(2,1)S(1)} collective-permute-done((bf16[128,1024]{1,0:T(8,128)(2,1)}, bf16[128,1024]{1,0:T(8,128)(2,1)S(1)}, u32[]{:S(2)}, u32[]{:S(2)}) %collective-permute-start.24) | collective-permute-done | bytes 262176 | tf_op jit(solution)/shard_map/ppermute | solution.py:287
  110.1 6.3 %collective-permute-done.25.four = bf16[128,1024]{1,0:T(8,128)(2,1)S(1)} collective-permute-done((bf16[128,1024]{1,0:T(8,128)(2,1)}, bf16[128,1024]{1,0:T(8,128)(2,1)S(1)}, u32[]{:S(2)}, u32[]{:S(2)}) %collective-permute-start.25) | collective-permute-done | bytes 262176 | tf_op jit(solution)/shard_map/ppermute | solution.py:287
  123.6 5.5 %collective-permute-done.28.n2 = bf16[128,1024]{1,0:T(8,128)(2,1)S(1)} collective-permute-done((bf16[128,1024]{1,0:T(8,128)(2,1)}, bf16[128,1024]{1,0:T(8,128)(2,1)S(1)}, u32[]{:S(2)}, u32[]{:S(2)}) %collective-permute-start.28) | collective-permute-done | bytes 262176 | tf_op jit(solution)/shard_map/ppermute | solution.py:287
  129.1 5.1 %collective-permute-done.29.n4 = bf16[128,1024]{1,0:T(8,128)(2,1)S(1)} collective-permute-done((bf16[128,1024]{1,0:T(8,128)(2,1)}, bf16[128,1024]{1,0:T(8,128)(2,1)S(1)}, u32[]{:S(2)}, u32[]{:S(2)}) %collective-permute-start.29) | collective-permute-done | bytes 262176 | tf_op jit(solution)/shard_map/ppermute | solution.py:287
  139.9 10.7 %shard_map.269 = (bf16[1024,512]{1,0:T(8,128)(2,1)}, bf16[1024,512]{1,0:T(8,128)(2,1)}, f32[1,512]{1,0:T(1,128)}, bf16[2,2,128,1024]{3,2,1,0:T(8,128)(2,1)}, bf1...) custom-call(bf16[128,1024]{1,0:T(8,128)(2,1)} %get-tuple-element.138.n0, ...), custom_call_target="tpu_custom_call" | custom-call | flops 4294967296 | bytes 8388608 | tf_op jit(solution)/shard_map/pallas_call | solution.py:472
  160.7 6.5 %shard_map.272 = bf16[4,256,1024]{2,1,0:T(8,128)(2,1)} custom-call(bf16[128,1024]{1,0:T(8,128)(2,1)} %get-tuple-element.138.n0, bf16[128,1024]{1,0:T(8,128)(2,1)} %copy-done.27, bf16[128,1024]{1,0:T(8,128)(2,1)} %copy-done.21, bf16[128,1024]{1,0:T(8,128)(2,1)} %copy-done.28, bf16[128,1024]{1,0:T(8,128)(2,1)} %copy-done.22, bf16[128,1024]{1,0:T(8,128)(2,1)} %copy-done.29, ...), custom_call_target="tpu_custom_call" | custom-call | flops 2147483648 | bytes 8388608 | tf_op jit(solution)/shard_map/pallas_call | solution.py:472
  180.8 5.8 %collective-permute-done.46.g2 = bf16[128,1024]{1,0:T(8,128)(2,1)S(1)} collective-permute-done((bf16[128,1024]{1,0:T(8,128)(2,1)S(1)}, bf16[128,1024]{1,0:T(8,128)(2,1)S(1)}, u32[]{:S(2)}, u32[]{:S(2)}) %collective-permute-start.46) | collective-permute-done | bytes 262176 | tf_op jit(solution)/shard_map/ppermute | solution.py:287
  186.5 4.7 %collective-permute-done.47.g4 = bf16[128,1024]{1,0:T(8,128)(2,1)S(1)} collective-permute-done((bf16[128,1024]{1,0:T(8,128)(2,1)S(1)}, bf16[128,1024]{1,0:T(8,128)(2,1)S(1)}, u32[]{:S(2)}, u32[]{:S(2)}) %collective-permute-start.47) | collective-permute-done | bytes 262176 | tf_op jit(solution)/shard_map/ppermute | solution.py:287
  196.2 12.7 %shard_map.274 = (bf16[1024,384]{1,0:T(8,128)(2,1)}, f32[1,384]{1,0:T(1,128)}, bf16[2,2,128,1024]{3,2,1,0:T(8,128)(2,1)}, bf16[2,2,128,1024]{3,2,1,0:T(8,128)(2,1)}) custom-call(bf16[2,1024,512]{2,1,0:T(8,128)(2,1)} %get-tuple-element.159.probs_hbm, bf16[128,1024]{1,0:T(8,128)(2,1)} %get-tuple-element.170.g0, bf16[128,1024]{1,0:T(8,128)(2,1)} %copy-done.17, ...), custom_call_target="tpu_custom_call" | custom-call | flops 2415919104 | bytes 8388608 | tf_op jit(solution)/shard_map/pallas_call | solution.py:472
  210.6 5.9 %shard_map.275 = (bf16[8,32,384]{2,1,0:T(8,128)(2,1)}, bf16[8,32,384]{2,1,0:T(8,128)(2,1)}, bf16[8,32,384]{2,1,0:T(8,128)(2,1)}, bf16[8,32,384]{2,1,0:T(8,128)(2,1)}) custom-call(bf16[128,1024]{1,0:T(8,128)(2,1)} %get-tuple-element.114.n0, bf16[128,1024]{1,0:T(8,128)(2,1)} %copy-done.46, bf16[128,1024]{1,0:T(8,128)(2,1)} %copy-done.43, ...), custom_call_target="tpu_custom_call" | custom-call | flops 805306368 | bytes 8388608 | tf_op jit(solution)/shard_map/pallas_call | solution.py:472
  225.9 3.7 %shard_map.277 = bf16[4,32,1024]{2,1,0:T(8,128)(2,1)} custom-call(bf16[1024,128]{1,0:T(8,128)(2,1)} %get-tuple-element.190.mixed_ref, bf16[128,1024]{1,0:T(8,128)(2,1)} %get-tuple-element.170.g0, bf16[128,1024]{1,0:T(8,128)(2,1)} %copy-done.17, bf16[128,1024]{1,0:T(8,128)(2,1)} %copy-done.13, bf16[128,1024]{1,0:T(8,128)(2,1)} %copy-done.18, ...), custom_call_target="tpu_custom_call" | custom-call | flops 268435456 | bytes 8388608 | tf_op jit(solution)/shard_map/pallas_call | solution.py:472
  234.4 4.0 %collective-permute-done.59 = bf16[8,32,384]{2,1,0:T(8,128)(2,1)S(1)} collective-permute-done((bf16[8,32,384]{2,1,0:T(8,128)(2,1)S(1)}, bf16[8,32,384]{2,1,0:T(8,128)(2,1)S(1)}, u32[]{:S(2)}, u32[]{:S(2)}) %collective-permute-start.59) | collective-permute-done | bytes 196640 | tf_op jit(solution)/shard_map/ppermute | solution.py:291
  246.7 10.6 %all-to-all-start = ((bf16[8,32,896]{2,1,0:T(8,128)(2,1)}), bf16[8,32,896]{2,1,0:T(8,128)(2,1)S(1)}, u32[]{:S(2)}, u32[]{:S(2)}) async-start(bf16[8,32,896]{2,1,0:T(8,128)(2,1)} %pad_maximum_fusion.1), calls=%async_computation.1 | async-start | bytes 917504 | tf_op jit(solution)/shard_map/all_to_all | solution.py:1123
  259.5 6.8 %all-to-all-done = bf16[8,32,896]{2,1,0:T(8,128)(2,1)S(1)} async-done(((bf16[8,32,896]{2,1,0:T(8,128)(2,1)}), bf16[8,32,896]{2,1,0:T(8,128)(2,1)S(1)}, u32[]{:S(2)}, u32[]{:S(2)}) %all-to-all-start) | async-done | bytes 458784 | tf_op jit(solution)/shard_map/all_to_all | solution.py:1123
  268.2 6.1 %all-to-all-start.1 = ((bf16[32,2,192]{2,1,0:T(2,128)(2,1)}), bf16[32,2,192]{2,1,0:T(2,128)(2,1)S(1)}, u32[]{:S(2)}, u32[]{:S(2)}) async-start(bf16[32,2,192]{2,1,0:T(2,128)(2,1)} %reshape.88), calls=%async_computation.2 | async-start | bytes 65536 | tf_op jit(solution)/shard_map/all_to_all | solution.py:1155
  (308 shorter events, 120.7 us)
Async XLA Ops:
  7.2 132.6 %all-gather.2.cloned.1.call-start = ((), (), s32[]{:S(2)}) async-start(), calls=%async_computation.4 | async-start | bytes 2621440 | tf_op jit(solution)/shard_map/all_gather | solution.py:1083
  8.3 24.9 %collective-permute-start = (bf16[256,1024]{1,0:T(8,128)(2,1)S(1)}, bf16[256,1024]{1,0:T(8,128)(2,1)S(1)}, u32[]{:S(2)}, u32[]{:S(2)}) collective-permute-start(bf16[256,1024]{1,0:T(8,128)(2,1)S(1)} %pad_maximum_fusion), channel_id=1, source_target_pairs={{0,0},{1,8},{2,4},{3,12},{4,2},{5,10},{6,6},{7,14},{8,16},{9,24},{... | collective-permute-start | bytes 1572872 | tf_op jit(solution)/shard_map/ppermute | solution.py:296
  13.1 15.5 %collective-permute-start.1 = (bf16[24,128]{1,0:T(8,128)(2,1)S(1)}, bf16[24,128]{1,0:T(8,128)(2,1)S(1)}, u32[]{:S(2)}, u32[]{:S(2)}) collective-permute-start(bf16[24,128]{1,0:T(8,128)(2,1)S(1)} %add_bitcast_fusion.p0), channel_id=1, source_target_pairs={{0,1},{1,2},{2,3},{3,0},{4,5},{5,6},{6,7},{7,4},{8,9},{9,10},{10,1... | collective-permute-start | bytes 18440 | tf_op jit(solution)/shard_map/ppermute | solution.py:291
  41.0 15.3 %collective-permute-start.11 = (bf16[256,384]{1,0:T(8,128)(2,1)}, bf16[256,384]{1,0:T(8,128)(2,1)S(1)}, u32[]{:S(2)}, u32[]{:S(2)}) collective-permute-start(bf16[256,384]{1,0:T(8,128)(2,1)} %get-tuple-element.120.w0), channel_id=1, source_target_pairs={{0,2},{1,3},{2,0},{3,1},{4,6},{5,7},{6,4},{7,5},{8,10},{9,11},{10,... | collective-permute-start | bytes 589832 | tf_op jit(solution)/shard_map/ppermute | solution.py:291
  41.0 18.2 %collective-permute-start.7 = (bf16[128,1024]{1,0:T(8,128)(2,1)}, bf16[128,1024]{1,0:T(8,128)(2,1)S(1)}, u32[]{:S(2)}, u32[]{:S(2)}) collective-permute-start(bf16[128,1024]{1,0:T(8,128)(2,1)} %get-tuple-element.114.n0), channel_id=1, source_target_pairs={{0,8},{4,12},{8,0},{12,4},{16,24},{20,28},{24,16},{28,20},{1,9},{5... | collective-permute-start | bytes 786440 | tf_op jit(solution)/shard_map/ppermute | solution.py:287
  43.1 16.1 %collective-permute-start.8 = (bf16[128,1024]{1,0:T(8,128)(2,1)}, bf16[128,1024]{1,0:T(8,128)(2,1)S(1)}, u32[]{:S(2)}, u32[]{:S(2)}) collective-permute-start(bf16[128,1024]{1,0:T(8,128)(2,1)} %get-tuple-element.114.n0), channel_id=1, source_target_pairs={{0,16},{4,20},{8,24},{12,28},{16,0},{20,4},{24,8},{28,12},{1,17},{... | collective-permute-start | bytes 786440 | tf_op jit(solution)/shard_map/ppermute | solution.py:287
  44.9 14.3 %collective-permute-start.9 = (bf16[128,1024]{1,0:T(8,128)(2,1)}, bf16[128,1024]{1,0:T(8,128)(2,1)S(1)}, u32[]{:S(2)}, u32[]{:S(2)}) collective-permute-start(bf16[128,1024]{1,0:T(8,128)(2,1)} %get-tuple-element.114.n0), channel_id=1, source_target_pairs={{0,24},{4,28},{8,16},{12,20},{16,8},{20,12},{24,0},{28,4},{1,25},{... | collective-permute-start | bytes 786440 | tf_op jit(solution)/shard_map/ppermute | solution.py:287
  66.1 23.9 %collective-permute-start.18 = (bf16[128,1024]{1,0:T(8,128)(2,1)}, bf16[128,1024]{1,0:T(8,128)(2,1)S(1)}, u32[]{:S(2)}, u32[]{:S(2)}) collective-permute-start(bf16[128,1024]{1,0:T(8,128)(2,1)} %get-tuple-element.126), channel_id=1, source_target_pairs={{0,3},{4,7},{9,8},{13,12},{18,17},{22,21},{27,26},{31,30}} | collective-permute-start | bytes 786440 | tf_op jit(solution)/shard_map/ppermute | solution.py:296
  69.3 20.7 %collective-permute-start.19 = (bf16[128,1024]{1,0:T(8,128)(2,1)S(1)}, bf16[128,1024]{1,0:T(8,128)(2,1)S(1)}, u32[]{:S(2)}, u32[]{:S(2)}) collective-permute-start(bf16[128,1024]{1,0:T(8,128)(2,1)S(1)} %slice_select_fusion.g0.seed_ref), channel_id=1, source_target_pairs={{0,4},{4,0},{8,12},{12,8},{16,20},{20,16},{24,28},{28,24},{1,5},{5... | collective-permute-start | bytes 786440 | tf_op jit(solution)/shard_map/ppermute | solution.py:287
  69.5 20.5 %collective-permute-start.20 = (bf16[128,1024]{1,0:T(8,128)(2,1)S(1)}, bf16[128,1024]{1,0:T(8,128)(2,1)S(1)}, u32[]{:S(2)}, u32[]{:S(2)}) collective-permute-start(bf16[128,1024]{1,0:T(8,128)(2,1)S(1)} %slice_select_fusion.g0.seed_ref), channel_id=1, source_target_pairs={{0,8},{4,12},{8,0},{12,4},{16,24},{20,28},{24,16},{28,20},{1,9},{5... | collective-permute-start | bytes 786440 | tf_op jit(solution)/shard_map/ppermute | solution.py:287
  71.0 19.1 %collective-permute-start.21 = (bf16[128,1024]{1,0:T(8,128)(2,1)S(1)}, bf16[128,1024]{1,0:T(8,128)(2,1)S(1)}, u32[]{:S(2)}, u32[]{:S(2)}) collective-permute-start(bf16[128,1024]{1,0:T(8,128)(2,1)S(1)} %slice_select_fusion.g0.seed_ref), channel_id=1, source_target_pairs={{0,16},{4,20},{8,24},{12,28},{16,0},{20,4},{24,8},{28,12},{1,17},{... | collective-permute-start | bytes 786440 | tf_op jit(solution)/shard_map/ppermute | solution.py:287
  91.0 153.6 %reduce-scatter.3.cloned.1.call-start = ((), (), s32[]{:S(2)}) async-start(), calls=%async_computation.5 | async-start | bytes 2621440 | tf_op jit(solution)/shard_map/reduce_scatter | solution.py:367
  100.8 15.6 %collective-permute-start.25 = (bf16[128,1024]{1,0:T(8,128)(2,1)}, bf16[128,1024]{1,0:T(8,128)(2,1)S(1)}, u32[]{:S(2)}, u32[]{:S(2)}) collective-permute-start(bf16[128,1024]{1,0:T(8,128)(2,1)} %get-tuple-element.135), channel_id=1, source_target_pairs={{0,16},{4,20},{8,24},{12,28},{16,0},{20,4},{24,8},{28,12},{1,17},{... | collective-permute-start | bytes 786440 | tf_op jit(solution)/shard_map/ppermute | solution.py:287
  176.3 80.9 %reduce-scatter.5.cloned.1.call-start = ((), (), s32[]{:S(2)}) async-start(), calls=%async_computation.6 | async-start | bytes 327680 | tf_op jit(solution)/shard_map/reduce_scatter | solution.py:367
  191.9 17.0 %collective-permute-start.41 = (bf16[128,1024]{1,0:T(8,128)(2,1)}, bf16[128,1024]{1,0:T(8,128)(2,1)S(1)}, u32[]{:S(2)}, u32[]{:S(2)}) collective-permute-start(bf16[128,1024]{1,0:T(8,128)(2,1)} %get-tuple-element.158), channel_id=1, source_target_pairs={{0,24},{4,28},{8,16},{12,20},{16,8},{20,12},{24,0},{28,4},{1,25},{... | collective-permute-start | bytes 786440 | tf_op jit(solution)/shard_map/ppermute | solution.py:287
  192.9 16.0 %collective-permute-start.40 = (bf16[128,1024]{1,0:T(8,128)(2,1)}, bf16[128,1024]{1,0:T(8,128)(2,1)S(1)}, u32[]{:S(2)}, u32[]{:S(2)}) collective-permute-start(bf16[128,1024]{1,0:T(8,128)(2,1)} %get-tuple-element.157), channel_id=1, source_target_pairs={{0,16},{4,20},{8,24},{12,28},{16,0},{20,4},{24,8},{28,12},{1,17},{... | collective-permute-start | bytes 786440 | tf_op jit(solution)/shard_map/ppermute | solution.py:287
  193.9 15.0 %collective-permute-start.39 = (bf16[128,1024]{1,0:T(8,128)(2,1)}, bf16[128,1024]{1,0:T(8,128)(2,1)S(1)}, u32[]{:S(2)}, u32[]{:S(2)}) collective-permute-start(bf16[128,1024]{1,0:T(8,128)(2,1)} %get-tuple-element.156), channel_id=1, source_target_pairs={{0,8},{4,12},{8,0},{12,4},{16,24},{20,28},{24,16},{28,20},{1,9},{5... | collective-permute-start | bytes 786440 | tf_op jit(solution)/shard_map/ppermute | solution.py:287
  216.5 17.2 %collective-permute-start.58 = (bf16[8,32,384]{2,1,0:T(8,128)(2,1)}, bf16[8,32,384]{2,1,0:T(8,128)(2,1)S(1)}, u32[]{:S(2)}, u32[]{:S(2)}) collective-permute-start(bf16[8,32,384]{2,1,0:T(8,128)(2,1)} %get-tuple-element.181), channel_id=1, source_target_pairs={{0,2},{1,3},{2,0},{3,1},{4,6},{5,7},{6,4},{7,5},{8,10},{9,11},{10,... | collective-permute-start | bytes 589832 | tf_op jit(solution)/shard_map/ppermute | solution.py:291
  222.3 16.1 %collective-permute-start.54 = (bf16[128,1024]{1,0:T(8,128)(2,1)}, bf16[128,1024]{1,0:T(8,128)(2,1)S(1)}, u32[]{:S(2)}, u32[]{:S(2)}) collective-permute-start(bf16[128,1024]{1,0:T(8,128)(2,1)} %get-tuple-element.187), channel_id=1, source_target_pairs={{0,8},{4,12},{8,0},{12,4},{16,24},{20,28},{24,16},{28,20},{1,9},{5... | collective-permute-start | bytes 786440 | tf_op jit(solution)/shard_map/ppermute | solution.py:287
  223.7 14.7 %collective-permute-start.55 = (bf16[128,1024]{1,0:T(8,128)(2,1)}, bf16[128,1024]{1,0:T(8,128)(2,1)S(1)}, u32[]{:S(2)}, u32[]{:S(2)}) collective-permute-start(bf16[128,1024]{1,0:T(8,128)(2,1)} %get-tuple-element.188), channel_id=1, source_target_pairs={{0,16},{4,20},{8,24},{12,28},{16,0},{20,4},{24,8},{28,12},{1,17},{... | collective-permute-start | bytes 786440 | tf_op jit(solution)/shard_map/ppermute | solution.py:287
  233.7 40.7 %collective-permute-start.53 = (bf16[128,1024]{1,0:T(8,128)(2,1)S(1)}, bf16[128,1024]{1,0:T(8,128)(2,1)S(1)}, u32[]{:S(2)}, u32[]{:S(2)}) collective-permute-start(bf16[128,1024]{1,0:T(8,128)(2,1)S(1)} %add_convert_fusion), channel_id=1, source_target_pairs={{0,0},{1,16},{2,4},{3,20},{4,2},{5,18},{6,6},{7,22},{8,1},{9,17},{... | collective-permute-start | bytes 786440 | tf_op jit(solution)/shard_map/ppermute | solution.py:296
  242.1 32.3 %collective-permute-start.60 = (bf16[128,1024]{1,0:T(8,128)(2,1)}, bf16[128,1024]{1,0:T(8,128)(2,1)S(1)}, u32[]{:S(2)}, u32[]{:S(2)}) collective-permute-start(bf16[128,1024]{1,0:T(8,128)(2,1)} %get-tuple-element.195), channel_id=1, source_target_pairs={{0,0},{1,16},{2,4},{3,20},{4,2},{5,18},{6,6},{7,22},{8,1},{9,17},{... | collective-permute-start | bytes 786440 | tf_op jit(solution)/shard_map/ppermute | solution.py:296
  246.7 19.7 %all-to-all-start = ((bf16[8,32,896]{2,1,0:T(8,128)(2,1)}), bf16[8,32,896]{2,1,0:T(8,128)(2,1)S(1)}, u32[]{:S(2)}, u32[]{:S(2)}) async-start(bf16[8,32,896]{2,1,0:T(8,128)(2,1)} %pad_maximum_fusion.1), calls=%async_computation.1 | async-start | bytes 917504 | tf_op jit(solution)/shard_map/all_to_all | solution.py:1123
  258.8 15.6 %collective-permute-start.61 = (bf16[128,1024]{1,0:T(8,128)(2,1)S(1)}, bf16[128,1024]{1,0:T(8,128)(2,1)S(1)}, u32[]{:S(2)}, u32[]{:S(2)}) collective-permute-start(bf16[128,1024]{1,0:T(8,128)(2,1)S(1)} %pad_maximum_fusion.2), channel_id=1, source_target_pairs={{0,0},{1,8},{2,16},{3,24},{4,1},{5,9},{6,17},{7,25},{8,2},{9,10},{... | collective-permute-start | bytes 786440 | tf_op jit(solution)/shard_map/ppermute | solution.py:296
  (105 other events, 914.5 us)
Sparse Core Ops, SparseCore 0:
  91.2 48.6 all-gather.1
  176.5 42.8 reduce-scatter.2
  229.7 25.3 reduce-scatter.4

commit v6 on v5

--- a/solution.py
+++ b/solution.py
@@ -453,8 +453,8 @@
     )
 
 
-def scores_of(query, keys, slope, distance, allowed, scale):
-    raw = dot_nt(query, keys) * scale - slope * distance
+def scores_of(query, keys, slope, distance, allowed):
+    raw = dot_nt(query, keys) - slope * distance
     return jnp.where(allowed, raw, -1e30)
 
 
@@ -677,13 +677,13 @@
                 at = pl.ds(s * span + first, step_rows)
                 query_pos = row_positions((step_rows, 1), 0, rep, first)
                 allowed = (key_pos <= query_pos) & inside
-                distance = (query_pos - key_pos).astype(jnp.float32)
-                query = joint_ref[at, :own]
+                distance = query_pos.astype(jnp.float32) - key_pos.astype(jnp.float32)
+                query = joint_ref[at, :own] * jnp.bfloat16(scale)
                 mixed = jnp.zeros((step_rows, own), jnp.float32)
                 for j in range(2):
                     mine = (lane >= j * head_size) & (lane < (j + 1) * head_size)
                     masked = jnp.where(mine, query, jnp.zeros_like(query))
-                    scores = scores_of(masked, keys, slopes_ref[j], distance, allowed, scale)
+                    scores = scores_of(masked, keys, slopes_ref[j], distance, allowed)
                     top = jnp.max(scores, 1, keepdims=True)
                     exps = jnp.exp(scores - top)
                     probs = exps * (1.0 / jnp.sum(exps, 1, keepdims=True))
@@ -773,6 +773,7 @@
                 query = joint_ref[at, :own]
                 mixed_grad = mixed_grad_ref[at, :]
                 query_grad = jnp.zeros((step_rows, own), jnp.float32)
+                score_grads, queries, all_probs, mixed_grads = [], [], [], []
                 for j in range(2):
                     mine = (lane >= j * head_size) & (lane < (j + 1) * head_size)
                     masked = jnp.where(mine, query, jnp.zeros_like(query))
@@ -783,8 +784,16 @@
                     row_dot = jnp.sum(probs * probs_grad, 1, keepdims=True)
                     score_grad = (probs * (probs_grad - row_dot)).astype(jnp.bfloat16)
                     query_grad = jnp.where(mine, dot_nn(score_grad, keys), query_grad)
-                    key_acc[...] += outer(score_grad, masked)
-                    value_acc[...] += outer(probs_low, masked_grad)
+                    score_grads.append(score_grad)
+                    queries.append(masked)
+                    all_probs.append(probs_low)
+                    mixed_grads.append(masked_grad)
+                key_acc[...] += outer(
+                    jnp.concatenate(score_grads, 0), jnp.concatenate(queries, 0)
+                )
+                value_acc[...] += outer(
+                    jnp.concatenate(all_probs, 0), jnp.concatenate(mixed_grads, 0)
+                )
                 joint_grad_ref[at, :own] = (query_grad * scale).astype(jnp.bfloat16)
 
             at = pl.ds(s * span, span)

time: 291 us -> 291 us (level)
  no operation moved by 1% of the time
where the time goes in v6:
time: 291 us; the launch traced here: 290 us
  waiting for transfers between devices  85 us (29%)
  starting transfers between devices  80 us (27%)
  Pallas kernels  78.4 us (27%)
  local copies, waits for them, and re-layouts  17.5 us (6%)
  between operations  16.1 us (6%)
  other arithmetic  13.2 us (5%)
    pallas_call x16, Pallas kernels, kernel_call(): pl.pallas_call(kernel, out_shape=outs, in_specs=ins, out_specs=[LOCAL] *...  78.4 us
    ppermute x45, waiting for transfers between devices, over_rep(): return lax.ppermute(value, 'rep', [(i, i ^ flip) for i in range(PLANE)])  42.3 us
    ppermute x45, starting transfers between devices, over_rep(): return lax.ppermute(value, 'rep', [(i, i ^ flip) for i in range(PLANE)])  31 us
    ppermute x9, waiting for transfers between devices, over_z(): lax.ppermute(value, 'shard', [(i, (i + step) % DEPTH) for i in range(DEPT...  23.9 us
    ppermute x9, starting transfers between devices, over_z(): lax.ppermute(value, 'shard', [(i, (i + step) % DEPTH) for i in range(DEPT...  21 us
    unnamed x128, local copies, waits for them, and re-layouts  11.1 us
    ppermute x8, starting transfers between devices, over_all(): return lax.ppermute(value, ('rep', 'shard'), pairs)  10.6 us
    all_to_all x1, starting transfers between devices, body_planes(): arrived = lax.all_to_all(both, 'rep', 0, 0, tiled=True)  10.4 us
  transfers between devices with their start and end apart: 67, of which 25 were waited for; matrix products, arithmetic and copies ran while one was open for 6% of the time, Pallas kernels for 21%

profile of v6, /device:TPU:0, one launch (start us, length us, event | category | flops | bytes accessed | tf_op | source)
XLA Modules:
  0.0 290.1 jit_solution(16352379137577021986)
XLA Ops:
  13.1 8.4 %collective-permute-start.1 = (bf16[24,128]{1,0:T(8,128)(2,1)S(1)}, bf16[24,128]{1,0:T(8,128)(2,1)S(1)}, u32[]{:S(2)}, u32[]{:S(2)}) collective-permute-start(bf16[24,128]{1,0:T(8,128)(2,1)S(1)} %add_bitcast_fusion.p0), channel_id=1, source_target_pairs={{0,1},{1,2},{2,3},{3,0},{4,5},{5,6},{6,7},{7,4},{8,9},{9,10},{10,1... | collective-permute-start | bytes 18440 | tf_op jit(solution)/shard_map/ppermute | solution.py:291
  21.5 4.1 %collective-permute-start.2 = (bf16[24,128]{1,0:T(8,128)(2,1)S(1)}, bf16[24,128]{1,0:T(8,128)(2,1)S(1)}, u32[]{:S(2)}, u32[]{:S(2)}) collective-permute-start(bf16[24,128]{1,0:T(8,128)(2,1)S(1)} %add_bitcast_fusion.p0), channel_id=1, source_target_pairs={{0,2},{1,3},{2,0},{3,1},{4,6},{5,7},{6,4},{7,5},{8,10},{9,11},{10,... | collective-permute-start | bytes 18440 | tf_op jit(solution)/shard_map/ppermute | solution.py:291
  28.6 4.5 %collective-permute-done.3.p3 = bf16[24,128]{1,0:T(8,128)(2,1)S(1)} collective-permute-done((bf16[24,128]{1,0:T(8,128)(2,1)S(1)}, bf16[24,128]{1,0:T(8,128)(2,1)S(1)}, u32[]{:S(2)}, u32[]{:S(2)}) %collective-permute-start.3) | collective-permute-done | bytes 6176 | tf_op jit(solution)/shard_map/ppermute | solution.py:291
  37.9 3.1 %collective-permute-start.10 = (bf16[256,384]{1,0:T(8,128)(2,1)}, bf16[256,384]{1,0:T(8,128)(2,1)S(1)}, u32[]{:S(2)}, u32[]{:S(2)}) collective-permute-start(bf16[256,384]{1,0:T(8,128)(2,1)} %get-tuple-element.120.w0), channel_id=1, source_target_pairs={{0,1},{1,2},{2,3},{3,0},{4,5},{5,6},{6,7},{7,4},{8,9},{9,10},{10,1... | collective-permute-start | bytes 589832 | tf_op jit(solution)/shard_map/ppermute | solution.py:291
  48.7 7.6 %collective-permute-done.11.w2 = bf16[256,384]{1,0:T(8,128)(2,1)S(1)} collective-permute-done((bf16[256,384]{1,0:T(8,128)(2,1)}, bf16[256,384]{1,0:T(8,128)(2,1)S(1)}, u32[]{:S(2)}, u32[]{:S(2)}) %collective-permute-start.11) | collective-permute-done | bytes 196640 | tf_op jit(solution)/shard_map/ppermute | solution.py:291
  60.4 3.7 %collective-permute-start.16 = (bf16[128,1024]{1,0:T(8,128)(2,1)}, bf16[128,1024]{1,0:T(8,128)(2,1)S(1)}, u32[]{:S(2)}, u32[]{:S(2)}) collective-permute-start(bf16[128,1024]{1,0:T(8,128)(2,1)} %get-tuple-element.126), channel_id=1, source_target_pairs={{0,1},{4,5},{9,10},{13,14},{18,19},{22,23},{27,24},{31,28}} | collective-permute-start | bytes 786440 | tf_op jit(solution)/shard_map/ppermute | solution.py:296
  71.0 5.6 %collective-permute-done.17 = bf16[128,1024]{1,0:T(8,128)(2,1)S(1)} collective-permute-done((bf16[128,1024]{1,0:T(8,128)(2,1)}, bf16[128,1024]{1,0:T(8,128)(2,1)S(1)}, u32[]{:S(2)}, u32[]{:S(2)}) %collective-permute-start.17) | collective-permute-done | bytes 262176 | tf_op jit(solution)/shard_map/ppermute | solution.py:296
  77.2 12.9 %shard_map.265 = (bf16[1024,384]{1,0:T(8,128)(2,1)}, bf16[1024,128]{1,0:T(8,128)(2,1)}, bf16[2,1024,512]{2,1,0:T(8,128)(2,1)}) custom-call(f32[8,128]{1,0:T(8,128)} %copy-done.60, f32[8,128]{1,0:T(8,128)} %copy-done.61, f32[2]{0:T(128)} %multiply_exponential_fusion.slopes_ref, bf16[128,1024]{1,0:T(8,128)(2,1)} %get-tuple-element.114.n0, ...), custom_call_target="tpu_custom_call" | custom-call | flops 1342177280 | bytes 8388608 | tf_op jit(solution)/shard_map/pallas_call | solution.py:472
  100.8 3.5 %collective-permute-start.25 = (bf16[128,1024]{1,0:T(8,128)(2,1)}, bf16[128,1024]{1,0:T(8,128)(2,1)S(1)}, u32[]{:S(2)}, u32[]{:S(2)}) collective-permute-start(bf16[128,1024]{1,0:T(8,128)(2,1)} %get-tuple-element.135), channel_id=1, source_target_pairs={{0,16},{4,20},{8,24},{12,28},{16,0},{20,4},{24,8},{28,12},{1,17},{... | collective-permute-start | bytes 786440 | tf_op jit(solution)/shard_map/ppermute | solution.py:287
  104.3 5.9 %collective-permute-done.24.two = bf16[128,1024]{1,0:T(8,128)(2,1)S(1)} collective-permute-done((bf16[128,1024]{1,0:T(8,128)(2,1)}, bf16[128,1024]{1,0:T(8,128)(2,1)S(1)}, u32[]{:S(2)}, u32[]{:S(2)}) %collective-permute-start.24) | collective-permute-done | bytes 262176 | tf_op jit(solution)/shard_map/ppermute | solution.py:287
  110.1 6.3 %collective-permute-done.25.four = bf16[128,1024]{1,0:T(8,128)(2,1)S(1)} collective-permute-done((bf16[128,1024]{1,0:T(8,128)(2,1)}, bf16[128,1024]{1,0:T(8,128)(2,1)S(1)}, u32[]{:S(2)}, u32[]{:S(2)}) %collective-permute-start.25) | collective-permute-done | bytes 262176 | tf_op jit(solution)/shard_map/ppermute | solution.py:287
  123.6 5.5 %collective-permute-done.28.n2 = bf16[128,1024]{1,0:T(8,128)(2,1)S(1)} collective-permute-done((bf16[128,1024]{1,0:T(8,128)(2,1)}, bf16[128,1024]{1,0:T(8,128)(2,1)S(1)}, u32[]{:S(2)}, u32[]{:S(2)}) %collective-permute-start.28) | collective-permute-done | bytes 262176 | tf_op jit(solution)/shard_map/ppermute | solution.py:287
  129.1 5.1 %collective-permute-done.29.n4 = bf16[128,1024]{1,0:T(8,128)(2,1)S(1)} collective-permute-done((bf16[128,1024]{1,0:T(8,128)(2,1)}, bf16[128,1024]{1,0:T(8,128)(2,1)S(1)}, u32[]{:S(2)}, u32[]{:S(2)}) %collective-permute-start.29) | collective-permute-done | bytes 262176 | tf_op jit(solution)/shard_map/ppermute | solution.py:287
  139.9 10.7 %shard_map.269 = (bf16[1024,512]{1,0:T(8,128)(2,1)}, bf16[1024,512]{1,0:T(8,128)(2,1)}, f32[1,512]{1,0:T(1,128)}, bf16[2,2,128,1024]{3,2,1,0:T(8,128)(2,1)}, bf1...) custom-call(bf16[128,1024]{1,0:T(8,128)(2,1)} %get-tuple-element.138.n0, ...), custom_call_target="tpu_custom_call" | custom-call | flops 4294967296 | bytes 8388608 | tf_op jit(solution)/shard_map/pallas_call | solution.py:472
  160.7 6.5 %shard_map.272 = bf16[4,256,1024]{2,1,0:T(8,128)(2,1)} custom-call(bf16[128,1024]{1,0:T(8,128)(2,1)} %get-tuple-element.138.n0, bf16[128,1024]{1,0:T(8,128)(2,1)} %copy-done.27, bf16[128,1024]{1,0:T(8,128)(2,1)} %copy-done.21, bf16[128,1024]{1,0:T(8,128)(2,1)} %copy-done.28, bf16[128,1024]{1,0:T(8,128)(2,1)} %copy-done.22, bf16[128,1024]{1,0:T(8,128)(2,1)} %copy-done.29, ...), custom_call_target="tpu_custom_call" | custom-call | flops 2147483648 | bytes 8388608 | tf_op jit(solution)/shard_map/pallas_call | solution.py:472
  180.8 5.8 %collective-permute-done.46.g2 = bf16[128,1024]{1,0:T(8,128)(2,1)S(1)} collective-permute-done((bf16[128,1024]{1,0:T(8,128)(2,1)S(1)}, bf16[128,1024]{1,0:T(8,128)(2,1)S(1)}, u32[]{:S(2)}, u32[]{:S(2)}) %collective-permute-start.46) | collective-permute-done | bytes 262176 | tf_op jit(solution)/shard_map/ppermute | solution.py:287
  186.5 4.7 %collective-permute-done.47.g4 = bf16[128,1024]{1,0:T(8,128)(2,1)S(1)} collective-permute-done((bf16[128,1024]{1,0:T(8,128)(2,1)S(1)}, bf16[128,1024]{1,0:T(8,128)(2,1)S(1)}, u32[]{:S(2)}, u32[]{:S(2)}) %collective-permute-start.47) | collective-permute-done | bytes 262176 | tf_op jit(solution)/shard_map/ppermute | solution.py:287
  196.2 12.5 %shard_map.274 = (bf16[1024,384]{1,0:T(8,128)(2,1)}, f32[1,384]{1,0:T(1,128)}, bf16[2,2,128,1024]{3,2,1,0:T(8,128)(2,1)}, bf16[2,2,128,1024]{3,2,1,0:T(8,128)(2,1)}) custom-call(bf16[2,1024,512]{2,1,0:T(8,128)(2,1)} %get-tuple-element.159.probs_hbm, bf16[128,1024]{1,0:T(8,128)(2,1)} %get-tuple-element.170.g0, bf16[128,1024]{1,0:T(8,128)(2,1)} %copy-done.17, ...), custom_call_target="tpu_custom_call" | custom-call | flops 2415919104 | bytes 8388608 | tf_op jit(solution)/shard_map/pallas_call | solution.py:472
  210.4 5.9 %shard_map.275 = (bf16[8,32,384]{2,1,0:T(8,128)(2,1)}, bf16[8,32,384]{2,1,0:T(8,128)(2,1)}, bf16[8,32,384]{2,1,0:T(8,128)(2,1)}, bf16[8,32,384]{2,1,0:T(8,128)(2,1)}) custom-call(bf16[128,1024]{1,0:T(8,128)(2,1)} %get-tuple-element.114.n0, bf16[128,1024]{1,0:T(8,128)(2,1)} %copy-done.46, bf16[128,1024]{1,0:T(8,128)(2,1)} %copy-done.43, ...), custom_call_target="tpu_custom_call" | custom-call | flops 805306368 | bytes 8388608 | tf_op jit(solution)/shard_map/pallas_call | solution.py:472
  225.7 3.7 %shard_map.277 = bf16[4,32,1024]{2,1,0:T(8,128)(2,1)} custom-call(bf16[1024,128]{1,0:T(8,128)(2,1)} %get-tuple-element.190.mixed_ref, bf16[128,1024]{1,0:T(8,128)(2,1)} %get-tuple-element.170.g0, bf16[128,1024]{1,0:T(8,128)(2,1)} %copy-done.17, bf16[128,1024]{1,0:T(8,128)(2,1)} %copy-done.13, bf16[128,1024]{1,0:T(8,128)(2,1)} %copy-done.18, ...), custom_call_target="tpu_custom_call" | custom-call | flops 268435456 | bytes 8388608 | tf_op jit(solution)/shard_map/pallas_call | solution.py:472
  234.2 4.0 %collective-permute-done.59 = bf16[8,32,384]{2,1,0:T(8,128)(2,1)S(1)} collective-permute-done((bf16[8,32,384]{2,1,0:T(8,128)(2,1)S(1)}, bf16[8,32,384]{2,1,0:T(8,128)(2,1)S(1)}, u32[]{:S(2)}, u32[]{:S(2)}) %collective-permute-start.59) | collective-permute-done | bytes 196640 | tf_op jit(solution)/shard_map/ppermute | solution.py:291
  246.5 10.4 %all-to-all-start = ((bf16[8,32,896]{2,1,0:T(8,128)(2,1)}), bf16[8,32,896]{2,1,0:T(8,128)(2,1)S(1)}, u32[]{:S(2)}, u32[]{:S(2)}) async-start(bf16[8,32,896]{2,1,0:T(8,128)(2,1)} %pad_maximum_fusion.1), calls=%async_computation.1 | async-start | bytes 917504 | tf_op jit(solution)/shard_map/all_to_all | solution.py:1132
  259.1 6.8 %all-to-all-done = bf16[8,32,896]{2,1,0:T(8,128)(2,1)S(1)} async-done(((bf16[8,32,896]{2,1,0:T(8,128)(2,1)}), bf16[8,32,896]{2,1,0:T(8,128)(2,1)S(1)}, u32[]{:S(2)}, u32[]{:S(2)}) %all-to-all-start) | async-done | bytes 458784 | tf_op jit(solution)/shard_map/all_to_all | solution.py:1132
  267.8 6.5 %all-to-all-start.1 = ((bf16[32,2,192]{2,1,0:T(2,128)(2,1)}), bf16[32,2,192]{2,1,0:T(2,128)(2,1)S(1)}, u32[]{:S(2)}, u32[]{:S(2)}) async-start(bf16[32,2,192]{2,1,0:T(2,128)(2,1)} %reshape.88), calls=%async_computation.2 | async-start | bytes 65536 | tf_op jit(solution)/shard_map/all_to_all | solution.py:1164
  (308 shorter events, 120.6 us)
Async XLA Ops:
  7.2 132.6 %all-gather.2.cloned.1.call-start = ((), (), s32[]{:S(2)}) async-start(), calls=%async_computation.4 | async-start | bytes 2621440 | tf_op jit(solution)/shard_map/all_gather | solution.py:1092
  8.3 24.9 %collective-permute-start = (bf16[256,1024]{1,0:T(8,128)(2,1)S(1)}, bf16[256,1024]{1,0:T(8,128)(2,1)S(1)}, u32[]{:S(2)}, u32[]{:S(2)}) collective-permute-start(bf16[256,1024]{1,0:T(8,128)(2,1)S(1)} %pad_maximum_fusion), channel_id=1, source_target_pairs={{0,0},{1,8},{2,4},{3,12},{4,2},{5,10},{6,6},{7,14},{8,16},{9,24},{... | collective-permute-start | bytes 1572872 | tf_op jit(solution)/shard_map/ppermute | solution.py:296
  13.1 15.5 %collective-permute-start.1 = (bf16[24,128]{1,0:T(8,128)(2,1)S(1)}, bf16[24,128]{1,0:T(8,128)(2,1)S(1)}, u32[]{:S(2)}, u32[]{:S(2)}) collective-permute-start(bf16[24,128]{1,0:T(8,128)(2,1)S(1)} %add_bitcast_fusion.p0), channel_id=1, source_target_pairs={{0,1},{1,2},{2,3},{3,0},{4,5},{5,6},{6,7},{7,4},{8,9},{9,10},{10,1... | collective-permute-start | bytes 18440 | tf_op jit(solution)/shard_map/ppermute | solution.py:291
  41.0 15.3 %collective-permute-start.11 = (bf16[256,384]{1,0:T(8,128)(2,1)}, bf16[256,384]{1,0:T(8,128)(2,1)S(1)}, u32[]{:S(2)}, u32[]{:S(2)}) collective-permute-start(bf16[256,384]{1,0:T(8,128)(2,1)} %get-tuple-element.120.w0), channel_id=1, source_target_pairs={{0,2},{1,3},{2,0},{3,1},{4,6},{5,7},{6,4},{7,5},{8,10},{9,11},{10,... | collective-permute-start | bytes 589832 | tf_op jit(solution)/shard_map/ppermute | solution.py:291
  41.0 18.2 %collective-permute-start.7 = (bf16[128,1024]{1,0:T(8,128)(2,1)}, bf16[128,1024]{1,0:T(8,128)(2,1)S(1)}, u32[]{:S(2)}, u32[]{:S(2)}) collective-permute-start(bf16[128,1024]{1,0:T(8,128)(2,1)} %get-tuple-element.114.n0), channel_id=1, source_target_pairs={{0,8},{4,12},{8,0},{12,4},{16,24},{20,28},{24,16},{28,20},{1,9},{5... | collective-permute-start | bytes 786440 | tf_op jit(solution)/shard_map/ppermute | solution.py:287
  43.1 16.1 %collective-permute-start.8 = (bf16[128,1024]{1,0:T(8,128)(2,1)}, bf16[128,1024]{1,0:T(8,128)(2,1)S(1)}, u32[]{:S(2)}, u32[]{:S(2)}) collective-permute-start(bf16[128,1024]{1,0:T(8,128)(2,1)} %get-tuple-element.114.n0), channel_id=1, source_target_pairs={{0,16},{4,20},{8,24},{12,28},{16,0},{20,4},{24,8},{28,12},{1,17},{... | collective-permute-start | bytes 786440 | tf_op jit(solution)/shard_map/ppermute | solution.py:287
  44.9 14.3 %collective-permute-start.9 = (bf16[128,1024]{1,0:T(8,128)(2,1)}, bf16[128,1024]{1,0:T(8,128)(2,1)S(1)}, u32[]{:S(2)}, u32[]{:S(2)}) collective-permute-start(bf16[128,1024]{1,0:T(8,128)(2,1)} %get-tuple-element.114.n0), channel_id=1, source_target_pairs={{0,24},{4,28},{8,16},{12,20},{16,8},{20,12},{24,0},{28,4},{1,25},{... | collective-permute-start | bytes 786440 | tf_op jit(solution)/shard_map/ppermute | solution.py:287
  66.1 24.0 %collective-permute-start.18 = (bf16[128,1024]{1,0:T(8,128)(2,1)}, bf16[128,1024]{1,0:T(8,128)(2,1)S(1)}, u32[]{:S(2)}, u32[]{:S(2)}) collective-permute-start(bf16[128,1024]{1,0:T(8,128)(2,1)} %get-tuple-element.126), channel_id=1, source_target_pairs={{0,3},{4,7},{9,8},{13,12},{18,17},{22,21},{27,26},{31,30}} | collective-permute-start | bytes 786440 | tf_op jit(solution)/shard_map/ppermute | solution.py:296
  69.3 20.8 %collective-permute-start.19 = (bf16[128,1024]{1,0:T(8,128)(2,1)S(1)}, bf16[128,1024]{1,0:T(8,128)(2,1)S(1)}, u32[]{:S(2)}, u32[]{:S(2)}) collective-permute-start(bf16[128,1024]{1,0:T(8,128)(2,1)S(1)} %slice_select_fusion.g0.seed_ref), channel_id=1, source_target_pairs={{0,4},{4,0},{8,12},{12,8},{16,20},{20,16},{24,28},{28,24},{1,5},{5... | collective-permute-start | bytes 786440 | tf_op jit(solution)/shard_map/ppermute | solution.py:287
  69.5 20.6 %collective-permute-start.20 = (bf16[128,1024]{1,0:T(8,128)(2,1)S(1)}, bf16[128,1024]{1,0:T(8,128)(2,1)S(1)}, u32[]{:S(2)}, u32[]{:S(2)}) collective-permute-start(bf16[128,1024]{1,0:T(8,128)(2,1)S(1)} %slice_select_fusion.g0.seed_ref), channel_id=1, source_target_pairs={{0,8},{4,12},{8,0},{12,4},{16,24},{20,28},{24,16},{28,20},{1,9},{5... | collective-permute-start | bytes 786440 | tf_op jit(solution)/shard_map/ppermute | solution.py:287
  71.0 19.1 %collective-permute-start.21 = (bf16[128,1024]{1,0:T(8,128)(2,1)S(1)}, bf16[128,1024]{1,0:T(8,128)(2,1)S(1)}, u32[]{:S(2)}, u32[]{:S(2)}) collective-permute-start(bf16[128,1024]{1,0:T(8,128)(2,1)S(1)} %slice_select_fusion.g0.seed_ref), channel_id=1, source_target_pairs={{0,16},{4,20},{8,24},{12,28},{16,0},{20,4},{24,8},{28,12},{1,17},{... | collective-permute-start | bytes 786440 | tf_op jit(solution)/shard_map/ppermute | solution.py:287
  91.1 153.4 %reduce-scatter.3.cloned.1.call-start = ((), (), s32[]{:S(2)}) async-start(), calls=%async_computation.5 | async-start | bytes 2621440 | tf_op jit(solution)/shard_map/reduce_scatter | solution.py:367
  100.8 15.6 %collective-permute-start.25 = (bf16[128,1024]{1,0:T(8,128)(2,1)}, bf16[128,1024]{1,0:T(8,128)(2,1)S(1)}, u32[]{:S(2)}, u32[]{:S(2)}) collective-permute-start(bf16[128,1024]{1,0:T(8,128)(2,1)} %get-tuple-element.135), channel_id=1, source_target_pairs={{0,16},{4,20},{8,24},{12,28},{16,0},{20,4},{24,8},{28,12},{1,17},{... | collective-permute-start | bytes 786440 | tf_op jit(solution)/shard_map/ppermute | solution.py:287
  176.3 80.5 %reduce-scatter.5.cloned.1.call-start = ((), (), s32[]{:S(2)}) async-start(), calls=%async_computation.6 | async-start | bytes 327680 | tf_op jit(solution)/shard_map/reduce_scatter | solution.py:367
  191.9 16.9 %collective-permute-start.41 = (bf16[128,1024]{1,0:T(8,128)(2,1)}, bf16[128,1024]{1,0:T(8,128)(2,1)S(1)}, u32[]{:S(2)}, u32[]{:S(2)}) collective-permute-start(bf16[128,1024]{1,0:T(8,128)(2,1)} %get-tuple-element.158), channel_id=1, source_target_pairs={{0,24},{4,28},{8,16},{12,20},{16,8},{20,12},{24,0},{28,4},{1,25},{... | collective-permute-start | bytes 786440 | tf_op jit(solution)/shard_map/ppermute | solution.py:287
  192.9 15.8 %collective-permute-start.40 = (bf16[128,1024]{1,0:T(8,128)(2,1)}, bf16[128,1024]{1,0:T(8,128)(2,1)S(1)}, u32[]{:S(2)}, u32[]{:S(2)}) collective-permute-start(bf16[128,1024]{1,0:T(8,128)(2,1)} %get-tuple-element.157), channel_id=1, source_target_pairs={{0,16},{4,20},{8,24},{12,28},{16,0},{20,4},{24,8},{28,12},{1,17},{... | collective-permute-start | bytes 786440 | tf_op jit(solution)/shard_map/ppermute | solution.py:287
  193.9 14.8 %collective-permute-start.39 = (bf16[128,1024]{1,0:T(8,128)(2,1)}, bf16[128,1024]{1,0:T(8,128)(2,1)S(1)}, u32[]{:S(2)}, u32[]{:S(2)}) collective-permute-start(bf16[128,1024]{1,0:T(8,128)(2,1)} %get-tuple-element.156), channel_id=1, source_target_pairs={{0,8},{4,12},{8,0},{12,4},{16,24},{20,28},{24,16},{28,20},{1,9},{5... | collective-permute-start | bytes 786440 | tf_op jit(solution)/shard_map/ppermute | solution.py:287
  216.3 17.2 %collective-permute-start.58 = (bf16[8,32,384]{2,1,0:T(8,128)(2,1)}, bf16[8,32,384]{2,1,0:T(8,128)(2,1)S(1)}, u32[]{:S(2)}, u32[]{:S(2)}) collective-permute-start(bf16[8,32,384]{2,1,0:T(8,128)(2,1)} %get-tuple-element.181), channel_id=1, source_target_pairs={{0,2},{1,3},{2,0},{3,1},{4,6},{5,7},{6,4},{7,5},{8,10},{9,11},{10,... | collective-permute-start | bytes 589832 | tf_op jit(solution)/shard_map/ppermute | solution.py:291
  222.2 16.0 %collective-permute-start.54 = (bf16[128,1024]{1,0:T(8,128)(2,1)}, bf16[128,1024]{1,0:T(8,128)(2,1)S(1)}, u32[]{:S(2)}, u32[]{:S(2)}) collective-permute-start(bf16[128,1024]{1,0:T(8,128)(2,1)} %get-tuple-element.187), channel_id=1, source_target_pairs={{0,8},{4,12},{8,0},{12,4},{16,24},{20,28},{24,16},{28,20},{1,9},{5... | collective-permute-start | bytes 786440 | tf_op jit(solution)/shard_map/ppermute | solution.py:287
  223.6 14.6 %collective-permute-start.55 = (bf16[128,1024]{1,0:T(8,128)(2,1)}, bf16[128,1024]{1,0:T(8,128)(2,1)S(1)}, u32[]{:S(2)}, u32[]{:S(2)}) collective-permute-start(bf16[128,1024]{1,0:T(8,128)(2,1)} %get-tuple-element.188), channel_id=1, source_target_pairs={{0,16},{4,20},{8,24},{12,28},{16,0},{20,4},{24,8},{28,12},{1,17},{... | collective-permute-start | bytes 786440 | tf_op jit(solution)/shard_map/ppermute | solution.py:287
  233.5 41.0 %collective-permute-start.53 = (bf16[128,1024]{1,0:T(8,128)(2,1)S(1)}, bf16[128,1024]{1,0:T(8,128)(2,1)S(1)}, u32[]{:S(2)}, u32[]{:S(2)}) collective-permute-start(bf16[128,1024]{1,0:T(8,128)(2,1)S(1)} %add_convert_fusion), channel_id=1, source_target_pairs={{0,0},{1,16},{2,4},{3,20},{4,2},{5,18},{6,6},{7,22},{8,1},{9,17},{... | collective-permute-start | bytes 786440 | tf_op jit(solution)/shard_map/ppermute | solution.py:296
  241.9 32.6 %collective-permute-start.60 = (bf16[128,1024]{1,0:T(8,128)(2,1)}, bf16[128,1024]{1,0:T(8,128)(2,1)S(1)}, u32[]{:S(2)}, u32[]{:S(2)}) collective-permute-start(bf16[128,1024]{1,0:T(8,128)(2,1)} %get-tuple-element.195), channel_id=1, source_target_pairs={{0,0},{1,16},{2,4},{3,20},{4,2},{5,18},{6,6},{7,22},{8,1},{9,17},{... | collective-permute-start | bytes 786440 | tf_op jit(solution)/shard_map/ppermute | solution.py:296
  246.5 19.5 %all-to-all-start = ((bf16[8,32,896]{2,1,0:T(8,128)(2,1)}), bf16[8,32,896]{2,1,0:T(8,128)(2,1)S(1)}, u32[]{:S(2)}, u32[]{:S(2)}) async-start(bf16[8,32,896]{2,1,0:T(8,128)(2,1)} %pad_maximum_fusion.1), calls=%async_computation.1 | async-start | bytes 917504 | tf_op jit(solution)/shard_map/all_to_all | solution.py:1132
  258.5 16.0 %collective-permute-start.61 = (bf16[128,1024]{1,0:T(8,128)(2,1)S(1)}, bf16[128,1024]{1,0:T(8,128)(2,1)S(1)}, u32[]{:S(2)}, u32[]{:S(2)}) collective-permute-start(bf16[128,1024]{1,0:T(8,128)(2,1)S(1)} %pad_maximum_fusion.2), channel_id=1, source_target_pairs={{0,0},{1,8},{2,16},{3,24},{4,1},{5,9},{6,17},{7,25},{8,2},{9,10},{... | collective-permute-start | bytes 786440 | tf_op jit(solution)/shard_map/ppermute | solution.py:296
  (105 other events, 913.9 us)
Sparse Core Ops, SparseCore 0:
  91.2 48.5 all-gather.1
  176.5 42.8 reduce-scatter.2
  229.6 25.3 reduce-scatter.4
